TPU v7x, 256 devices: a whole 4x4x8 slice. The times are simulated.
256 devices in a mesh: dp: 64 (over y_hi, z, x), inner: 4 (over y_lo, core).
Axes of the slice: x: 4, y: 4 (y_hi: 2, y_lo: 2; y = y_hi * 2 + y_lo), z: 8, core: 2. Of those that a mesh axis runs over, the one named last changes fastest.
Arguments:
- picture_vectors: bfloat16 [131072, 1152], P(('dp', 'inner')), may hold values from -6 to 6
- caption_vectors: bfloat16 [131072, 1152], P(('dp', 'inner')), may hold values from -6 to 6
- matching_caption_position: int32 [131072], P(('dp', 'inner')), may hold values from 0 to 131071
- score_multiplier: float32 [], replicated, may hold values from 5 to 20
- offset_shift: float32 [], replicated, may hold values from -3 to 1
Outputs:
- picture_derivative: float32 [131072, 1152], P(('dp', 'inner'))
- grad_texts: float32 [131072, 1152], P(('dp', 'inner'))
All inputs are finite; a program needn't handle non-finite values.
Results may differ from a plain program's by a relative error of at most 0.0041.
Values may be sent and summed in bfloat16 or wider, within the bound.
No kernel may reach another device: no remote copies, remote signals or barrier semaphores. Data moves between devices by JAX's collectives and lax.ppermute only.
A program may use at most 128 MiB of HBM per device.

v0:
```python
import jax
import jax.numpy as jnp
from jax import lax
from jax.sharding import PartitionSpec as P


def from_behind(block, axis, distance):
    devices = range(lax.axis_size(axis))
    route = [((i - distance) % len(devices), i) for i in devices]
    return lax.ppermute(block, axis, route)


def normalize(picture_count):
    values = picture_count.astype(jnp.float32)
    scale = lax.rsqrt(jnp.sum(values * values, axis=1, keepdims=True) + 1e-06)
    return (values * scale).astype(jnp.bfloat16)


def shards(
    picture_vectors, caption_vectors, matching_caption_position, score_multiplier, offset_shift
):
    image_norm = normalize(picture_vectors)
    text_norm = normalize(caption_vectors)
    cycle = lax.axis_size("dp")
    here = lax.axis_index("dp")
    resident_caption_tile = lax.all_gather(text_norm, "inner", axis=0, tiled=True)
    former_caption_tile = from_behind(resident_caption_tile, "dp", 1)
    block_rows = resident_caption_tile.shape[0]

    def weights(caption_tile, index):
        matched_scores = (
            score_multiplier
            * lax.dot_general(
                image_norm,
                caption_tile,
                (((1,), (1,)), ((), ())),
                preferred_element_type=jnp.float32,
            )
            + offset_shift
        )
        columns = index * block_rows + jnp.arange(block_rows, dtype=jnp.int32)
        positive = (matching_caption_position[:, None] == columns[None, :]).astype(jnp.float32)
        return (jax.nn.sigmoid(matched_scores) - positive).astype(jnp.bfloat16)

    resident_caption_factor = weights(resident_caption_tile, here)
    former_caption_factor = weights(former_caption_tile, (here - 1 + cycle) % cycle)
    picture_derivative = score_multiplier * (
        jnp.dot(resident_caption_factor, resident_caption_tile, preferred_element_type=jnp.float32)
        + jnp.dot(former_caption_factor, former_caption_tile, preferred_element_type=jnp.float32)
    )
    reduced_axes_spec = (((0,), (0,)), ((), ()))
    resident_caption_share = score_multiplier * lax.dot_general(
        resident_caption_factor, image_norm, reduced_axes_spec, preferred_element_type=jnp.float32
    )
    former_caption_share = score_multiplier * lax.dot_general(
        former_caption_factor, image_norm, reduced_axes_spec, preferred_element_type=jnp.float32
    )
    returned = from_behind(former_caption_share, "dp", -1)
    grad_texts = lax.psum_scatter(
        resident_caption_share + returned, "inner", scatter_dimension=0, tiled=True
    )
    return (picture_derivative, grad_texts)


def solution(mesh):
    return jax.shard_map(
        shards,
        mesh=mesh,
        in_specs=(P(("dp", "inner"), None), P(("dp", "inner"), None), P(("dp", "inner")), P(), P()),
        out_specs=(P(("dp", "inner"), None), P(("dp", "inner"), None)),
        check_vma=False,
    )
```

profile of v0, /device:TPU:1, one launch (start us, length us, event | category | flops | bytes accessed | tf_op | source)
XLA Modules:
  0.0 499.0 jit_solution(1822663586864126791)
XLA Ops:
  7.2 0.0 copy-start
  7.2 0.0 all-gather.2.cloned.1.call-start
  7.2 1.7 fusion.4
  8.9 0.0 copy-start.1
  8.9 2.6 fusion.5
  11.5 0.0 all-gather.2.cloned.1.call-update
  11.5 0.0 reduce-scatter.2.cloned.1.call-start
  11.5 57.8 %all-gather.2.cloned.1.call-done = bf16[2048,1152]{1,0:T(8,128)(2,1)} async-done(((bf16[512,1152]{1,0:T(8,128)(2,1)}), bf16[2048,1152]{1,0:T(8,128)(2,1)}) %all-gather.2.cloned.1.call-update) | async-done | bytes 4718608 | tf_op jit(solution)/shard_map/all_gather | solution.py:26
  69.3 1.2 collective-permute-start
  71.8 0.3 fusion.2
  72.1 107.1 %collective-permute-done = bf16[2048,1152]{1,0:T(8,128)(2,1)} collective-permute-done((bf16[2048,1152]{1,0:T(8,128)(2,1)}, bf16[2048,1152]{1,0:T(8,128)(2,1)}, u32[]{:S(2)}, u32[]{:S(2)}) %collective-permute-start) | collective-permute-done | bytes 4718624 | tf_op jit(solution)/shard_map/ppermute | solution.py:10
  179.2 6.0 %subtract_convert_fusion = bf16[512,2048]{1,0:T(8,128)(2,1)S(1)} fusion(bf16[2048,1152]{1,0:T(8,128)(2,1)} %collective-permute-done, s32[2048]{0:T(1024)S(1)} %iota_add_fusion, f32[]{:T(128)S(6)} %copy.8, f32[]{:T(128)S(6)} %copy.7, s32[512]{0:T(512)S(1)} %copy-done.1, bf16[512,1152]{1,0:T(8,128)(2,1)S(1)} %copy-done, f32[512]{0:T(512)S(1)} %add_rsqrt_fusion.1), kind=kOutput, calls=%fused_computation.3 | convolution fusion | flops 2427125760 | bytes 8007688 | tf_op jit(solution)/shard_map/dot_general | solution.py:33
  185.2 0.0 copy-start.2
  185.2 5.5 %convolution_multiply_fusion = f32[2048,1152]{1,0:T(8,128)} fusion(bf16[512,2048]{1,0:T(8,128)(2,1)S(1)} %subtract_convert_fusion, f32[]{:T(128)S(6)} %copy.7, bf16[512,1152]{1,0:T(8,128)(2,1)S(1)} %copy-done, f32[512]{0:T(512)S(1)} %add_rsqrt_fusion.1), kind=kOutput, calls=%fused_computation | convolution fusion | flops 2420047872 | bytes 12716036 | tf_op jit(solution)/shard_map/dot_general | solution.py:55
  190.7 1.4 collective-permute-start.1
  192.1 6.0 %subtract_convert_fusion.1 = bf16[512,2048]{1,0:T(8,128)(2,1)S(1)} fusion(bf16[2048,1152]{1,0:T(8,128)(2,1)} %all-gather.2.cloned.1.call-done, s32[2048]{0:T(1024)S(1)} %iota_add_fusion.1, f32[]{:T(128)S(6)} %copy.8, f32[]{:T(128)S(6)} %copy.7, s32[512]{0:T(512)S(1)} %copy-done.1, bf16[512,1152]{1,0:T(8,128)(2,1)S(1)} %copy-done, f32[512]{0:T(512)S(1)} %add_rsqrt_fusion.1), kind=kOutput, calls=%fused_computation.4 | convolution fusion | flops 2427125760 | bytes 8007688 | tf_op jit(solution)/shard_map/dot_general | solution.py:33
  198.1 197.0 %collective-permute-done.1 = f32[2048,1152]{1,0:T(8,128)} collective-permute-done((f32[2048,1152]{1,0:T(8,128)}, f32[2048,1152]{1,0:T(8,128)}, u32[]{:S(2)}, u32[]{:S(2)}) %collective-permute-start.1) | collective-permute-done | bytes 9437216 | tf_op jit(solution)/shard_map/ppermute | solution.py:10
  395.1 7.8 %fusion = f32[2048,1152]{1,0:T(8,128)} fusion(f32[2048,1152]{1,0:T(8,128)} %collective-permute-done.1, bf16[512,2048]{1,0:T(8,128)(2,1)S(1)} %subtract_convert_fusion.1, f32[]{:T(128)S(6)} %copy.7, bf16[512,1152]{1,0:T(8,128)(2,1)S(1)} %copy-done, f32[512]{0:T(512)S(1)} %add_rsqrt_fusion.1), kind=kOutput, calls=%fused_computation.2 | convolution fusion | flops 2422407168 | bytes 22153220 | tf_op jit(solution)/shard_map/dot_general | solution.py:52
  402.9 0.0 reduce-scatter.2.cloned.1.call-update
  402.9 0.0 copy-start.3
  403.0 5.3 %fusion.10 = f32[512,1152]{1,0:T(8,128)S(1)} fusion(bf16[512,2048]{1,0:T(8,128)(2,1)S(1)} %subtract_convert_fusion.1, bf16[2048,1152]{1,0:T(8,128)(2,1)} %all-gather.2.cloned.1.call-done), kind=kOutput, calls=%fused_computation.19 | convolution fusion | flops 2415919104 | bytes 9175040 | tf_op jit(solution)/shard_map/dot_general | solution.py:48
  408.3 0.0 copy-done.3
  408.3 6.7 %fusion.1 = f32[512,1152]{1,0:T(8,128)} fusion(f32[512,1152]{1,0:T(8,128)S(1)} %fusion.10, bf16[512,2048]{1,0:T(8,128)(2,1)S(1)} %copy-done.3, bf16[2048,1152]{1,0:T(8,128)(2,1)} %collective-permute-done, f32[]{:T(128)S(6)} %copy.7), kind=kOutput, calls=%fused_computation.6 | convolution fusion | flops 2417098752 | bytes 11534340 | tf_op jit(solution)/shard_map/dot_general | solution.py:49
  415.0 77.1 %reduce-scatter.2.cloned.1.call-done = f32[512,1152]{1,0:T(8,128)} async-done(((f32[2048,1152]{1,0:T(8,128)}), f32[512,1152]{1,0:T(8,128)}) %reduce-scatter.2.cloned.1.call-update) | async-done | bytes 2359312 | tf_op jit(solution)/shard_map/reduce_scatter | solution.py:59
  (7 shorter events, 0.0 us)
Async XLA Ops:
  7.2 64.7 %copy-start = (bf16[512,1152]{1,0:T(8,128)(2,1)S(1)}, bf16[512,1152]{1,0:T(8,128)(2,1)}, u32[]{:S(2)}) copy-start(bf16[512,1152]{1,0:T(8,128)(2,1)} %param.5) | copy-start | bytes 3538948
  7.2 62.1 %all-gather.2.cloned.1.call-start = ((), (), s32[]{:S(2)}) async-start(), calls=%async_computation.1 | async-start | bytes 5898240 | tf_op jit(solution)/shard_map/all_gather | solution.py:26
  8.9 170.3 %copy-start.1 = (s32[512]{0:T(512)S(1)}, s32[512]{0:T(512)}, u32[]{:S(2)}) copy-start(s32[512]{0:T(512)} %param.7) | copy-start | bytes 6148
  11.5 480.7 %reduce-scatter.2.cloned.1.call-start = ((), (), s32[]{:S(2)}) async-start(), calls=%async_computation.2 | async-start | bytes 11796480 | tf_op jit(solution)/shard_map/reduce_scatter | solution.py:59
  69.3 109.9 %collective-permute-start = (bf16[2048,1152]{1,0:T(8,128)(2,1)}, bf16[2048,1152]{1,0:T(8,128)(2,1)}, u32[]{:S(2)}, u32[]{:S(2)}) collective-permute-start(bf16[2048,1152]{1,0:T(8,128)(2,1)} %all-gather.2.cloned.1.call-done), channel_id=1, source_target_pairs={{252,0},{0,4},{4,8},{8,12},{12,16},{16,20},{20,24},{24,28},{28,32}... | collective-permute-start | bytes 14155784 | tf_op jit(solution)/shard_map/ppermute | solution.py:10
  185.2 5.5 %copy-start.2 = (bf16[512,2048]{1,0:T(8,128)(2,1)}, bf16[512,2048]{1,0:T(8,128)(2,1)S(1)}, u32[]{:S(2)}) copy-start(bf16[512,2048]{1,0:T(8,128)(2,1)S(1)} %subtract_convert_fusion) | copy-start | bytes 6291460
  190.7 204.4 %collective-permute-start.1 = (f32[2048,1152]{1,0:T(8,128)}, f32[2048,1152]{1,0:T(8,128)}, u32[]{:S(2)}, u32[]{:S(2)}) collective-permute-start(f32[2048,1152]{1,0:T(8,128)} %convolution_multiply_fusion), channel_id=1, source_target_pairs={{4,0},{8,4},{12,8},{16,12},{20,16},{24,20},{28,24},{32,28},{36,32}... | collective-permute-start | bytes 28311560 | tf_op jit(solution)/shard_map/ppermute | solution.py:10
  402.9 5.4 %copy-start.3 = (bf16[512,2048]{1,0:T(8,128)(2,1)S(1)}, bf16[512,2048]{1,0:T(8,128)(2,1)}, u32[]{:S(2)}) copy-start(bf16[512,2048]{1,0:T(8,128)(2,1)} %copy-done.2) | copy-start | bytes 6291460
Sparse Core Ops, SparseCore 0:
  11.6 57.6 all-gather.1
  403.1 89.0 reduce-scatter.1
where the time goes:
time: 499 us
  waiting for transfers between devices  439 us (88%)
  matrix products  37.2 us (7%)
  between operations  15.4 us (3%)
    ppermute x2, waiting for transfers between devices, from_behind(): return lax.ppermute(block, axis, route)  304 us
    reduce_scatter x1, waiting for transfers between devices, shards(): lax.psum_scatter(resident_caption_share + returned, 'inner', scatter_dime...  77.1 us
    all_gather x1, waiting for transfers between devices, shards(): lax.all_gather(text_norm, 'inner', axis=0, tiled=True)  57.8 us
    dot_general x2, matrix products, weights(): lax.dot_general(image_norm, caption_tile, (((1,), (1,)), ((), ())), prefe...  12 us
  transfers between devices with their start and end apart: 4, of which 4 were waited for; matrix products, arithmetic and copies ran while one was open for 4% of the time, Pallas kernels for 0%

commit v1 on v0

v1 whole, which is shorter than its diff:
```python
import functools

import jax
import jax.numpy as jnp
from jax import lax
from jax.experimental import pallas as pl
from jax.experimental.pallas import tpu as pltpu
from jax.sharding import PartitionSpec as P

AXES = ("dp", "inner")
ROWS = 512
BLOCK = 2048
D = 1152
EXTRA = 16
FORWARD = 2
BACK = 2
FR = ROWS // FORWARD
BR = ROWS // BACK


def routes(dp):
    half = dp // 2

    def crossed(g):
        return 2 if g % half == half - 1 else 0

    every = [(g, i) for g in range(dp) for i in range(4)]
    chip = [(g * 4 + i, g * 4 + (i ^ 2)) for g, i in every]
    core = [(g * 4 + i, g * 4 + (i ^ 1)) for g, i in every]
    ahead = [(g * 4 + i, ((g + 1) % dp) * 4 + (i ^ crossed(g))) for g, i in every]
    behind = [(d, s) for s, d in ahead]
    return chip, core, ahead, behind


def unit_rows(values):
    values = values.astype(jnp.float32)
    scale = lax.rsqrt(jnp.sum(values * values, axis=1, keepdims=True) + 1e-06)
    return (values * scale).astype(jnp.bfloat16)


def norm_body(pos_ref, a_ref, t_ref, *outs):
    pos = pos_ref[...]
    for j in range(FORWARD):
        image, text = outs[j], outs[FORWARD + j]
        here = pl.ds(j * FR, FR)
        image[pl.ds(0, FR)] = unit_rows(a_ref[here])
        text[...] = unit_rows(t_ref[here])
        part = pos[:, j * FR : (j + 1) * FR]
        digits = [part & 63, (part >> 6) & 63, part >> 12]
        rows = lax.broadcasted_iota(jnp.int32, (EXTRA, FR), 0)
        coded = jnp.zeros((EXTRA, FR), jnp.int32)
        for n, digit in enumerate(digits):
            coded = jnp.where(rows == n, jnp.broadcast_to(digit, (EXTRA, FR)), coded)
        image[pl.ds(FR, EXTRA)] = jnp.zeros((EXTRA, D), jnp.bfloat16)
        image[pl.ds(FR, EXTRA), pl.ds(0, FR)] = coded.astype(jnp.float32).astype(jnp.bfloat16)


def norms(pos, a, t):
    image = jax.ShapeDtypeStruct((FR + EXTRA, D), jnp.bfloat16)
    text = jax.ShapeDtypeStruct((FR, D), jnp.bfloat16)
    vmem = pl.BlockSpec(memory_space=pltpu.VMEM)
    outs = pl.pallas_call(
        norm_body,
        out_shape=[image] * FORWARD + [text] * FORWARD,
        in_specs=[vmem] * 3,
        out_specs=[vmem] * (2 * FORWARD),
        compiler_params=pltpu.CompilerParams(vmem_limit_bytes=24 << 20),
        cost_estimate=pl.CostEstimate(flops=4 * ROWS * D, bytes_accessed=8 * ROWS * D, transcendentals=0),
        name="norms",
    )(pos, a, t)
    return list(outs[:FORWARD]), list(outs[FORWARD:])


def positions(ref):
    digits = ref[pl.ds(FR, EXTRA), pl.ds(0, FR)].astype(jnp.float32)
    return digits[0:1] + 64.0 * digits[1:2] + 4096.0 * digits[2:3]


def gram_body(scale_ref, base_ref, *refs, nx, ny, with_sum, x_is_image):
    xs, ys = refs[:nx], refs[nx : nx + ny]
    given = refs[nx + ny] if with_sum else None
    out, weights = refs[nx + ny + with_sum :]
    scale, shift = scale_ref[0], scale_ref[1]
    for i, x_ref in enumerate(xs):
        x = x_ref[pl.ds(0, FR)]
        if x_is_image:
            mine = jnp.transpose(jnp.broadcast_to(positions(x_ref), (128, FR)))
        else:
            mine = (base_ref[i] + lax.broadcasted_iota(jnp.int32, (FR, 128), 0)).astype(jnp.float32)
        for j, y_ref in enumerate(ys):
            y = y_ref[pl.ds(0, FR)]
            dots = lax.dot_general(x, y, (((1,), (1,)), ((), ())), preferred_element_type=jnp.float32)
            logits = scale * dots + shift
            w = 1.0 / (1.0 + jnp.exp(-logits))
            hits = []
            for q in range(FR // 128):
                if x_is_image:
                    first = base_ref[j] + 128 * q
                    other = (first + lax.broadcasted_iota(jnp.int32, (FR, 128), 1)).astype(jnp.float32)
                else:
                    other = positions(y_ref)[:, 128 * q : 128 * (q + 1)]
                hits.append(mine == other)
            w = jnp.where(jnp.concatenate(hits, axis=1), w - 1.0, w)
            weights[pl.ds(i * FR, FR), pl.ds(j * FR, FR)] = w.astype(jnp.bfloat16)
    total = 0.0
    for j, y_ref in enumerate(ys):
        w = weights[:, pl.ds(j * FR, FR)]
        total = total + jnp.dot(w, y_ref[pl.ds(0, FR)], preferred_element_type=jnp.float32)
    total = scale * total
    if with_sum:
        total = total + given[...].astype(jnp.float32)
    out[...] = total.astype(out.dtype)


def gram(scales, bases, xs, ys, given, dtype, x_is_image, name):
    nx, ny = len(xs), len(ys)
    rows = nx * FR
    vmem = pl.BlockSpec(memory_space=pltpu.VMEM)
    smem = pl.BlockSpec(memory_space=pltpu.SMEM)
    extra = [] if given is None else [given]
    return pl.pallas_call(
        functools.partial(gram_body, nx=nx, ny=ny, with_sum=len(extra), x_is_image=x_is_image),
        out_shape=jax.ShapeDtypeStruct((rows, D), dtype),
        in_specs=[smem, smem] + [vmem] * (nx + ny + len(extra)),
        out_specs=vmem,
        scratch_shapes=[pltpu.VMEM((rows, ny * FR), jnp.bfloat16)],
        compiler_params=pltpu.CompilerParams(vmem_limit_bytes=32 << 20),
        cost_estimate=pl.CostEstimate(
            flops=4 * rows * ny * FR * D,
            bytes_accessed=2 * (rows + ny * FR) * D + 4 * rows * D,
            transcendentals=rows * ny * FR,
        ),
        name=name,
    )(scales, bases, *xs, *ys, *extra)


def add_body(mine, *refs):
    out = refs[-1]
    for j, got in enumerate(refs[:-1]):
        here = pl.ds(j * BR, BR)
        out[here] = mine[here] + got[...].astype(jnp.float32)


def shards(picture_vectors, caption_vectors, matching_caption_position, score_multiplier, offset_shift):
    dp = lax.axis_size("dp")
    half = dp // 2
    chip, core, ahead, behind = routes(dp)
    here, inner = lax.axis_index("dp"), lax.axis_index("inner")
    move = lambda blocks, route: [lax.ppermute(b, AXES, route) for b in blocks]

    scales = jnp.stack([score_multiplier, offset_shift])
    own = here * BLOCK + inner * ROWS
    mate = here * BLOCK + (inner ^ 1) * ROWS
    past = (here + dp - 1) % dp
    flip = jnp.where(here % half == 0, 2, 0)
    past_own = past * BLOCK + (inner ^ flip) * ROWS
    past_mate = past * BLOCK + (inner ^ 1 ^ flip) * ROWS
    spread = lambda starts: jnp.stack([s + j * FR for s in starts for j in range(FORWARD)]).astype(jnp.int32)

    image, text = norms(matching_caption_position.reshape(1, ROWS), picture_vectors, caption_vectors)
    image_far = move(image, chip)
    text_past = move(text, ahead)
    image_mate = move(image, core)
    text_mate = move(text, core)
    image_far_mate = move(image_far, core)
    text_past_mate = move(text_past, core)

    texts_near = text + text_mate
    texts_past = text_past + text_past_mate
    images_near = image + image_mate
    images_far = image_far + image_far_mate
    near_bases = spread([own, mate])
    past_bases = spread([past_own, past_mate])
    all_bases = spread([own, mate, past_own, past_mate])
    own_bases = spread([own])
    past_own_bases = spread([past_own])

    f32, bf16 = jnp.float32, jnp.bfloat16
    image_sum = gram(scales, near_bases, image, texts_near, None, f32, True, "image_near")
    text_sum = gram(scales, own_bases, text, images_near, None, f32, False, "text_near")
    far_terms = [
        gram(scales, all_bases, [image_far[j]], texts_near + texts_past, None, bf16, True, f"far_{j}")
        for j in range(BACK)
    ]
    past_terms = [
        gram(scales, past_own_bases[j : j + 1], [text_past[j]], images_near + images_far, None, bf16, False, f"past_{j}")
        for j in range(BACK)
    ]
    far_back = move(far_terms, chip)
    past_back = move(past_terms, behind)
    image_sum = gram(scales, past_bases, image, texts_past, image_sum, f32, True, "image_past")
    text_sum = gram(scales, own_bases, text, images_far, text_sum, f32, False, "text_far")
    picture_derivative = image_sum + jnp.concatenate(far_back, axis=0).astype(f32)
    grad_texts = text_sum + jnp.concatenate(past_back, axis=0).astype(f32)
    return (picture_derivative, grad_texts)


def solution(mesh):
    return jax.shard_map(
        shards,
        mesh=mesh,
        in_specs=(P(AXES, None), P(AXES, None), P(AXES), P(), P()),
        out_specs=(P(AXES, None), P(AXES, None)),
        check_vma=False,
    )
```

time: 499 us -> 114 us (0.23)
  waiting for transfers between devices: 439 us -> 49.2 us
  Pallas kernels: 0 us -> 38.2 us
  matrix products: 37.2 us -> 0 us
  starting transfers between devices: 2.71 us -> 16.1 us
  between operations: 15.4 us -> 2.09 us
    ppermute x2 -> x16, waiting for transfers between devices: 304 us -> 49.2 us  [shards(): move = lambda blocks, route: [lax.ppermute(b, AXES, route) for b in blocks]]
    reduce_scatter x1 -> x0, waiting for transfers between devices: 77.1 us -> none  [shards(): lax.psum_scatter(resident_caption_share + returned, 'inner', scatter_dime...]
    all_gather x1 -> x0, waiting for transfers between devices: 57.8 us -> none  [shards(): lax.all_gather(text_norm, 'inner', axis=0, tiled=True)]
    pallas_call x0 -> x9, Pallas kernels: none -> 38.2 us  [the longest x8 36.6 us: gram(): pl.pallas_call(functools.partial(gram_body, nx=nx, ny=ny, with_sum=len(ex...]
    dot_general x6 -> x0, matrix products: 37.2 us -> none  [the longest x2 12 us: weights(): lax.dot_general(image_norm, caption_tile, (((1,), (1,)), ((), ())), prefe...]
    ppermute x2 -> x16, starting transfers between devices: 2.63 us -> 16.1 us  [shards(): move = lambda blocks, route: [lax.ppermute(b, AXES, route) for b in blocks]]
  transfers between devices with their start and end apart: 4 -> 16, of which waited for: 4 -> 6; matrix products, arithmetic and copies ran while one was open for 4% -> 2% of each run, Pallas kernels for 0% -> 32%
where the time goes in v1:
time: 114 us; the launch traced here: 113 us
  waiting for transfers between devices  49.2 us (43%)
  Pallas kernels  38.2 us (34%)
  starting transfers between devices  16.1 us (14%)
  local copies, waits for them, and re-layouts  4.11 us (4%)
  other arithmetic  3.56 us (3%)
  between operations  2.09 us (2%)
    ppermute x16, waiting for transfers between devices, shards(): move = lambda blocks, route: [lax.ppermute(b, AXES, route) for b in blocks]  49.2 us
    pallas_call x8, Pallas kernels, gram(): pl.pallas_call(functools.partial(gram_body, nx=nx, ny=ny, with_sum=len(ex...  36.6 us
    ppermute x16, starting transfers between devices, shards(): move = lambda blocks, route: [lax.ppermute(b, AXES, route) for b in blocks]  16.1 us
    unnamed x10, local copies, waits for them, and re-layouts  4.03 us
  transfers between devices with their start and end apart: 16, of which 6 were waited for; matrix products, arithmetic and copies ran while one was open for 2% of the time, Pallas kernels for 32%

profile of v1, /device:TPU:1, one launch (start us, length us, event | category | flops | bytes accessed | tf_op | source)
XLA Modules:
  0.0 113.4 jit_solution(9347118807302913196)
XLA Ops:
  0.6 1.3 %copy-done = bf16[512,1152]{1,0:T(8,128)(2,1)S(1)} copy-done((bf16[512,1152]{1,0:T(8,128)(2,1)S(1)}, bf16[512,1152]{1,0:T(8,128)(2,1)}, u32[]{:S(2)}) %copy-start) | copy-done | bytes 1179672
  1.9 1.3 %copy-done.1 = bf16[512,1152]{1,0:T(8,128)(2,1)S(1)} copy-done((bf16[512,1152]{1,0:T(8,128)(2,1)S(1)}, bf16[512,1152]{1,0:T(8,128)(2,1)}, u32[]{:S(2)}) %copy-start.1) | copy-done | bytes 1179672
  3.9 1.7 %norms.1 = (bf16[272,1152]{1,0:T(8,128)(2,1)S(1)}, bf16[272,1152]{1,0:T(8,128)(2,1)S(1)}, bf16[256,1152]{1,0:T(8,128)(2,1)}, bf16[256,1152]{1,0:T(8,128)(2,1)}) custom-call(s32[1,512]{1,0:T(1,128)S(1)} %bitcast.13, bf16[512,1152]{1,0:T(8,128)(2,1)S(1)} %copy-done, bf16[512,1152]{1,0:T(8,128)(2,1)S(1)} %copy-done.1), custom_call_target="tpu_custom_call" | custom-call | flops 2359296 | bytes 4718592 | tf_op jit(solution)/shard_map/norms/pallas_call | solution.py:62
  5.5 2.0 %collective-permute-start = (bf16[256,1152]{1,0:T(8,128)(2,1)}, bf16[256,1152]{1,0:T(8,128)(2,1)}, u32[]{:S(2)}, u32[]{:S(2)}) collective-permute-start(bf16[256,1152]{1,0:T(8,128)(2,1)} %get-tuple-element.8.refs_2_.refs_1_.refs_0_), channel_id=1, source_target_pairs={{0,4},{1,5},{2,6},{3,7},{4,8},{5,9},{6,10},{7,11},{8,12},{9,13},{1... | collective-permute-start | bytes 1769480 | tf_op jit(solution)/shard_map/ppermute | solution.py:149
  8.8 1.2 %collective-permute-start.4 = (bf16[256,1152]{1,0:T(8,128)(2,1)}, bf16[256,1152]{1,0:T(8,128)(2,1)}, u32[]{:S(2)}, u32[]{:S(2)}) collective-permute-start(bf16[256,1152]{1,0:T(8,128)(2,1)} %get-tuple-element.8.refs_2_.refs_1_.refs_0_), channel_id=1, source_target_pairs={{0,1},{1,0},{2,3},{3,2},{4,5},{5,4},{6,7},{7,6},{8,9},{9,8},{10,11... | collective-permute-start | bytes 1769480 | tf_op jit(solution)/shard_map/ppermute | solution.py:149
  10.0 1.3 %collective-permute-start.6 = (bf16[272,1152]{1,0:T(8,128)(2,1)S(1)}, bf16[272,1152]{1,0:T(8,128)(2,1)S(1)}, u32[]{:S(2)}, u32[]{:S(2)}) collective-permute-start(bf16[272,1152]{1,0:T(8,128)(2,1)S(1)} %get-tuple-element.6.refs_0_.refs_2_.refs_1_), channel_id=1, source_target_pairs={{0,2},{1,3},{2,0},{3,1},{4,6},{5,7},{6,4},{7,5},{8,10},{9,11},{10,... | collective-permute-start | bytes 1880072 | tf_op jit(solution)/shard_map/ppermute | solution.py:149
  11.6 18.4 %collective-permute-done.refs_2_.refs_5_.refs_0_ = bf16[256,1152]{1,0:T(8,128)(2,1)} collective-permute-done((bf16[256,1152]{1,0:T(8,128)(2,1)}, bf16[256,1152]{1,0:T(8,128)(2,1)}, u32[]{:S(2)}, u32[]{:S(2)}) %collective-permute-start) | collective-permute-done | bytes 589856 | tf_op jit(solution)/shard_map/ppermute | solution.py:149
  29.9 2.1 %collective-permute-start.12 = (bf16[272,1152]{1,0:T(8,128)(2,1)S(1)}, bf16[272,1152]{1,0:T(8,128)(2,1)S(1)}, u32[]{:S(2)}, u32[]{:S(2)}) collective-permute-start(bf16[272,1152]{1,0:T(8,128)(2,1)S(1)} %get-tuple-element.6.refs_0_.refs_2_.refs_1_), channel_id=1, source_target_pairs={{0,1},{1,0},{2,3},{3,2},{4,5},{5,4},{6,7},{7,6},{8,9},{9,8},{10,11... | collective-permute-start | bytes 1880072 | tf_op jit(solution)/shard_map/ppermute | solution.py:149
  32.0 10.5 %collective-permute-done.1.refs_3_.refs_6_.refs_0_ = bf16[256,1152]{1,0:T(8,128)(2,1)S(1)} collective-permute-done((bf16[256,1152]{1,0:T(8,128)(2,1)}, bf16[256,1152]{1,0:T(8,128)(2,1)S(1)}, u32[]{:S(2)}, u32[]{:S(2)}) %collective-permute-start.1) | collective-permute-done | bytes 589856 | tf_op jit(solution)/shard_map/ppermute | solution.py:149
  43.3 1.4 %collective-permute-start.13 = (bf16[272,1152]{1,0:T(8,128)(2,1)S(1)}, bf16[272,1152]{1,0:T(8,128)(2,1)}, u32[]{:S(2)}, u32[]{:S(2)}) collective-permute-start(bf16[272,1152]{1,0:T(8,128)(2,1)S(1)} %get-tuple-element.7.refs_1_.refs_3_.refs_2_), channel_id=1, source_target_pairs={{0,1},{1,0},{2,3},{3,2},{4,5},{5,4},{6,7},{7,6},{8,9},{9,8},{10,11... | collective-permute-start | bytes 1880072 | tf_op jit(solution)/shard_map/ppermute | solution.py:149
  46.9 4.6 %image_near.1.refs_6_ = f32[512,1152]{1,0:T(8,128)S(1)} custom-call(f32[2]{0:T(128)S(1)} %pad_maximum_fusion.scale_ref, s32[4]{0:T(128)S(1)} %pad_add_fusion.1.base_ref, bf16[272,1152]{1,0:T(8,128)(2,1)S(1)} %get-tuple-element.6.refs_0_.refs_2_.refs_1_, bf16[272,1152]{1,0:T(8,128)(2,1)S(1)} %get-tuple-element.7.refs_1_.refs_3_.refs_2_, ...), custom_call_target="tpu_custom_call" | custom-call | flops 2415919104 | bytes 5898240 | tf_op jit(solution)/shard_map/image_near/pallas_call | solution.py:121
  51.5 6.1 %collective-permute-done.8.refs_0_.refs_3_.refs_6_ = bf16[272,1152]{1,0:T(8,128)(2,1)S(1)} collective-permute-done((bf16[272,1152]{1,0:T(8,128)(2,1)S(1)}, bf16[272,1152]{1,0:T(8,128)(2,1)S(1)}, u32[]{:S(2)}, u32[]{:S(2)}) %collective-permute-start.8) | collective-permute-done | bytes 626720 | tf_op jit(solution)/shard_map/ppermute | solution.py:149
  57.7 2.1 %collective-permute-start.10 = (bf16[272,1152]{1,0:T(8,128)(2,1)S(1)}, bf16[272,1152]{1,0:T(8,128)(2,1)S(1)}, u32[]{:S(2)}, u32[]{:S(2)}) collective-permute-start(bf16[272,1152]{1,0:T(8,128)(2,1)S(1)} %collective-permute-done.6.refs_0_.refs_2_.refs_5_), channel_id=1, source_target_pairs={{0,1},{1,0},{2,3},{3,2},{4,5},{5,4},{6,7},{7,6},{8,9},{9,8},{10,11... | collective-permute-start | bytes 1880072 | tf_op jit(solution)/shard_map/ppermute | solution.py:149
  59.8 4.5 %text_near.1.refs_6_ = f32[512,1152]{1,0:T(8,128)S(1)} custom-call(f32[2]{0:T(128)S(1)} %pad_maximum_fusion.scale_ref, s32[2]{0:T(128)S(1)} %pad_add_fusion.2.base_ref, bf16[256,1152]{1,0:T(8,128)(2,1)} %get-tuple-element.8.refs_2_.refs_1_.refs_0_, bf16[256,1152]{1,0:T(8,128)(2,1)} %get-tuple-element.9.refs_3_.refs_2_.refs_1_, ...), custom_call_target="tpu_custom_call" | custom-call | flops 2415919104 | bytes 5898240 | tf_op jit(solution)/shard_map/text_near/pallas_call | solution.py:121
  64.3 5.1 %far_0.1 = bf16[256,1152]{1,0:T(8,128)(2,1)S(1)} custom-call(f32[2]{0:T(128)S(1)} %pad_maximum_fusion.scale_ref, s32[8]{0:T(128)S(1)} %stack.70.base_ref, bf16[272,1152]{1,0:T(8,128)(2,1)S(1)} %collective-permute-done.6.refs_0_.refs_2_.refs_5_, bf16[256,1152]{1,0:T(8,128)(2,1)} %get-tuple-element.8.refs_2_.refs_1_.refs_0_, ...), custom_call_target="tpu_custom_call" | custom-call | flops 2415919104 | bytes 6488064 | tf_op jit(solution)/shard_map/far_0/pallas_call | solution.py:121
  69.6 5.1 %far_1.1 = bf16[256,1152]{1,0:T(8,128)(2,1)S(1)} custom-call(f32[2]{0:T(128)S(1)} %pad_maximum_fusion.scale_ref, s32[8]{0:T(128)S(1)} %stack.70.base_ref, bf16[272,1152]{1,0:T(8,128)(2,1)S(1)} %collective-permute-done.8.refs_0_.refs_3_.refs_6_, bf16[256,1152]{1,0:T(8,128)(2,1)} %get-tuple-element.8.refs_2_.refs_1_.refs_0_, ...), custom_call_target="tpu_custom_call" | custom-call | flops 2415919104 | bytes 6488064 | tf_op jit(solution)/shard_map/far_1/pallas_call | solution.py:121
  74.7 1.8 %collective-permute-start.9 = (bf16[256,1152]{1,0:T(8,128)(2,1)S(1)}, bf16[256,1152]{1,0:T(8,128)(2,1)S(1)}, u32[]{:S(2)}, u32[]{:S(2)}) collective-permute-start(bf16[256,1152]{1,0:T(8,128)(2,1)S(1)} %far_1.1), channel_id=1, source_target_pairs={{0,2},{1,3},{2,0},{3,1},{4,6},{5,7},{6,4},{7,5},{8,10},{9,11},{10,... | collective-permute-start | bytes 1769480 | tf_op jit(solution)/shard_map/ppermute | solution.py:149
  76.5 4.5 %image_past.1 = f32[512,1152]{1,0:T(8,128)S(1)} custom-call(f32[2]{0:T(128)S(1)} %pad_maximum_fusion.scale_ref, s32[4]{0:T(128)S(1)} %pad_add_fusion.base_ref, bf16[272,1152]{1,0:T(8,128)(2,1)S(1)} %get-tuple-element.6.refs_0_.refs_2_.refs_1_, bf16[272,1152]{1,0:T(8,128)(2,1)S(1)} %get-tuple-element.7.refs_1_.refs_3_.refs_2_, ...), custom_call_target="tpu_custom_call" | custom-call | flops 2415919104 | bytes 5898240 | tf_op jit(solution)/shard_map/image_past/pallas_call | solution.py:121
  81.0 4.3 %past_0.1 = bf16[256,1152]{1,0:T(8,128)(2,1)S(1)} custom-call(f32[2]{0:T(128)S(1)} %pad_maximum_fusion.scale_ref, s32[1]{0:T(128)} %bitcast.2.base_ref, bf16[256,1152]{1,0:T(8,128)(2,1)} %collective-permute-done.refs_2_.refs_5_.refs_0_, bf16[272,1152]{1,0:T(8,128)(2,1)S(1)} %get-tuple-element.6.refs_0_.refs_2_.refs_1_, ...), custom_call_target="tpu_custom_call" | custom-call | flops 2415919104 | bytes 6488064 | tf_op jit(solution)/shard_map/past_0/pallas_call | solution.py:121
  86.5 4.1 %past_1.1 = bf16[256,1152]{1,0:T(8,128)(2,1)S(1)} custom-call(f32[2]{0:T(128)S(1)} %pad_maximum_fusion.scale_ref, s32[1]{0:T(128)} %bitcast.3.base_ref, bf16[256,1152]{1,0:T(8,128)(2,1)S(1)} %copy-done.4, bf16[272,1152]{1,0:T(8,128)(2,1)S(1)} %get-tuple-element.6.refs_0_.refs_2_.refs_1_, bf16[272,1152]{1,0:T(8,128)(2,1)S(1)} %get-tuple-element.7.refs_1_.refs_3_.refs_2_, ...), custom_call_target="tpu_custom_call" | custom-call | flops 2415919104 | bytes 6488064 | tf_op jit(solution)/shard_map/past_1/pallas_call | solution.py:121
  91.5 4.3 %text_far.1 = f32[512,1152]{1,0:T(8,128)S(1)} custom-call(f32[2]{0:T(128)S(1)} %pad_maximum_fusion.scale_ref, s32[2]{0:T(128)S(1)} %pad_add_fusion.2.base_ref, bf16[256,1152]{1,0:T(8,128)(2,1)} %get-tuple-element.8.refs_2_.refs_1_.refs_0_, bf16[256,1152]{1,0:T(8,128)(2,1)} %get-tuple-element.9.refs_3_.refs_2_.refs_1_, ...), custom_call_target="tpu_custom_call" | custom-call | flops 2415919104 | bytes 5898240 | tf_op jit(solution)/shard_map/text_far/pallas_call | solution.py:121
  96.6 1.7 %convert_add_fusion.1 = f32[512,1152]{1,0:T(8,128)} fusion(f32[512,1152]{1,0:T(8,128)S(1)} %image_past.1, bf16[256,1152]{1,0:T(8,128)(2,1)S(1)} %collective-permute-done.9, bf16[256,1152]{1,0:T(8,128)(2,1)S(1)} %collective-permute-done.7), kind=kLoop, calls=%fused_computation.1 | loop fusion | flops 2949120 | bytes 5898240 | tf_op jit(solution)/shard_map/add | solution.py:193
  99.1 12.6 %collective-permute-done.15 = bf16[256,1152]{1,0:T(8,128)(2,1)S(1)} collective-permute-done((bf16[256,1152]{1,0:T(8,128)(2,1)S(1)}, bf16[256,1152]{1,0:T(8,128)(2,1)S(1)}, u32[]{:S(2)}, u32[]{:S(2)}) %collective-permute-start.15) | collective-permute-done | bytes 589856 | tf_op jit(solution)/shard_map/ppermute | solution.py:149
  111.8 1.6 %convert_add_fusion = f32[512,1152]{1,0:T(8,128)} fusion(f32[512,1152]{1,0:T(8,128)S(1)} %text_far.1, bf16[256,1152]{1,0:T(8,128)(2,1)S(1)} %collective-permute-done.15, bf16[256,1152]{1,0:T(8,128)(2,1)S(1)} %collective-permute-done.14), kind=kLoop, calls=%fused_computation | loop fusion | flops 2949120 | bytes 5898240 | tf_op jit(solution)/shard_map/add | solution.py:194
  (34 shorter events, 7.7 us)
Async XLA Ops:
  0.6 1.3 %copy-start = (bf16[512,1152]{1,0:T(8,128)(2,1)S(1)}, bf16[512,1152]{1,0:T(8,128)(2,1)}, u32[]{:S(2)}) copy-start(bf16[512,1152]{1,0:T(8,128)(2,1)} %a_ref.1) | copy-start | bytes 3538948
  1.9 1.3 %copy-start.1 = (bf16[512,1152]{1,0:T(8,128)(2,1)S(1)}, bf16[512,1152]{1,0:T(8,128)(2,1)}, u32[]{:S(2)}) copy-start(bf16[512,1152]{1,0:T(8,128)(2,1)} %t_ref.1) | copy-start | bytes 3538948
  3.2 0.7 copy-start.2
  5.5 24.4 %collective-permute-start = (bf16[256,1152]{1,0:T(8,128)(2,1)}, bf16[256,1152]{1,0:T(8,128)(2,1)}, u32[]{:S(2)}, u32[]{:S(2)}) collective-permute-start(bf16[256,1152]{1,0:T(8,128)(2,1)} %get-tuple-element.8.refs_2_.refs_1_.refs_0_), channel_id=1, source_target_pairs={{0,4},{1,5},{2,6},{3,7},{4,8},{5,9},{6,10},{7,11},{8,12},{9,13},{1... | collective-permute-start | bytes 1769480 | tf_op jit(solution)/shard_map/ppermute | solution.py:149
  7.6 34.9 %collective-permute-start.1 = (bf16[256,1152]{1,0:T(8,128)(2,1)}, bf16[256,1152]{1,0:T(8,128)(2,1)S(1)}, u32[]{:S(2)}, u32[]{:S(2)}) collective-permute-start(bf16[256,1152]{1,0:T(8,128)(2,1)} %get-tuple-element.9.refs_3_.refs_2_.refs_1_), channel_id=1, source_target_pairs={{0,4},{1,5},{2,6},{3,7},{4,8},{5,9},{6,10},{7,11},{8,12},{9,13},{1... | collective-permute-start | bytes 1769480 | tf_op jit(solution)/shard_map/ppermute | solution.py:149
  8.8 34.5 %collective-permute-start.4 = (bf16[256,1152]{1,0:T(8,128)(2,1)}, bf16[256,1152]{1,0:T(8,128)(2,1)}, u32[]{:S(2)}, u32[]{:S(2)}) collective-permute-start(bf16[256,1152]{1,0:T(8,128)(2,1)} %get-tuple-element.8.refs_2_.refs_1_.refs_0_), channel_id=1, source_target_pairs={{0,1},{1,0},{2,3},{3,2},{4,5},{5,4},{6,7},{7,6},{8,9},{9,8},{10,11... | collective-permute-start | bytes 1769480 | tf_op jit(solution)/shard_map/ppermute | solution.py:149
  10.0 34.9 %collective-permute-start.6 = (bf16[272,1152]{1,0:T(8,128)(2,1)S(1)}, bf16[272,1152]{1,0:T(8,128)(2,1)S(1)}, u32[]{:S(2)}, u32[]{:S(2)}) collective-permute-start(bf16[272,1152]{1,0:T(8,128)(2,1)S(1)} %get-tuple-element.6.refs_0_.refs_2_.refs_1_), channel_id=1, source_target_pairs={{0,2},{1,3},{2,0},{3,1},{4,6},{5,7},{6,4},{7,5},{8,10},{9,11},{10,... | collective-permute-start | bytes 1880072 | tf_op jit(solution)/shard_map/ppermute | solution.py:149
  11.3 33.5 %collective-permute-start.5 = (bf16[256,1152]{1,0:T(8,128)(2,1)}, bf16[256,1152]{1,0:T(8,128)(2,1)}, u32[]{:S(2)}, u32[]{:S(2)}) collective-permute-start(bf16[256,1152]{1,0:T(8,128)(2,1)} %get-tuple-element.9.refs_3_.refs_2_.refs_1_), channel_id=1, source_target_pairs={{0,1},{1,0},{2,3},{3,2},{4,5},{5,4},{6,7},{7,6},{8,9},{9,8},{10,11... | collective-permute-start | bytes 1769480 | tf_op jit(solution)/shard_map/ppermute | solution.py:149
  29.9 29.9 %collective-permute-start.12 = (bf16[272,1152]{1,0:T(8,128)(2,1)S(1)}, bf16[272,1152]{1,0:T(8,128)(2,1)S(1)}, u32[]{:S(2)}, u32[]{:S(2)}) collective-permute-start(bf16[272,1152]{1,0:T(8,128)(2,1)S(1)} %get-tuple-element.6.refs_0_.refs_2_.refs_1_), channel_id=1, source_target_pairs={{0,1},{1,0},{2,3},{3,2},{4,5},{5,4},{6,7},{7,6},{8,9},{9,8},{10,11... | collective-permute-start | bytes 1880072 | tf_op jit(solution)/shard_map/ppermute | solution.py:149
  42.5 0.8 copy-start.3
  43.3 14.4 %collective-permute-start.8 = (bf16[272,1152]{1,0:T(8,128)(2,1)S(1)}, bf16[272,1152]{1,0:T(8,128)(2,1)S(1)}, u32[]{:S(2)}, u32[]{:S(2)}) collective-permute-start(bf16[272,1152]{1,0:T(8,128)(2,1)S(1)} %get-tuple-element.7.refs_1_.refs_3_.refs_2_), channel_id=1, source_target_pairs={{0,2},{1,3},{2,0},{3,1},{4,6},{5,7},{6,4},{7,5},{8,10},{9,11},{10,... | collective-permute-start | bytes 1880072 | tf_op jit(solution)/shard_map/ppermute | solution.py:149
  43.3 16.5 %collective-permute-start.13 = (bf16[272,1152]{1,0:T(8,128)(2,1)S(1)}, bf16[272,1152]{1,0:T(8,128)(2,1)}, u32[]{:S(2)}, u32[]{:S(2)}) collective-permute-start(bf16[272,1152]{1,0:T(8,128)(2,1)S(1)} %get-tuple-element.7.refs_1_.refs_3_.refs_2_), channel_id=1, source_target_pairs={{0,1},{1,0},{2,3},{3,2},{4,5},{5,4},{6,7},{7,6},{8,9},{9,8},{10,11... | collective-permute-start | bytes 1880072 | tf_op jit(solution)/shard_map/ppermute | solution.py:149
  44.8 19.5 %collective-permute-start.2 = (bf16[256,1152]{1,0:T(8,128)(2,1)}, bf16[256,1152]{1,0:T(8,128)(2,1)}, u32[]{:S(2)}, u32[]{:S(2)}) collective-permute-start(bf16[256,1152]{1,0:T(8,128)(2,1)} %collective-permute-done.refs_2_.refs_5_.refs_0_), channel_id=1, source_target_pairs={{0,1},{1,0},{2,3},{3,2},{4,5},{5,4},{6,7},{7,6},{8,9},{9,8},{10,11... | collective-permute-start | bytes 1769480 | tf_op jit(solution)/shard_map/ppermute | solution.py:149
  44.9 19.5 %collective-permute-start.3 = (bf16[256,1152]{1,0:T(8,128)(2,1)}, bf16[256,1152]{1,0:T(8,128)(2,1)}, u32[]{:S(2)}, u32[]{:S(2)}) collective-permute-start(bf16[256,1152]{1,0:T(8,128)(2,1)} %copy-done.3), channel_id=1, source_target_pairs={{0,1},{1,0},{2,3},{3,2},{4,5},{5,4},{6,7},{7,6},{8,9},{9,8},{10,11... | collective-permute-start | bytes 1769480 | tf_op jit(solution)/shard_map/ppermute | solution.py:149
  51.5 12.8 %copy-start.4 = (bf16[256,1152]{1,0:T(8,128)(2,1)S(1)}, bf16[256,1152]{1,0:T(8,128)(2,1)}, u32[]{:S(2)}) copy-start(bf16[256,1152]{1,0:T(8,128)(2,1)} %copy-done.3) | copy-start | bytes 1769476
  57.7 23.3 %collective-permute-start.10 = (bf16[272,1152]{1,0:T(8,128)(2,1)S(1)}, bf16[272,1152]{1,0:T(8,128)(2,1)S(1)}, u32[]{:S(2)}, u32[]{:S(2)}) collective-permute-start(bf16[272,1152]{1,0:T(8,128)(2,1)S(1)} %collective-permute-done.6.refs_0_.refs_2_.refs_5_), channel_id=1, source_target_pairs={{0,1},{1,0},{2,3},{3,2},{4,5},{5,4},{6,7},{7,6},{8,9},{9,8},{10,11... | collective-permute-start | bytes 1880072 | tf_op jit(solution)/shard_map/ppermute | solution.py:149
  59.8 21.2 %collective-permute-start.11 = (bf16[272,1152]{1,0:T(8,128)(2,1)S(1)}, bf16[272,1152]{1,0:T(8,128)(2,1)S(1)}, u32[]{:S(2)}, u32[]{:S(2)}) collective-permute-start(bf16[272,1152]{1,0:T(8,128)(2,1)S(1)} %collective-permute-done.8.refs_0_.refs_3_.refs_6_), channel_id=1, source_target_pairs={{0,1},{1,0},{2,3},{3,2},{4,5},{5,4},{6,7},{7,6},{8,9},{9,8},{10,11... | collective-permute-start | bytes 1880072 | tf_op jit(solution)/shard_map/ppermute | solution.py:149
  69.5 26.4 %collective-permute-start.7 = (bf16[256,1152]{1,0:T(8,128)(2,1)S(1)}, bf16[256,1152]{1,0:T(8,128)(2,1)S(1)}, u32[]{:S(2)}, u32[]{:S(2)}) collective-permute-start(bf16[256,1152]{1,0:T(8,128)(2,1)S(1)} %far_0.1), channel_id=1, source_target_pairs={{0,2},{1,3},{2,0},{3,1},{4,6},{5,7},{6,4},{7,5},{8,10},{9,11},{10,... | collective-permute-start | bytes 1769480 | tf_op jit(solution)/shard_map/ppermute | solution.py:149
  74.7 21.9 %collective-permute-start.9 = (bf16[256,1152]{1,0:T(8,128)(2,1)S(1)}, bf16[256,1152]{1,0:T(8,128)(2,1)S(1)}, u32[]{:S(2)}, u32[]{:S(2)}) collective-permute-start(bf16[256,1152]{1,0:T(8,128)(2,1)S(1)} %far_1.1), channel_id=1, source_target_pairs={{0,2},{1,3},{2,0},{3,1},{4,6},{5,7},{6,4},{7,5},{8,10},{9,11},{10,... | collective-permute-start | bytes 1769480 | tf_op jit(solution)/shard_map/ppermute | solution.py:149
  85.3 13.8 %collective-permute-start.14 = (bf16[256,1152]{1,0:T(8,128)(2,1)S(1)}, bf16[256,1152]{1,0:T(8,128)(2,1)S(1)}, u32[]{:S(2)}, u32[]{:S(2)}) collective-permute-start(bf16[256,1152]{1,0:T(8,128)(2,1)S(1)} %past_0.1), channel_id=1, source_target_pairs={{4,0},{5,1},{6,2},{7,3},{8,4},{9,5},{10,6},{11,7},{12,8},{13,9},{1... | collective-permute-start | bytes 1769480 | tf_op jit(solution)/shard_map/ppermute | solution.py:149
  90.6 21.1 %collective-permute-start.15 = (bf16[256,1152]{1,0:T(8,128)(2,1)S(1)}, bf16[256,1152]{1,0:T(8,128)(2,1)S(1)}, u32[]{:S(2)}, u32[]{:S(2)}) collective-permute-start(bf16[256,1152]{1,0:T(8,128)(2,1)S(1)} %past_1.1), channel_id=1, source_target_pairs={{4,0},{5,1},{6,2},{7,3},{8,4},{9,5},{10,6},{11,7},{12,8},{13,9},{1... | collective-permute-start | bytes 1769480 | tf_op jit(solution)/shard_map/ppermute | solution.py:149

commit v2 on v0

v2 whole, which is shorter than its diff:
```python
import functools

import jax
import jax.numpy as jnp
from jax import lax
from jax.experimental import pallas as pl
from jax.experimental.pallas import tpu as pltpu
from jax.sharding import PartitionSpec as P

AXES = ("dp", "inner")
ROWS = 512
BLOCK = 2048
D = 1152
EXTRA = 16
LOG2E = 1.4426950408889634
FR = ROWS // 2
PIECE = 64
VMEM = pl.BlockSpec(memory_space=pltpu.VMEM)
SMEM = pl.BlockSpec(memory_space=pltpu.SMEM)
HBM = pl.BlockSpec(memory_space=pltpu.HBM)
ANY = pl.BlockSpec(memory_space=pl.ANY)


def routes(dp):
    half = dp // 2

    def crossed(g):
        return 2 if g % half == half - 1 else 0

    every = [(g, i) for g in range(dp) for i in range(4)]
    chip = [(g * 4 + i, g * 4 + (i ^ 2)) for g, i in every]
    core = [(g * 4 + i, g * 4 + (i ^ 1)) for g, i in every]
    ahead = [(g * 4 + i, ((g + 1) % dp) * 4 + (i ^ crossed(g))) for g, i in every]
    behind = [(d, s) for s, d in ahead]
    return chip, core, ahead, behind


def after_body(*refs):
    pass


def after(blocks, earlier):
    return pl.pallas_call(
        after_body,
        out_shape=[jax.ShapeDtypeStruct(b.shape, b.dtype) for b in blocks],
        in_specs=[ANY] * (len(blocks) + len(earlier)),
        out_specs=[ANY] * len(blocks),
        input_output_aliases={k: k for k in range(len(blocks))},
        compiler_params=pltpu.CompilerParams(vmem_limit_bytes=1 << 20),
        cost_estimate=pl.CostEstimate(flops=0, bytes_accessed=0, transcendentals=0),
        name="after",
    )(*blocks, *earlier)


def unit_rows(values):
    values = values.astype(jnp.float32)
    scale = lax.rsqrt(jnp.sum(values * values, axis=1, keepdims=True) + 1e-06)
    return (values * scale).astype(jnp.bfloat16)


def fetch(source, held, sems):
    copies = []
    for at in range(0, ROWS, PIECE):
        copies.append(pltpu.make_async_copy(source.at[pl.ds(at, PIECE)], held.at[pl.ds(at, PIECE)], sems.at[at // PIECE]))
        copies[-1].start()
    return copies


def image_norm_body(pos_ref, a_ref, token, image_0, image_1, held, pos_held, sems, pos_sem):
    pos_copy = pltpu.make_async_copy(pos_ref, pos_held, pos_sem)
    pos_copy.start()
    copies = fetch(a_ref, held, sems)
    pos_copy.wait()
    pos = pos_held[...]
    lines = lax.broadcasted_iota(jnp.int32, (EXTRA, ROWS), 0)
    coded = jnp.zeros((EXTRA, ROWS), jnp.int32)
    for k, digit in enumerate([pos & 63, (pos >> 6) & 63, pos >> 12]):
        coded = jnp.where(lines == k, jnp.broadcast_to(digit, (EXTRA, ROWS)), coded)
    image_0[pl.ds(FR, EXTRA)] = jnp.zeros((EXTRA, D), jnp.bfloat16)
    image_0[pl.ds(FR, EXTRA), pl.ds(0, ROWS)] = coded.astype(jnp.float32).astype(jnp.bfloat16)
    for at, out in zip(range(0, ROWS, FR), (image_0, image_1)):
        for k in range(at // PIECE, (at + FR) // PIECE):
            copies[k].wait()
        out[pl.ds(0, FR)] = unit_rows(held[pl.ds(at, FR)])


def text_norm_body(t_ref, text, held, sems):
    copies = fetch(t_ref, held, sems)
    for at in range(0, ROWS, FR):
        for k in range(at // PIECE, (at + FR) // PIECE):
            copies[k].wait()
        text[pl.ds(at, FR)] = unit_rows(held[pl.ds(at, FR)])


def block(rows, dtype=jnp.bfloat16):
    return pltpu.VMEM((rows, D), dtype)


def params(mib):
    return dict(
        compiler_params=pltpu.CompilerParams(vmem_limit_bytes=mib << 20),
        cost_estimate=pl.CostEstimate(flops=0, bytes_accessed=0, transcendentals=0),
    )


def image_norm(pos, a, earlier):
    hbm = lambda x: pltpu.with_memory_space_constraint(x, pltpu.HBM)
    return pl.pallas_call(
        image_norm_body,
        out_shape=[block(FR + EXTRA), block(FR)],
        in_specs=[HBM, HBM, ANY],
        out_specs=[VMEM, VMEM],
        scratch_shapes=[
            block(ROWS),
            pltpu.VMEM((1, ROWS), jnp.int32),
            pltpu.SemaphoreType.DMA((ROWS // PIECE,)),
            pltpu.SemaphoreType.DMA,
        ],
        name="image_norm",
        **params(16),
    )(hbm(pos), hbm(a), earlier)


def text_norm(t):
    hbm = lambda x: pltpu.with_memory_space_constraint(x, pltpu.HBM)
    return pl.pallas_call(
        text_norm_body,
        out_shape=block(ROWS),
        in_specs=[HBM],
        out_specs=VMEM,
        scratch_shapes=[block(ROWS), pltpu.SemaphoreType.DMA((ROWS // PIECE,))],
        name="text_norm",
        **params(16),
    )(hbm(t))


def rows_of(arrays, pieces):
    loaded = [arrays[a][pl.ds(row, n)] for a, row, n in pieces]
    return loaded[0] if len(loaded) == 1 else jnp.concatenate(loaded, axis=0)


def positions(arrays, place):
    array, row, column = place
    digits = arrays[array][pl.ds(row, EXTRA), pl.ds(column, FR)].astype(jnp.float32)
    return digits[0:1] + 64.0 * digits[1:2] + 4096.0 * digits[2:3]


def gram_rows(scale, shift, base_ref, arrays, xs, ys, given, out, weights, x_is_image):
    slope, level = -LOG2E * scale, -LOG2E * shift
    for i, (xr, xp) in enumerate(xs):
        x = rows_of(arrays, xr)
        if x_is_image:
            mine = jnp.transpose(jnp.broadcast_to(positions(arrays, xp), (128, FR)))
        else:
            mine = (base_ref[xp[0]] + xp[1] + lax.broadcasted_iota(jnp.int32, (FR, 128), 0)).astype(jnp.float32)
        for j, (yr, yp) in enumerate(ys):
            y = rows_of(arrays, yr)
            dots = lax.dot_general(x, y, (((1,), (1,)), ((), ())), preferred_element_type=jnp.float32)
            grown = jnp.exp2(dots * slope + level)
            w = pl.reciprocal(1.0 + grown, approx=True)
            if not x_is_image:
                others = positions(arrays, yp)
            hits = []
            for q in range(FR // 128):
                if x_is_image:
                    first = base_ref[yp[0]] + yp[1] + 128 * q
                    other = (first + lax.broadcasted_iota(jnp.int32, (1, 128), 1)).astype(jnp.float32)
                else:
                    other = others[:, 128 * q : 128 * (q + 1)]
                hits.append(mine == other)
            w = jnp.where(jnp.concatenate(hits, axis=1), w - 1.0, w)
            weights[pl.ds(i * FR, FR), pl.ds(j * FR, FR)] = w.astype(jnp.bfloat16)
    total = 0.0
    for j, (yr, _) in enumerate(ys):
        w = weights[pl.ds(0, len(xs) * FR), pl.ds(j * FR, FR)]
        total = total + jnp.dot(w, rows_of(arrays, yr), preferred_element_type=jnp.float32)
    total = scale * total
    if given is not None:
        total = total + given[0][pl.ds(given[1], len(xs) * FR)]
    out[...] = total.astype(out.dtype)


def gram_body(scale_ref, shift_ref, base_ref, *refs, n, n_given, jobs):
    arrays, given = refs[:n], list(refs[n : n + n_given])
    outs, weights = refs[-1 - len(jobs) : -1], refs[-1]
    for out, (xs, ys, with_sum, x_is_image) in zip(outs, jobs):
        before = (given.pop(0), with_sum[0]) if with_sum else None
        gram_rows(scale_ref[0], shift_ref[0], base_ref, arrays, xs, ys, before, out, weights, x_is_image)


def gram(scalars, jobs, earlier, name, far=False):
    arrays, given, plans, outs = [], [], [], []

    def number(array):
        for k, a in enumerate(arrays):
            if a is array:
                return k
        arrays.append(array)
        return len(arrays) - 1

    def place(part):
        pieces, where = part
        pieces = [(number(a), row, n) for a, row, n in pieces]
        return (pieces, (number(where[0]), *where[1:]) if len(where) == 3 else where)

    for xs, ys, before, dtype, x_is_image in jobs:
        plans.append(([place(p) for p in xs], [place(p) for p in ys], before and before[1:], x_is_image))
        outs.append((pltpu.HBM if far else pltpu.VMEM)((len(xs) * FR, D), dtype))
        if before is not None:
            given.append(before[0])
    rows = max(len(p[0]) for p in plans) * FR
    columns = max(len(p[1]) for p in plans) * FR
    return pl.pallas_call(
        functools.partial(gram_body, n=len(arrays), n_given=len(given), jobs=plans),
        out_shape=outs,
        in_specs=[SMEM] * 3 + [VMEM] * (len(arrays) + len(given)) + [ANY] * len(earlier),
        out_specs=[VMEM] * len(outs),
        scratch_shapes=[pltpu.VMEM((rows, columns), jnp.bfloat16)],
        compiler_params=pltpu.CompilerParams(vmem_limit_bytes=20 << 20),
        cost_estimate=pl.CostEstimate(flops=0, bytes_accessed=0, transcendentals=0),
        name=name,
    )(*scalars, *arrays, *given, *earlier)


def add_body(*refs, start):
    total, got, out, token, held, sems = *refs[:2], *refs[-4:]
    token[...] = jnp.zeros(token.shape, token.dtype)
    copies = []
    for k in range(FR // PIECE):
        rows = pl.ds(k * PIECE, PIECE)
        at = pl.ds(start + k * PIECE, PIECE)
        held[rows] = total[at] + got[rows].astype(jnp.float32)
        copies.append(pltpu.make_async_copy(held.at[rows], out.at[at], sems.at[k]))
        copies[-1].start()
    for copy in copies:
        copy.wait()


def add(total, got, out, start, earlier, name):
    given = [] if out is None else [out]
    return pl.pallas_call(
        functools.partial(add_body, start=start),
        out_shape=[jax.ShapeDtypeStruct((ROWS, D), jnp.float32), jax.ShapeDtypeStruct((8, 128), jnp.float32)],
        in_specs=[VMEM, VMEM] + [HBM] * len(given) + [ANY] * len(earlier),
        out_specs=[HBM, VMEM],
        input_output_aliases={2: 0} if given else {},
        scratch_shapes=[pltpu.VMEM((FR, D), jnp.float32), pltpu.SemaphoreType.DMA((FR // PIECE,))],
        compiler_params=pltpu.CompilerParams(vmem_limit_bytes=16 << 20),
        cost_estimate=pl.CostEstimate(flops=0, bytes_accessed=0, transcendentals=0),
        name=name,
    )(total, got, *given, *earlier)


def shards(picture_vectors, caption_vectors, matching_caption_position, score_multiplier, offset_shift):
    dp = lax.axis_size("dp")
    half = dp // 2
    chip, core, ahead, behind = routes(dp)
    here, inner = lax.axis_index("dp"), lax.axis_index("inner")
    move = lambda block, route: lax.ppermute(block, AXES, route)
    f32, bf16 = jnp.float32, jnp.bfloat16

    past = (here + dp - 1) % dp
    flip = jnp.where(here % half == 0, 2, 0)
    starts = [
        here * BLOCK + inner * ROWS,
        here * BLOCK + (inner ^ 1) * ROWS,
        past * BLOCK + (inner ^ flip) * ROWS,
        past * BLOCK + (inner ^ 1 ^ flip) * ROWS,
    ]
    scalars = (score_multiplier.reshape(1), offset_shift.reshape(1), jnp.stack(starts).astype(jnp.int32))
    pos = matching_caption_position.reshape(1, ROWS)

    run = functools.partial(gram, scalars)
    image_job = lambda xs, ys, given, dtype: (xs, ys, given, dtype, True)
    text_job = lambda xs, ys, given, dtype: (xs, ys, given, dtype, False)
    image_parts = lambda a, b: [([(a, 0, FR)], (a, FR, 0)), ([(b, 0, FR)], (a, FR, FR))]
    text_parts = lambda a, n: [([(a, j * FR, FR)], (n, j * FR)) for j in range(2)]

    text = text_norm(caption_vectors)
    past, text_mate = move(text, ahead), move(text, core)
    image = image_norm(pos, picture_vectors, text)
    far, image_mate = [move(b, chip) for b in image], [move(b, core) for b in image]

    images, texts = image_parts(*image), text_parts(text, 0)
    images_near, texts_near = images + image_parts(*image_mate), texts + text_parts(text_mate, 1)
    image_sum, text_sum = run(
        [image_job(images, texts_near, None, f32), text_job(texts, images_near, None, f32)], [], "near", True
    )
    (far_sum,) = run([image_job(image_parts(*far)[:1], texts_near, None, f32)], [image_sum], "far_near")
    (past,) = after([past], [far_sum])
    past_mate = move(past, core)
    texts_past = text_parts(past, 2)
    texts_there = texts_past + text_parts(past_mate, 3)
    (past_sum,) = run([text_job(texts_past[:1], images_near, None, f32)], [], "past_near")
    far = after(far, [past_sum])
    images_far = image_parts(*far)
    images_there = images_far + image_parts(*[move(b, core) for b in far])
    (far_terms_0,) = run([image_job(images_far[:1], texts_there, (far_sum, 0), bf16)], [past_sum], "far_0")
    far_back_0 = move(far_terms_0, chip)
    (past_terms_0,) = run([text_job(texts_past[:1], images_there, (past_sum, 0), bf16)], [far_terms_0], "past_0")
    past_back_0 = move(past_terms_0, behind)
    (far_terms_1,) = run([image_job(images_far[1:], texts_near + texts_there, None, bf16)], [past_terms_0], "far_1")
    far_back_1 = move(far_terms_1, chip)
    (past_terms_1,) = run([text_job(texts_past[1:], images_near + images_there, None, bf16)], [far_terms_1], "past_1")
    past_back_1 = move(past_terms_1, behind)
    image_sum, text_sum = run(
        [
            image_job(images, texts_there, (image_sum, 0), f32),
            text_job(texts, images_there, (text_sum, 0), f32),
        ],
        [past_terms_1],
        "last",
    )
    out_a, done = add(image_sum, far_back_0, None, 0, [], "image_add_0")
    out_t, done = add(text_sum, past_back_0, None, 0, [done], "text_add_0")
    out_a, done = add(image_sum, far_back_1, out_a, FR, [done], "image_add_1")
    out_t, done = add(text_sum, past_back_1, out_t, FR, [done], "text_add_1")
    return (out_a, out_t)


def solution(mesh):
    return jax.shard_map(
        shards,
        mesh=mesh,
        in_specs=(P(AXES, None), P(AXES, None), P(AXES), P(), P()),
        out_specs=(P(AXES, None), P(AXES, None)),
        check_vma=False,
    )
```

time: 499 us -> 79.2 us (0.16)
  waiting for transfers between devices: 439 us -> 17.3 us
  Pallas kernels: 0 us -> 45.8 us
  matrix products: 37.2 us -> 0 us
  between operations: 15.4 us -> 2.28 us
  starting transfers between devices: 2.71 us -> 11.6 us
    ppermute x2 -> x13, waiting for transfers between devices: 304 us -> 17.3 us  [shards(): move = lambda block, route: lax.ppermute(block, AXES, route)]
    reduce_scatter x1 -> x0, waiting for transfers between devices: 77.1 us -> none  [shards(): lax.psum_scatter(resident_caption_share + returned, 'inner', scatter_dime...]
    all_gather x1 -> x0, waiting for transfers between devices: 57.8 us -> none  [shards(): lax.all_gather(text_norm, 'inner', axis=0, tiled=True)]
    pallas_call x0 -> x16, Pallas kernels: none -> 45.8 us  [the longest x8 36.8 us: gram(): pl.pallas_call(functools.partial(gram_body, n=len(arrays), n_given=len(gi...]
    dot_general x6 -> x0, matrix products: 37.2 us -> none  [the longest x2 12 us: weights(): lax.dot_general(image_norm, caption_tile, (((1,), (1,)), ((), ())), prefe...]
    ppermute x2 -> x13, starting transfers between devices: 2.63 us -> 11.6 us  [shards(): move = lambda block, route: lax.ppermute(block, AXES, route)]
  transfers between devices with their start and end apart: 4 -> 13, of which waited for: 4 -> 6; matrix products, arithmetic and copies ran while one was open for 4% -> 0% of each run, Pallas kernels for 0% -> 54%
where the time goes in v2:
time: 79.2 us; the launch traced here: 78.8 us
  Pallas kernels  45.8 us (58%)
  waiting for transfers between devices  17.3 us (22%)
  starting transfers between devices  11.6 us (15%)
  between operations  2.28 us (3%)
  local copies, waits for them, and re-layouts  1.67 us (2%)
    pallas_call x8, Pallas kernels, gram(): pl.pallas_call(functools.partial(gram_body, n=len(arrays), n_given=len(gi...  36.8 us
    ppermute x13, waiting for transfers between devices, shards(): move = lambda block, route: lax.ppermute(block, AXES, route)  17.3 us
    ppermute x13, starting transfers between devices, shards(): move = lambda block, route: lax.ppermute(block, AXES, route)  11.6 us
    pallas_call x4, Pallas kernels, add(): pl.pallas_call(functools.partial(add_body, start=start), out_shape=[jax.S...  4.87 us
    pallas_call x1, Pallas kernels, image_norm(): pl.pallas_call(image_norm_body, out_shape=[block(FR + EXTRA), block(FR)],...  2.46 us
    unnamed x6, local copies, waits for them, and re-layouts  1.67 us
    pallas_call x1, Pallas kernels, text_norm(): pl.pallas_call(text_norm_body, out_shape=block(ROWS), in_specs=[HBM], out...  1.61 us
  transfers between devices with their start and end apart: 13, of which 6 were waited for; matrix products, arithmetic and copies ran while one was open for 0% of the time, Pallas kernels for 54%

profile of v2, /device:TPU:1, one launch (start us, length us, event | category | flops | bytes accessed | tf_op | source)
XLA Modules:
  0.0 78.8 jit_solution(6185725841917919478)
XLA Ops:
  0.6 1.6 %text_norm.1.token.refs_2_.refs_1_.refs_4_ = bf16[512,1152]{1,0:T(8,128)(2,1)S(1)} custom-call(bf16[512,1152]{1,0:T(8,128)(2,1)} %t_ref.1), custom_call_target="tpu_custom_call" | custom-call | tf_op jit(solution)/shard_map/text_norm/pallas_call | solution.py:126
  2.2 3.3 %collective-permute-start.2 = (bf16[512,1152]{1,0:T(8,128)(2,1)S(1)}, bf16[512,1152]{1,0:T(8,128)(2,1)}, u32[]{:S(2)}, u32[]{:S(2)}) collective-permute-start(bf16[512,1152]{1,0:T(8,128)(2,1)S(1)} %text_norm.1.token.refs_2_.refs_1_.refs_4_), channel_id=1, source_target_pairs={{0,1},{1,0},{2,3},{3,2},{4,5},{5,4},{6,7},{7,6},{8,9},{9,8},{10,11... | collective-permute-start | bytes 3538952 | tf_op jit(solution)/shard_map/ppermute | solution.py:259
  5.6 2.5 %image_norm.1 = (bf16[272,1152]{1,0:T(8,128)(2,1)}, bf16[256,1152]{1,0:T(8,128)(2,1)}) custom-call(s32[1,512]{1,0:T(1,128)} %bitcast.23, bf16[512,1152]{1,0:T(8,128)(2,1)} %a_ref.1, bf16[512,1152]{1,0:T(8,128)(2,1)S(1)} %text_norm.1.token.refs_2_.refs_1_.refs_4_), custom_call_target="tpu_custom_call" | custom-call | tf_op jit(solution)/shard_map/image_norm/pallas_call | solution.py:108
  8.6 0.8 collective-permute-start.1
  9.4 1.1 %collective-permute-done.4.refs_5_.refs_4_ = bf16[256,1152]{1,0:T(8,128)(2,1)} collective-permute-done((bf16[256,1152]{1,0:T(8,128)(2,1)}, bf16[256,1152]{1,0:T(8,128)(2,1)}, u32[]{:S(2)}, u32[]{:S(2)}) %collective-permute-start.4) | collective-permute-done | bytes 589856 | tf_op jit(solution)/shard_map/ppermute | solution.py:259
  10.5 0.8 collective-permute-start.6
  12.7 9.3 %near.1 = (f32[512,1152]{1,0:T(8,128)}, f32[512,1152]{1,0:T(8,128)}) custom-call(f32[1]{0:T(128)} %bitcast.7.scale_ref, f32[1]{0:T(128)} %bitcast.15.shift_ref, s32[4]{0:T(128)S(1)} %pad_add_fusion.base_ref, bf16[272,1152]{1,0:T(8,128)(2,1)} %get-tuple-element.17.refs_0_.refs_1_, bf16[256,1152]{1,0:T(8,128)(2,1)} %get-tuple-element.18.refs_1_.refs_2_, ...), custom_call_target="tpu_custom_call" | custom-call | tf_op jit(solution)/shard_map/near/pallas_call | solution.py:213
  21.9 2.6 %collective-permute-done.1.refs_0_ = bf16[272,1152]{1,0:T(8,128)(2,1)S(1)} collective-permute-done((bf16[272,1152]{1,0:T(8,128)(2,1)}, bf16[272,1152]{1,0:T(8,128)(2,1)S(1)}, u32[]{:S(2)}, u32[]{:S(2)}) %collective-permute-start.1) | collective-permute-done | bytes 626720 | tf_op jit(solution)/shard_map/ppermute | solution.py:259
  24.5 1.7 %copy-done = f32[512,1152]{1,0:T(8,128)S(1)} copy-done((f32[512,1152]{1,0:T(8,128)S(1)}, f32[512,1152]{1,0:T(8,128)}, u32[]{:S(2)}) %copy-start) | copy-done | bytes 2359320
  26.2 2.9 %far_near.1.refs_1_.refs_3_ = f32[256,1152]{1,0:T(8,128)S(1)} custom-call(f32[1]{0:T(128)} %bitcast.8.scale_ref, f32[1]{0:T(128)} %bitcast.16.shift_ref, s32[4]{0:T(128)S(1)} %pad_add_fusion.base_ref, bf16[272,1152]{1,0:T(8,128)(2,1)S(1)} %collective-permute-done.1.refs_0_, bf16[512,1152]{1,0:T(8,128)(2,1)S(1)} %text_norm.1.token.refs_2_.refs_1_.refs_4_, ...), custom_call_target="tpu_custom_call" | custom-call | tf_op jit(solution)/shard_map/far_near/pallas_call | solution.py:213
  29.1 11.2 %collective-permute-done.refs_0_ = bf16[512,1152]{1,0:T(8,128)(2,1)S(1)} collective-permute-done((bf16[512,1152]{1,0:T(8,128)(2,1)S(1)}, bf16[512,1152]{1,0:T(8,128)(2,1)S(1)}, u32[]{:S(2)}, u32[]{:S(2)}) %collective-permute-start) | collective-permute-done | bytes 1179680 | tf_op jit(solution)/shard_map/ppermute | solution.py:259
  41.0 3.2 %past_near.1.refs_2_.refs_4_.refs_5_ = f32[256,1152]{1,0:T(8,128)S(1)} custom-call(f32[1]{0:T(128)} %bitcast.9.scale_ref, f32[1]{0:T(128)} %bitcast.17.shift_ref, s32[4]{0:T(128)S(1)} %pad_add_fusion.base_ref, bf16[512,1152]{1,0:T(8,128)(2,1)S(1)} %after.2.refs_0_.refs_1_.refs_4_.refs_2_, bf16[272,1152]{1,0:T(8,128)(2,1)} %get-tuple-element.17.refs_0_.refs_1_, ...), custom_call_target="tpu_custom_call" | custom-call | tf_op jit(solution)/shard_map/past_near/pallas_call | solution.py:213
  44.9 2.1 %far_0.1.refs_6_ = bf16[256,1152]{1,0:T(8,128)(2,1)S(1)} custom-call(f32[1]{0:T(128)} %bitcast.10.scale_ref, f32[1]{0:T(128)} %bitcast.18.shift_ref, s32[4]{0:T(128)S(1)} %pad_add_fusion.base_ref, bf16[272,1152]{1,0:T(8,128)(2,1)S(1)} %get-tuple-element.20.refs_0_.refs_1_.refs_5_, bf16[512,1152]{1,0:T(8,128)(2,1)S(1)} %after.2.refs_0_.refs_1_.refs_4_.refs_2_, ...), custom_call_target="tpu_custom_call" | custom-call | tf_op jit(solution)/shard_map/far_0/pallas_call | solution.py:213
  47.5 2.7 %past_0.1.refs_6_ = bf16[256,1152]{1,0:T(8,128)(2,1)S(1)} custom-call(f32[1]{0:T(128)} %bitcast.11.scale_ref, f32[1]{0:T(128)} %bitcast.19.shift_ref, s32[4]{0:T(128)S(1)} %pad_add_fusion.base_ref, bf16[512,1152]{1,0:T(8,128)(2,1)S(1)} %after.2.refs_0_.refs_1_.refs_4_.refs_2_, bf16[272,1152]{1,0:T(8,128)(2,1)S(1)} %get-tuple-element.20.refs_0_.refs_1_.refs_5_, ...), custom_call_target="tpu_custom_call" | custom-call | tf_op jit(solution)/shard_map/past_0/pallas_call | solution.py:213
  50.1 2.0 %collective-permute-start.11 = (bf16[256,1152]{1,0:T(8,128)(2,1)S(1)}, bf16[256,1152]{1,0:T(8,128)(2,1)S(1)}, u32[]{:S(2)}, u32[]{:S(2)}) collective-permute-start(bf16[256,1152]{1,0:T(8,128)(2,1)S(1)} %past_0.1.refs_6_), channel_id=1, source_target_pairs={{4,0},{5,1},{6,2},{7,3},{8,4},{9,5},{10,6},{11,7},{12,8},{13,9},{1... | collective-permute-start | bytes 1769480 | tf_op jit(solution)/shard_map/ppermute | solution.py:259
  52.1 4.4 %far_1.1.refs_9_ = bf16[256,1152]{1,0:T(8,128)(2,1)S(1)} custom-call(f32[1]{0:T(128)} %bitcast.12.scale_ref, f32[1]{0:T(128)} %bitcast.20.shift_ref, s32[4]{0:T(128)S(1)} %pad_add_fusion.base_ref, bf16[256,1152]{1,0:T(8,128)(2,1)} %get-tuple-element.21.refs_2_.refs_0_.refs_6_, bf16[272,1152]{1,0:T(8,128)(2,1)S(1)} %get-tuple-element.20.refs_0_.refs_1_.refs_5_, ...), custom_call_target="tpu_custom_call" | custom-call | tf_op jit(solution)/shard_map/far_1/pallas_call | solution.py:213
  57.0 4.9 %past_1.1.refs_11_ = bf16[256,1152]{1,0:T(8,128)(2,1)S(1)} custom-call(f32[1]{0:T(128)} %bitcast.13.scale_ref, f32[1]{0:T(128)} %bitcast.21.shift_ref, s32[4]{0:T(128)S(1)} %pad_add_fusion.base_ref, bf16[512,1152]{1,0:T(8,128)(2,1)S(1)} %after.2.refs_0_.refs_1_.refs_4_.refs_2_, bf16[272,1152]{1,0:T(8,128)(2,1)} %get-tuple-element.17.refs_0_.refs_1_, ...), custom_call_target="tpu_custom_call" | custom-call | tf_op jit(solution)/shard_map/past_1/pallas_call | solution.py:213
  61.9 2.4 %collective-permute-start.12 = (bf16[256,1152]{1,0:T(8,128)(2,1)S(1)}, bf16[256,1152]{1,0:T(8,128)(2,1)S(1)}, u32[]{:S(2)}, u32[]{:S(2)}) collective-permute-start(bf16[256,1152]{1,0:T(8,128)(2,1)S(1)} %past_1.1.refs_11_), channel_id=1, source_target_pairs={{4,0},{5,1},{6,2},{7,3},{8,4},{9,5},{10,6},{11,7},{12,8},{13,9},{1... | collective-permute-start | bytes 1769480 | tf_op jit(solution)/shard_map/ppermute | solution.py:259
  64.3 7.3 %last.1 = (f32[512,1152]{1,0:T(8,128)S(1)}, f32[512,1152]{1,0:T(8,128)S(1)}) custom-call(f32[1]{0:T(128)} %bitcast.14.scale_ref, f32[1]{0:T(128)} %bitcast.22.shift_ref, s32[4]{0:T(128)S(1)} %pad_add_fusion.base_ref, bf16[272,1152]{1,0:T(8,128)(2,1)} %get-tuple-element.17.refs_0_.refs_1_, bf16[256,1152]{1,0:T(8,128)(2,1)} %get-tuple-element.18.refs_1_.refs_2_, ...), custom_call_target="tpu_custom_call" | custom-call | tf_op jit(solution)/shard_map/last/pallas_call | solution.py:213
  71.6 1.1 %image_add_0.1 = (f32[512,1152]{1,0:T(8,128)}, f32[8,128]{1,0:T(8,128)S(1)}) custom-call(f32[512,1152]{1,0:T(8,128)S(1)} %get-tuple-element.23.refs_0_, bf16[256,1152]{1,0:T(8,128)(2,1)S(1)} %collective-permute-done.10.refs_1_), custom_call_target="tpu_custom_call" | custom-call | tf_op jit(solution)/shard_map/image_add_0/pallas_call | solution.py:241
  72.7 1.1 %text_add_0.1 = (f32[512,1152]{1,0:T(8,128)}, f32[8,128]{1,0:T(8,128)S(1)}) custom-call(f32[512,1152]{1,0:T(8,128)S(1)} %get-tuple-element.25.refs_0_, bf16[256,1152]{1,0:T(8,128)(2,1)S(1)} %collective-permute-done.11.refs_1_, f32[8,128]{1,0:T(8,128)S(1)} %get-tuple-element.26.refs_2_), custom_call_target="tpu_custom_call" | custom-call | tf_op jit(solution)/shard_map/text_add_0/pallas_call | solution.py:241
  74.6 1.1 %image_add_1.1 = (f32[512,1152]{1,0:T(8,128)}, f32[8,128]{1,0:T(8,128)S(1)}) custom-call(f32[512,1152]{1,0:T(8,128)S(1)} %get-tuple-element.23.refs_0_, bf16[256,1152]{1,0:T(8,128)(2,1)S(1)} %collective-permute-done.9.refs_1_, f32[512,1152]{1,0:T(8,128)} %get-tuple-element.24.refs_2_, ...), custom_call_target="tpu_custom_call", output_to_operand_aliasing={{0}: (2, {})} | custom-call | tf_op jit(solution)/shard_map/image_add_1/pallas_call | solution.py:241
  75.7 1.3 %collective-permute-done.12.refs_1_ = bf16[256,1152]{1,0:T(8,128)(2,1)S(1)} collective-permute-done((bf16[256,1152]{1,0:T(8,128)(2,1)S(1)}, bf16[256,1152]{1,0:T(8,128)(2,1)S(1)}, u32[]{:S(2)}, u32[]{:S(2)}) %collective-permute-start.12) | collective-permute-done | bytes 589856 | tf_op jit(solution)/shard_map/ppermute | solution.py:259
  76.9 1.7 %text_add_1.1 = (f32[512,1152]{1,0:T(8,128)}, f32[8,128]{1,0:T(8,128)}) custom-call(f32[512,1152]{1,0:T(8,128)S(1)} %get-tuple-element.25.refs_0_, bf16[256,1152]{1,0:T(8,128)(2,1)S(1)} %collective-permute-done.12.refs_1_, f32[512,1152]{1,0:T(8,128)} %get-tuple-element.29.refs_2_, ...), custom_call_target="tpu_custom_call", output_to_operand_aliasing={{0}: (2, {})} | custom-call | tf_op jit(solution)/shard_map/text_add_1/pallas_call | solution.py:241
  (25 shorter events, 3.7 us)
Async XLA Ops:
  2.2 10.4 %collective-permute-start.2 = (bf16[512,1152]{1,0:T(8,128)(2,1)S(1)}, bf16[512,1152]{1,0:T(8,128)(2,1)}, u32[]{:S(2)}, u32[]{:S(2)}) collective-permute-start(bf16[512,1152]{1,0:T(8,128)(2,1)S(1)} %text_norm.1.token.refs_2_.refs_1_.refs_4_), channel_id=1, source_target_pairs={{0,1},{1,0},{2,3},{3,2},{4,5},{5,4},{6,7},{7,6},{8,9},{9,8},{10,11... | collective-permute-start | bytes 3538952 | tf_op jit(solution)/shard_map/ppermute | solution.py:259
  5.6 34.7 %collective-permute-start = (bf16[512,1152]{1,0:T(8,128)(2,1)S(1)}, bf16[512,1152]{1,0:T(8,128)(2,1)S(1)}, u32[]{:S(2)}, u32[]{:S(2)}) collective-permute-start(bf16[512,1152]{1,0:T(8,128)(2,1)S(1)} %text_norm.1.token.refs_2_.refs_1_.refs_4_), channel_id=1, source_target_pairs={{0,4},{1,5},{2,6},{3,7},{4,8},{5,9},{6,10},{7,11},{8,12},{9,13},{1... | collective-permute-start | bytes 3538952 | tf_op jit(solution)/shard_map/ppermute | solution.py:259
  8.0 2.4 %collective-permute-start.4 = (bf16[256,1152]{1,0:T(8,128)(2,1)}, bf16[256,1152]{1,0:T(8,128)(2,1)}, u32[]{:S(2)}, u32[]{:S(2)}) collective-permute-start(bf16[256,1152]{1,0:T(8,128)(2,1)} %get-tuple-element.18.refs_1_.refs_2_), channel_id=1, source_target_pairs={{0,1},{1,0},{2,3},{3,2},{4,5},{5,4},{6,7},{7,6},{8,9},{9,8},{10,11... | collective-permute-start | bytes 1769480 | tf_op jit(solution)/shard_map/ppermute | solution.py:259
  8.2 4.4 %collective-permute-start.3 = (bf16[272,1152]{1,0:T(8,128)(2,1)}, bf16[272,1152]{1,0:T(8,128)(2,1)}, u32[]{:S(2)}, u32[]{:S(2)}) collective-permute-start(bf16[272,1152]{1,0:T(8,128)(2,1)} %get-tuple-element.17.refs_0_.refs_1_), channel_id=1, source_target_pairs={{0,1},{1,0},{2,3},{3,2},{4,5},{5,4},{6,7},{7,6},{8,9},{9,8},{10,11... | collective-permute-start | bytes 1880072 | tf_op jit(solution)/shard_map/ppermute | solution.py:259
  8.6 15.9 %collective-permute-start.1 = (bf16[272,1152]{1,0:T(8,128)(2,1)}, bf16[272,1152]{1,0:T(8,128)(2,1)S(1)}, u32[]{:S(2)}, u32[]{:S(2)}) collective-permute-start(bf16[272,1152]{1,0:T(8,128)(2,1)} %get-tuple-element.17.refs_0_.refs_1_), channel_id=1, source_target_pairs={{0,2},{1,3},{2,0},{3,1},{4,6},{5,7},{6,4},{7,5},{8,10},{9,11},{10,... | collective-permute-start | bytes 1880072 | tf_op jit(solution)/shard_map/ppermute | solution.py:259
  10.5 33.8 %collective-permute-start.6 = (bf16[256,1152]{1,0:T(8,128)(2,1)}, bf16[256,1152]{1,0:T(8,128)(2,1)}, u32[]{:S(2)}, u32[]{:S(2)}) collective-permute-start(bf16[256,1152]{1,0:T(8,128)(2,1)} %get-tuple-element.18.refs_1_.refs_2_), channel_id=1, source_target_pairs={{0,2},{1,3},{2,0},{3,1},{4,6},{5,7},{6,4},{7,5},{8,10},{9,11},{10,... | collective-permute-start | bytes 1769480 | tf_op jit(solution)/shard_map/ppermute | solution.py:259
  24.5 1.7 %copy-start = (f32[512,1152]{1,0:T(8,128)S(1)}, f32[512,1152]{1,0:T(8,128)}, u32[]{:S(2)}) copy-start(f32[512,1152]{1,0:T(8,128)} %get-tuple-element.19.refs_3_.refs_9_) | copy-start | bytes 7077892
  40.3 4.5 %collective-permute-start.5 = (bf16[512,1152]{1,0:T(8,128)(2,1)S(1)}, bf16[512,1152]{1,0:T(8,128)(2,1)S(1)}, u32[]{:S(2)}, u32[]{:S(2)}) collective-permute-start(bf16[512,1152]{1,0:T(8,128)(2,1)S(1)} %after.2.refs_0_.refs_1_.refs_4_.refs_2_), channel_id=1, source_target_pairs={{0,1},{1,0},{2,3},{3,2},{4,5},{5,4},{6,7},{7,6},{8,9},{9,8},{10,11... | collective-permute-start | bytes 3538952 | tf_op jit(solution)/shard_map/ppermute | solution.py:259
  44.3 3.2 %collective-permute-start.7 = (bf16[272,1152]{1,0:T(8,128)(2,1)S(1)}, bf16[272,1152]{1,0:T(8,128)(2,1)S(1)}, u32[]{:S(2)}, u32[]{:S(2)}) collective-permute-start(bf16[272,1152]{1,0:T(8,128)(2,1)S(1)} %get-tuple-element.20.refs_0_.refs_1_.refs_5_), channel_id=1, source_target_pairs={{0,1},{1,0},{2,3},{3,2},{4,5},{5,4},{6,7},{7,6},{8,9},{9,8},{10,11... | collective-permute-start | bytes 1880072 | tf_op jit(solution)/shard_map/ppermute | solution.py:259
  44.4 3.1 %collective-permute-start.8 = (bf16[256,1152]{1,0:T(8,128)(2,1)}, bf16[256,1152]{1,0:T(8,128)(2,1)S(1)}, u32[]{:S(2)}, u32[]{:S(2)}) collective-permute-start(bf16[256,1152]{1,0:T(8,128)(2,1)} %get-tuple-element.21.refs_2_.refs_0_.refs_6_), channel_id=1, source_target_pairs={{0,1},{1,0},{2,3},{3,2},{4,5},{5,4},{6,7},{7,6},{8,9},{9,8},{10,11... | collective-permute-start | bytes 1769480 | tf_op jit(solution)/shard_map/ppermute | solution.py:259
  47.0 24.6 %collective-permute-start.10 = (bf16[256,1152]{1,0:T(8,128)(2,1)S(1)}, bf16[256,1152]{1,0:T(8,128)(2,1)S(1)}, u32[]{:S(2)}, u32[]{:S(2)}) collective-permute-start(bf16[256,1152]{1,0:T(8,128)(2,1)S(1)} %far_0.1.refs_6_), channel_id=1, source_target_pairs={{0,2},{1,3},{2,0},{3,1},{4,6},{5,7},{6,4},{7,5},{8,10},{9,11},{10,... | collective-permute-start | bytes 1769480 | tf_op jit(solution)/shard_map/ppermute | solution.py:259
  50.1 22.6 %collective-permute-start.11 = (bf16[256,1152]{1,0:T(8,128)(2,1)S(1)}, bf16[256,1152]{1,0:T(8,128)(2,1)S(1)}, u32[]{:S(2)}, u32[]{:S(2)}) collective-permute-start(bf16[256,1152]{1,0:T(8,128)(2,1)S(1)} %past_0.1.refs_6_), channel_id=1, source_target_pairs={{4,0},{5,1},{6,2},{7,3},{8,4},{9,5},{10,6},{11,7},{12,8},{13,9},{1... | collective-permute-start | bytes 1769480 | tf_op jit(solution)/shard_map/ppermute | solution.py:259
  56.5 18.1 %collective-permute-start.9 = (bf16[256,1152]{1,0:T(8,128)(2,1)S(1)}, bf16[256,1152]{1,0:T(8,128)(2,1)S(1)}, u32[]{:S(2)}, u32[]{:S(2)}) collective-permute-start(bf16[256,1152]{1,0:T(8,128)(2,1)S(1)} %far_1.1.refs_9_), channel_id=1, source_target_pairs={{0,2},{1,3},{2,0},{3,1},{4,6},{5,7},{6,4},{7,5},{8,10},{9,11},{10,... | collective-permute-start | bytes 1769480 | tf_op jit(solution)/shard_map/ppermute | solution.py:259
  57.0 7.3 %copy-start.1 = (f32[512,1152]{1,0:T(8,128)S(1)}, f32[512,1152]{1,0:T(8,128)}, u32[]{:S(2)}) copy-start(f32[512,1152]{1,0:T(8,128)} %get-tuple-element.19.refs_3_.refs_9_) | copy-start | bytes 7077892
  57.0 7.3 %copy-start.2 = (f32[512,1152]{1,0:T(8,128)S(1)}, f32[512,1152]{1,0:T(8,128)}, u32[]{:S(2)}) copy-start(f32[512,1152]{1,0:T(8,128)} %get-tuple-element.22.refs_10_) | copy-start | bytes 7077892
  61.9 15.0 %collective-permute-start.12 = (bf16[256,1152]{1,0:T(8,128)(2,1)S(1)}, bf16[256,1152]{1,0:T(8,128)(2,1)S(1)}, u32[]{:S(2)}, u32[]{:S(2)}) collective-permute-start(bf16[256,1152]{1,0:T(8,128)(2,1)S(1)} %past_1.1.refs_11_), channel_id=1, source_target_pairs={{4,0},{5,1},{6,2},{7,3},{8,4},{9,5},{10,6},{11,7},{12,8},{13,9},{1... | collective-permute-start | bytes 1769480 | tf_op jit(solution)/shard_map/ppermute | solution.py:259

commit v3 on v2

--- a/solution.py
+++ b/solution.py
@@ -84,6 +84,35 @@
         out[pl.ds(0, FR)] = unit_rows(held[pl.ds(at, FR)])
 
 
+def hbm(x):
+    return pltpu.with_memory_space_constraint(x, pltpu.HBM)
+
+
+def scalar_body(scale_ref, shift_ref, out, dp):
+    here, inner = lax.axis_index("dp"), lax.axis_index("inner")
+    past = lax.rem(here + dp - 1, dp)
+    flip = jnp.where(lax.rem(here, dp // 2) == 0, 2, 0)
+    values = [scale_ref[0], shift_ref[0]]
+    for block_index, role in ((here, inner), (here, inner ^ 1), (past, inner ^ flip), (past, inner ^ flip ^ 1)):
+        values.append((block_index * BLOCK + role * ROWS).astype(jnp.float32))
+    lanes = lax.broadcasted_iota(jnp.int32, (8, 128), 1)
+    found = jnp.zeros((8, 128), jnp.float32)
+    for k, value in enumerate(values):
+        found = jnp.where(lanes == k, value, found)
+    out[...] = found
+
+
+def scalar_block(scale, shift):
+    return pl.pallas_call(
+        functools.partial(scalar_body, dp=lax.axis_size("dp")),
+        out_shape=pltpu.VMEM((8, 128), jnp.float32),
+        in_specs=[SMEM, SMEM],
+        out_specs=VMEM,
+        name="scalars",
+        **params(1),
+    )(scale, shift)
+
+
 def text_norm_body(t_ref, text, held, sems):
     copies = fetch(t_ref, held, sems)
     for at in range(0, ROWS, FR):
@@ -104,7 +133,6 @@
 
 
 def image_norm(pos, a, earlier):
-    hbm = lambda x: pltpu.with_memory_space_constraint(x, pltpu.HBM)
     return pl.pallas_call(
         image_norm_body,
         out_shape=[block(FR + EXTRA), block(FR)],
@@ -122,7 +150,6 @@
 
 
 def text_norm(t):
-    hbm = lambda x: pltpu.with_memory_space_constraint(x, pltpu.HBM)
     return pl.pallas_call(
         text_norm_body,
         out_shape=block(ROWS),
@@ -145,14 +172,15 @@
     return digits[0:1] + 64.0 * digits[1:2] + 4096.0 * digits[2:3]
 
 
-def gram_rows(scale, shift, base_ref, arrays, xs, ys, given, out, weights, x_is_image):
+def gram_rows(scalar, arrays, xs, ys, given, out, weights, x_is_image):
+    scale, shift, *bases = scalar
     slope, level = -LOG2E * scale, -LOG2E * shift
     for i, (xr, xp) in enumerate(xs):
         x = rows_of(arrays, xr)
         if x_is_image:
             mine = jnp.transpose(jnp.broadcast_to(positions(arrays, xp), (128, FR)))
         else:
-            mine = (base_ref[xp[0]] + xp[1] + lax.broadcasted_iota(jnp.int32, (FR, 128), 0)).astype(jnp.float32)
+            mine = bases[xp[0]] + (xp[1] + lax.broadcasted_iota(jnp.int32, (FR, 128), 0)).astype(jnp.float32)
         for j, (yr, yp) in enumerate(ys):
             y = rows_of(arrays, yr)
             dots = lax.dot_general(x, y, (((1,), (1,)), ((), ())), preferred_element_type=jnp.float32)
@@ -163,8 +191,8 @@
             hits = []
             for q in range(FR // 128):
                 if x_is_image:
-                    first = base_ref[yp[0]] + yp[1] + 128 * q
-                    other = (first + lax.broadcasted_iota(jnp.int32, (1, 128), 1)).astype(jnp.float32)
+                    columns = yp[1] + 128 * q + lax.broadcasted_iota(jnp.int32, (1, 128), 1)
+                    other = bases[yp[0]] + columns.astype(jnp.float32)
                 else:
                     other = others[:, 128 * q : 128 * (q + 1)]
                 hits.append(mine == other)
@@ -180,15 +208,19 @@
     out[...] = total.astype(out.dtype)
 
 
-def gram_body(scale_ref, shift_ref, base_ref, *refs, n, n_given, jobs):
-    arrays, given = refs[:n], list(refs[n : n + n_given])
-    outs, weights = refs[-1 - len(jobs) : -1], refs[-1]
+def gram_body(scalar_ref, *refs, n, n_given, jobs, kept):
+    arrays = refs[:n]
+    scalar = [scalar_ref[0:1, k : k + 1] for k in range(6)]
+    given = list(refs[n : n + n_given])
+    outs, extras, weights = refs[-1 - len(jobs) - len(kept) : -1 - len(kept)], refs[-1 - len(kept) : -1], refs[-1]
+    for k, extra in zip(kept, extras):
+        extra[...] = arrays[k][...]
     for out, (xs, ys, with_sum, x_is_image) in zip(outs, jobs):
         before = (given.pop(0), with_sum[0]) if with_sum else None
-        gram_rows(scale_ref[0], shift_ref[0], base_ref, arrays, xs, ys, before, out, weights, x_is_image)
-
-
-def gram(scalars, jobs, earlier, name, far=False):
+        gram_rows(scalar, arrays, xs, ys, before, out, weights, x_is_image)
+
+
+def gram(scalars, jobs, earlier, name, far=False, keep=()):
     arrays, given, plans, outs = [], [], [], []
 
     def number(array):
@@ -208,23 +240,23 @@
         outs.append((pltpu.HBM if far else pltpu.VMEM)((len(xs) * FR, D), dtype))
         if before is not None:
             given.append(before[0])
+    kept = [number(a) for a in keep]
     rows = max(len(p[0]) for p in plans) * FR
     columns = max(len(p[1]) for p in plans) * FR
     return pl.pallas_call(
-        functools.partial(gram_body, n=len(arrays), n_given=len(given), jobs=plans),
-        out_shape=outs,
-        in_specs=[SMEM] * 3 + [VMEM] * (len(arrays) + len(given)) + [ANY] * len(earlier),
-        out_specs=[VMEM] * len(outs),
+        functools.partial(gram_body, n=len(arrays), n_given=len(given), jobs=plans, kept=kept),
+        out_shape=outs + [block(a.shape[0]) for a in keep],
+        in_specs=[VMEM] * (1 + len(arrays) + len(given)) + [ANY] * len(earlier),
+        out_specs=[VMEM] * (len(outs) + len(keep)),
         scratch_shapes=[pltpu.VMEM((rows, columns), jnp.bfloat16)],
         compiler_params=pltpu.CompilerParams(vmem_limit_bytes=20 << 20),
         cost_estimate=pl.CostEstimate(flops=0, bytes_accessed=0, transcendentals=0),
         name=name,
-    )(*scalars, *arrays, *given, *earlier)
+    )(scalars, *arrays, *given, *earlier)
 
 
 def add_body(*refs, start):
-    total, got, out, token, held, sems = *refs[:2], *refs[-4:]
-    token[...] = jnp.zeros(token.shape, token.dtype)
+    total, got, out, held, sems = *refs[:2], *refs[-3:]
     copies = []
     for k in range(FR // PIECE):
         rows = pl.ds(k * PIECE, PIECE)
@@ -240,34 +272,23 @@
     given = [] if out is None else [out]
     return pl.pallas_call(
         functools.partial(add_body, start=start),
-        out_shape=[jax.ShapeDtypeStruct((ROWS, D), jnp.float32), jax.ShapeDtypeStruct((8, 128), jnp.float32)],
-        in_specs=[VMEM, VMEM] + [HBM] * len(given) + [ANY] * len(earlier),
-        out_specs=[HBM, VMEM],
+        out_shape=jax.ShapeDtypeStruct((ROWS, D), jnp.float32),
+        in_specs=[VMEM, VMEM] + [HBM] * (len(given) + len(earlier)),
+        out_specs=HBM,
         input_output_aliases={2: 0} if given else {},
         scratch_shapes=[pltpu.VMEM((FR, D), jnp.float32), pltpu.SemaphoreType.DMA((FR // PIECE,))],
-        compiler_params=pltpu.CompilerParams(vmem_limit_bytes=16 << 20),
-        cost_estimate=pl.CostEstimate(flops=0, bytes_accessed=0, transcendentals=0),
         name=name,
-    )(total, got, *given, *earlier)
+        **params(16),
+    )(total, got, *[hbm(x) for x in given + earlier])
 
 
 def shards(picture_vectors, caption_vectors, matching_caption_position, score_multiplier, offset_shift):
     dp = lax.axis_size("dp")
-    half = dp // 2
     chip, core, ahead, behind = routes(dp)
-    here, inner = lax.axis_index("dp"), lax.axis_index("inner")
+    f32, bf16 = jnp.float32, jnp.bfloat16
     move = lambda block, route: lax.ppermute(block, AXES, route)
-    f32, bf16 = jnp.float32, jnp.bfloat16
-
-    past = (here + dp - 1) % dp
-    flip = jnp.where(here % half == 0, 2, 0)
-    starts = [
-        here * BLOCK + inner * ROWS,
-        here * BLOCK + (inner ^ 1) * ROWS,
-        past * BLOCK + (inner ^ flip) * ROWS,
-        past * BLOCK + (inner ^ 1 ^ flip) * ROWS,
-    ]
-    scalars = (score_multiplier.reshape(1), offset_shift.reshape(1), jnp.stack(starts).astype(jnp.int32))
+
+    scalars = scalar_block(score_multiplier.reshape(1), offset_shift.reshape(1))
     pos = matching_caption_position.reshape(1, ROWS)
 
     run = functools.partial(gram, scalars)
@@ -278,7 +299,7 @@
 
     text = text_norm(caption_vectors)
     past, text_mate = move(text, ahead), move(text, core)
-    image = image_norm(pos, picture_vectors, text)
+    image = list(image_norm(pos, picture_vectors, text))
     far, image_mate = [move(b, chip) for b in image], [move(b, core) for b in image]
 
     images, texts = image_parts(*image), text_parts(text, 0)
@@ -286,22 +307,32 @@
     image_sum, text_sum = run(
         [image_job(images, texts_near, None, f32), text_job(texts, images_near, None, f32)], [], "near", True
     )
-    (far_sum,) = run([image_job(image_parts(*far)[:1], texts_near, None, f32)], [image_sum], "far_near")
+    far_sum, *copies = run(
+        [image_job(image_parts(*far)[:1], texts_near, None, f32)], [hbm(image_sum)], "far_near", keep=image + image_mate
+    )
     (past,) = after([past], [far_sum])
     past_mate = move(past, core)
     texts_past = text_parts(past, 2)
     texts_there = texts_past + text_parts(past_mate, 3)
-    (past_sum,) = run([text_job(texts_past[:1], images_near, None, f32)], [], "past_near")
+    (past_sum,) = run(
+        [text_job(texts_past[:1], image_parts(*copies[:2]) + image_parts(*copies[2:]), None, f32)], [], "past_near"
+    )
     far = after(far, [past_sum])
     images_far = image_parts(*far)
     images_there = images_far + image_parts(*[move(b, core) for b in far])
     (far_terms_0,) = run([image_job(images_far[:1], texts_there, (far_sum, 0), bf16)], [past_sum], "far_0")
     far_back_0 = move(far_terms_0, chip)
-    (past_terms_0,) = run([text_job(texts_past[:1], images_there, (past_sum, 0), bf16)], [far_terms_0], "past_0")
+    (past_terms_0,) = run(
+        [text_job(texts_past[:1], images_there, (past_sum, 0), bf16)], [far_terms_0], "past_0"
+    )
     past_back_0 = move(past_terms_0, behind)
-    (far_terms_1,) = run([image_job(images_far[1:], texts_near + texts_there, None, bf16)], [past_terms_0], "far_1")
+    (far_terms_1,) = run(
+        [image_job(images_far[1:], texts_there + texts_near, None, bf16)], [past_terms_0], "far_1"
+    )
     far_back_1 = move(far_terms_1, chip)
-    (past_terms_1,) = run([text_job(texts_past[1:], images_near + images_there, None, bf16)], [far_terms_1], "past_1")
+    (past_terms_1,) = run(
+        [text_job(texts_past[1:], images_there + images_near, None, bf16)], [far_terms_1], "past_1"
+    )
     past_back_1 = move(past_terms_1, behind)
     image_sum, text_sum = run(
         [
@@ -311,10 +342,10 @@
         [past_terms_1],
         "last",
     )
-    out_a, done = add(image_sum, far_back_0, None, 0, [], "image_add_0")
-    out_t, done = add(text_sum, past_back_0, None, 0, [done], "text_add_0")
-    out_a, done = add(image_sum, far_back_1, out_a, FR, [done], "image_add_1")
-    out_t, done = add(text_sum, past_back_1, out_t, FR, [done], "text_add_1")
+    out_a = add(image_sum, far_back_0, None, 0, [], "image_add_0")
+    out_t = add(text_sum, past_back_0, None, 0, [out_a], "text_add_0")
+    out_a = add(image_sum, far_back_1, out_a, FR, [out_t], "image_add_1")
+    out_t = add(text_sum, past_back_1, out_t, FR, [out_a], "text_add_1")
     return (out_a, out_t)
 
 

time: 79.2 us -> 78.1 us (0.986)
  Pallas kernels: 45.8 us -> 44 us
  starting transfers between devices: 11.6 us -> 12.7 us
    pallas_call x8, Pallas kernels: 36.8 us -> 35.6 us  [gram(): pl.pallas_call(functools.partial(gram_body, n=len(arrays), n_given=len(gi...]
    ppermute x13, starting transfers between devices: 11.6 us -> 12.7 us  [shards(): move = lambda block, route: lax.ppermute(block, AXES, route)]
    pallas_call x4 -> x5, Pallas kernels: 4.87 us -> 4.29 us  [the longest x4 4.27 us: add(): pl.pallas_call(functools.partial(add_body, start=start), out_shape=jax.Sh...]
    unnamed x6 -> x10, local copies, waits for them, and re-layouts: 1.67 us -> 1.89 us
  transfers between devices with their start and end apart: 13 -> 13, of which waited for: 6 -> 5; matrix products, arithmetic and copies ran while one was open for 0% -> 0% of each run, Pallas kernels for 54% -> 53%
where the time goes in v3:
time: 78.1 us; the launch traced here: 77.7 us
  Pallas kernels  44 us (56%)
  waiting for transfers between devices  16.8 us (22%)
  starting transfers between devices  12.7 us (16%)
  between operations  2.34 us (3%)
  local copies, waits for them, and re-layouts  1.89 us (2%)
    pallas_call x8, Pallas kernels, gram(): pl.pallas_call(functools.partial(gram_body, n=len(arrays), n_given=len(gi...  35.6 us
    ppermute x13, waiting for transfers between devices, shards(): move = lambda block, route: lax.ppermute(block, AXES, route)  16.8 us
    ppermute x13, starting transfers between devices, shards(): move = lambda block, route: lax.ppermute(block, AXES, route)  12.7 us
    pallas_call x4, Pallas kernels, add(): pl.pallas_call(functools.partial(add_body, start=start), out_shape=jax.Sh...  4.27 us
    pallas_call x1, Pallas kernels, image_norm(): pl.pallas_call(image_norm_body, out_shape=[block(FR + EXTRA), block(FR)],...  2.46 us
    unnamed x10, local copies, waits for them, and re-layouts  1.89 us
    pallas_call x1, Pallas kernels, text_norm(): pl.pallas_call(text_norm_body, out_shape=block(ROWS), in_specs=[HBM], out...  1.61 us
  transfers between devices with their start and end apart: 13, of which 5 were waited for; matrix products, arithmetic and copies ran while one was open for 0% of the time, Pallas kernels for 53%

profile of v3, /device:TPU:1, one launch (start us, length us, event | category | flops | bytes accessed | tf_op | source)
XLA Modules:
  0.0 77.7 jit_solution(4300833297648268521)
XLA Ops:
  0.6 1.6 %text_norm.1.token.refs_2_.refs_1_.refs_4_ = bf16[512,1152]{1,0:T(8,128)(2,1)S(1)} custom-call(bf16[512,1152]{1,0:T(8,128)(2,1)} %t_ref.1), custom_call_target="tpu_custom_call" | custom-call | tf_op jit(solution)/shard_map/text_norm/pallas_call | solution.py:153
  2.2 3.3 %collective-permute-start.2 = (bf16[512,1152]{1,0:T(8,128)(2,1)S(1)}, bf16[512,1152]{1,0:T(8,128)(2,1)}, u32[]{:S(2)}, u32[]{:S(2)}) collective-permute-start(bf16[512,1152]{1,0:T(8,128)(2,1)S(1)} %text_norm.1.token.refs_2_.refs_1_.refs_4_), channel_id=1, source_target_pairs={{0,1},{1,0},{2,3},{3,2},{4,5},{5,4},{6,7},{7,6},{8,9},{9,8},{10,11... | collective-permute-start | bytes 3538952 | tf_op jit(solution)/shard_map/ppermute | solution.py:289
  5.6 2.5 %image_norm.1 = (bf16[272,1152]{1,0:T(8,128)(2,1)}, bf16[256,1152]{1,0:T(8,128)(2,1)}) custom-call(s32[1,512]{1,0:T(1,128)} %bitcast.5, bf16[512,1152]{1,0:T(8,128)(2,1)} %a_ref.1, bf16[512,1152]{1,0:T(8,128)(2,1)S(1)} %text_norm.1.token.refs_2_.refs_1_.refs_4_), custom_call_target="tpu_custom_call" | custom-call | tf_op jit(solution)/shard_map/image_norm/pallas_call | solution.py:136
  8.2 1.0 %collective-permute-start.1 = (bf16[272,1152]{1,0:T(8,128)(2,1)}, bf16[272,1152]{1,0:T(8,128)(2,1)S(1)}, u32[]{:S(2)}, u32[]{:S(2)}) collective-permute-start(bf16[272,1152]{1,0:T(8,128)(2,1)} %get-tuple-element.15.refs_0_.refs_3_.refs_5_), channel_id=1, source_target_pairs={{0,2},{1,3},{2,0},{3,1},{4,6},{5,7},{6,4},{7,5},{8,10},{9,11},{10,... | collective-permute-start | bytes 1880072 | tf_op jit(solution)/shard_map/ppermute | solution.py:289
  9.7 1.8 %collective-permute-done.4.refs_5_.refs_6_.refs_8_ = bf16[256,1152]{1,0:T(8,128)(2,1)S(1)} collective-permute-done((bf16[256,1152]{1,0:T(8,128)(2,1)}, bf16[256,1152]{1,0:T(8,128)(2,1)S(1)}, u32[]{:S(2)}, u32[]{:S(2)}) %collective-permute-start.4) | collective-permute-done | bytes 589856 | tf_op jit(solution)/shard_map/ppermute | solution.py:289
  11.6 0.8 %copy-done.1 = bf16[256,1152]{1,0:T(8,128)(2,1)} copy-done((bf16[256,1152]{1,0:T(8,128)(2,1)}, bf16[256,1152]{1,0:T(8,128)(2,1)S(1)}, u32[]{:S(2)}) %copy-start.1) | copy-done | bytes 589848
  14.4 1.1 %copy-done.2 = bf16[256,1152]{1,0:T(8,128)(2,1)S(1)} copy-done((bf16[256,1152]{1,0:T(8,128)(2,1)S(1)}, bf16[256,1152]{1,0:T(8,128)(2,1)}, u32[]{:S(2)}) %copy-start.2) | copy-done | bytes 589848
  15.5 9.6 %near.1 = (f32[512,1152]{1,0:T(8,128)}, f32[512,1152]{1,0:T(8,128)}) custom-call(f32[8,128]{1,0:T(8,128)S(1)} %scalars.1.scalar_ref, bf16[272,1152]{1,0:T(8,128)(2,1)} %get-tuple-element.15.refs_0_.refs_3_.refs_5_, bf16[256,1152]{1,0:T(8,128)(2,1)} %get-tuple-element.16.refs_1_.refs_4_.refs_6_, bf16[512,1152]{1,0:T(8,128)(2,1)S(1)} %text_norm.1.token.refs_2_.refs_1_.refs_4_, ...), custom_call_target="tpu_custom_call" | custom-call | tf_op jit(solution)/shard_map/near/pallas_call | solution.py:246
  25.0 3.6 %far_near.1 = (f32[256,1152]{1,0:T(8,128)S(1)}, bf16[272,1152]{1,0:T(8,128)(2,1)S(1)}, bf16[256,1152]{1,0:T(8,128)(2,1)S(1)}, bf16[272,1152]{1,0:T(8,128)(2,1)S(1)}, bf16[256,1152]{1,0:T(8,128)(2,1)S(1)}) custom-call(f32[8,128]{1,0:T(8,128)S(1)} %scalars.1.scalar_ref, bf16[272,1152]{1,0:T(8,128)(2,1)S(1)} %collective-permute-done.1.refs_0_, ...), custom_call_target="tpu_custom_call" | custom-call | tf_op jit(solution)/shard_map/far_near/pallas_call | solution.py:246
  28.6 11.7 %collective-permute-done.refs_0_ = bf16[512,1152]{1,0:T(8,128)(2,1)S(1)} collective-permute-done((bf16[512,1152]{1,0:T(8,128)(2,1)S(1)}, bf16[512,1152]{1,0:T(8,128)(2,1)S(1)}, u32[]{:S(2)}, u32[]{:S(2)}) %collective-permute-start) | collective-permute-done | bytes 1179680 | tf_op jit(solution)/shard_map/ppermute | solution.py:289
  40.3 0.7 collective-permute-start.5
  41.0 1.6 %past_near.1.refs_2_.refs_4_.refs_5_ = f32[256,1152]{1,0:T(8,128)S(1)} custom-call(f32[8,128]{1,0:T(8,128)S(1)} %scalars.1.scalar_ref, bf16[512,1152]{1,0:T(8,128)(2,1)S(1)} %after.2.refs_0_.refs_1_.refs_2_, bf16[272,1152]{1,0:T(8,128)(2,1)S(1)} %get-tuple-element.19.refs_1_, bf16[256,1152]{1,0:T(8,128)(2,1)S(1)} %get-tuple-element.20.refs_2_, ...), custom_call_target="tpu_custom_call" | custom-call | tf_op jit(solution)/shard_map/past_near/pallas_call | solution.py:246
  43.5 1.6 %far_0.1.refs_6_ = bf16[256,1152]{1,0:T(8,128)(2,1)S(1)} custom-call(f32[8,128]{1,0:T(8,128)S(1)} %scalars.1.scalar_ref, bf16[272,1152]{1,0:T(8,128)(2,1)S(1)} %get-tuple-element.23.refs_0_.refs_1_.refs_5_, bf16[512,1152]{1,0:T(8,128)(2,1)S(1)} %after.2.refs_0_.refs_1_.refs_2_, bf16[512,1152]{1,0:T(8,128)(2,1)S(1)} %collective-permute-done.5.refs_2_.refs_3_, ...), custom_call_target="tpu_custom_call" | custom-call | tf_op jit(solution)/shard_map/far_0/pallas_call | solution.py:246
  45.8 2.7 %past_0.1.refs_6_ = bf16[256,1152]{1,0:T(8,128)(2,1)S(1)} custom-call(f32[8,128]{1,0:T(8,128)S(1)} %scalars.1.scalar_ref, bf16[512,1152]{1,0:T(8,128)(2,1)S(1)} %after.2.refs_0_.refs_1_.refs_2_, bf16[272,1152]{1,0:T(8,128)(2,1)S(1)} %get-tuple-element.23.refs_0_.refs_1_.refs_5_, bf16[256,1152]{1,0:T(8,128)(2,1)} %get-tuple-element.24.refs_2_.refs_0_.refs_6_, ...), custom_call_target="tpu_custom_call" | custom-call | tf_op jit(solution)/shard_map/past_0/pallas_call | solution.py:246
  48.5 3.2 %collective-permute-start.11 = (bf16[256,1152]{1,0:T(8,128)(2,1)S(1)}, bf16[256,1152]{1,0:T(8,128)(2,1)S(1)}, u32[]{:S(2)}, u32[]{:S(2)}) collective-permute-start(bf16[256,1152]{1,0:T(8,128)(2,1)S(1)} %past_0.1.refs_6_), channel_id=1, source_target_pairs={{4,0},{5,1},{6,2},{7,3},{8,4},{9,5},{10,6},{11,7},{12,8},{13,9},{1... | collective-permute-start | bytes 1769480 | tf_op jit(solution)/shard_map/ppermute | solution.py:289
  51.7 4.4 %far_1.1.refs_9_ = bf16[256,1152]{1,0:T(8,128)(2,1)S(1)} custom-call(f32[8,128]{1,0:T(8,128)S(1)} %scalars.1.scalar_ref, bf16[256,1152]{1,0:T(8,128)(2,1)} %get-tuple-element.24.refs_2_.refs_0_.refs_6_, bf16[272,1152]{1,0:T(8,128)(2,1)S(1)} %get-tuple-element.23.refs_0_.refs_1_.refs_5_, bf16[512,1152]{1,0:T(8,128)(2,1)S(1)} %after.2.refs_0_.refs_1_.refs_2_, ...), custom_call_target="tpu_custom_call" | custom-call | tf_op jit(solution)/shard_map/far_1/pallas_call | solution.py:246
  56.3 4.7 %past_1.1.refs_11_ = bf16[256,1152]{1,0:T(8,128)(2,1)S(1)} custom-call(f32[8,128]{1,0:T(8,128)S(1)} %scalars.1.scalar_ref, bf16[512,1152]{1,0:T(8,128)(2,1)S(1)} %after.2.refs_0_.refs_1_.refs_2_, bf16[272,1152]{1,0:T(8,128)(2,1)S(1)} %get-tuple-element.23.refs_0_.refs_1_.refs_5_, bf16[256,1152]{1,0:T(8,128)(2,1)} %get-tuple-element.24.refs_2_.refs_0_.refs_6_, ...), custom_call_target="tpu_custom_call" | custom-call | tf_op jit(solution)/shard_map/past_1/pallas_call | solution.py:246
  61.0 2.4 %collective-permute-start.12 = (bf16[256,1152]{1,0:T(8,128)(2,1)S(1)}, bf16[256,1152]{1,0:T(8,128)(2,1)S(1)}, u32[]{:S(2)}, u32[]{:S(2)}) collective-permute-start(bf16[256,1152]{1,0:T(8,128)(2,1)S(1)} %past_1.1.refs_11_), channel_id=1, source_target_pairs={{4,0},{5,1},{6,2},{7,3},{8,4},{9,5},{10,6},{11,7},{12,8},{13,9},{1... | collective-permute-start | bytes 1769480 | tf_op jit(solution)/shard_map/ppermute | solution.py:289
  63.5 7.4 %last.1 = (f32[512,1152]{1,0:T(8,128)S(1)}, f32[512,1152]{1,0:T(8,128)S(1)}) custom-call(f32[8,128]{1,0:T(8,128)S(1)} %scalars.1.scalar_ref, bf16[272,1152]{1,0:T(8,128)(2,1)} %get-tuple-element.15.refs_0_.refs_3_.refs_5_, bf16[256,1152]{1,0:T(8,128)(2,1)} %get-tuple-element.16.refs_1_.refs_4_.refs_6_, bf16[512,1152]{1,0:T(8,128)(2,1)S(1)} %after.2.refs_0_.refs_1_.refs_2_, ...), custom_call_target="tpu_custom_call" | custom-call | tf_op jit(solution)/shard_map/last/pallas_call | solution.py:246
  70.9 1.1 %image_add_0.1.refs_2_ = f32[512,1152]{1,0:T(8,128)} custom-call(f32[512,1152]{1,0:T(8,128)S(1)} %get-tuple-element.26.refs_0_, bf16[256,1152]{1,0:T(8,128)(2,1)S(1)} %collective-permute-done.10.refs_1_), custom_call_target="tpu_custom_call" | custom-call | tf_op jit(solution)/shard_map/image_add_0/pallas_call | solution.py:273
  71.9 1.1 %text_add_0.1.refs_3_.refs_2_ = f32[512,1152]{1,0:T(8,128)} custom-call(f32[512,1152]{1,0:T(8,128)S(1)} %get-tuple-element.27.refs_0_, bf16[256,1152]{1,0:T(8,128)(2,1)S(1)} %collective-permute-done.11.refs_1_, f32[512,1152]{1,0:T(8,128)} %image_add_0.1.refs_2_), custom_call_target="tpu_custom_call" | custom-call | tf_op jit(solution)/shard_map/text_add_0/pallas_call | solution.py:273
  73.0 1.1 %image_add_1.1.refs_3_ = f32[512,1152]{1,0:T(8,128)} custom-call(f32[512,1152]{1,0:T(8,128)S(1)} %get-tuple-element.26.refs_0_, bf16[256,1152]{1,0:T(8,128)(2,1)S(1)} %collective-permute-done.9.refs_1_, f32[512,1152]{1,0:T(8,128)} %image_add_0.1.refs_2_, f32[512,1152]{1,0:T(8,128)} %text_add_0.1.refs_3_.refs_2_), custom_call_target="tpu_custom_call", output_to_operand_aliasing={{}: (2, {})} | custom-call | tf_op jit(solution)/shard_map/image_add_1/pallas_call | solution.py:273
  74.1 2.4 %collective-permute-done.12.refs_1_ = bf16[256,1152]{1,0:T(8,128)(2,1)S(1)} collective-permute-done((bf16[256,1152]{1,0:T(8,128)(2,1)S(1)}, bf16[256,1152]{1,0:T(8,128)(2,1)S(1)}, u32[]{:S(2)}, u32[]{:S(2)}) %collective-permute-start.12) | collective-permute-done | bytes 589856 | tf_op jit(solution)/shard_map/ppermute | solution.py:289
  76.5 1.1 %text_add_1.1 = f32[512,1152]{1,0:T(8,128)} custom-call(f32[512,1152]{1,0:T(8,128)S(1)} %get-tuple-element.27.refs_0_, bf16[256,1152]{1,0:T(8,128)(2,1)S(1)} %collective-permute-done.12.refs_1_, f32[512,1152]{1,0:T(8,128)} %text_add_0.1.refs_3_.refs_2_, f32[512,1152]{1,0:T(8,128)} %image_add_1.1.refs_3_), custom_call_target="tpu_custom_call", output_to_operand_aliasing={{}: (2, {})} | custom-call | tf_op jit(solution)/shard_map/text_add_1/pallas_call | solution.py:273
  (29 shorter events, 3.0 us)
Async XLA Ops:
  2.2 12.1 %collective-permute-start.2 = (bf16[512,1152]{1,0:T(8,128)(2,1)S(1)}, bf16[512,1152]{1,0:T(8,128)(2,1)}, u32[]{:S(2)}, u32[]{:S(2)}) collective-permute-start(bf16[512,1152]{1,0:T(8,128)(2,1)S(1)} %text_norm.1.token.refs_2_.refs_1_.refs_4_), channel_id=1, source_target_pairs={{0,1},{1,0},{2,3},{3,2},{4,5},{5,4},{6,7},{7,6},{8,9},{9,8},{10,11... | collective-permute-start | bytes 3538952 | tf_op jit(solution)/shard_map/ppermute | solution.py:289
  5.6 34.7 %collective-permute-start = (bf16[512,1152]{1,0:T(8,128)(2,1)S(1)}, bf16[512,1152]{1,0:T(8,128)(2,1)S(1)}, u32[]{:S(2)}, u32[]{:S(2)}) collective-permute-start(bf16[512,1152]{1,0:T(8,128)(2,1)S(1)} %text_norm.1.token.refs_2_.refs_1_.refs_4_), channel_id=1, source_target_pairs={{0,4},{1,5},{2,6},{3,7},{4,8},{5,9},{6,10},{7,11},{8,12},{9,13},{1... | collective-permute-start | bytes 3538952 | tf_op jit(solution)/shard_map/ppermute | solution.py:289
  8.0 6.3 %collective-permute-start.3 = (bf16[272,1152]{1,0:T(8,128)(2,1)}, bf16[272,1152]{1,0:T(8,128)(2,1)}, u32[]{:S(2)}, u32[]{:S(2)}) collective-permute-start(bf16[272,1152]{1,0:T(8,128)(2,1)} %get-tuple-element.15.refs_0_.refs_3_.refs_5_), channel_id=1, source_target_pairs={{0,1},{1,0},{2,3},{3,2},{4,5},{5,4},{6,7},{7,6},{8,9},{9,8},{10,11... | collective-permute-start | bytes 1880072 | tf_op jit(solution)/shard_map/ppermute | solution.py:289
  8.2 16.8 %collective-permute-start.1 = (bf16[272,1152]{1,0:T(8,128)(2,1)}, bf16[272,1152]{1,0:T(8,128)(2,1)S(1)}, u32[]{:S(2)}, u32[]{:S(2)}) collective-permute-start(bf16[272,1152]{1,0:T(8,128)(2,1)} %get-tuple-element.15.refs_0_.refs_3_.refs_5_), channel_id=1, source_target_pairs={{0,2},{1,3},{2,0},{3,1},{4,6},{5,7},{6,4},{7,5},{8,10},{9,11},{10,... | collective-permute-start | bytes 1880072 | tf_op jit(solution)/shard_map/ppermute | solution.py:289
  9.3 2.3 %collective-permute-start.4 = (bf16[256,1152]{1,0:T(8,128)(2,1)}, bf16[256,1152]{1,0:T(8,128)(2,1)S(1)}, u32[]{:S(2)}, u32[]{:S(2)}) collective-permute-start(bf16[256,1152]{1,0:T(8,128)(2,1)} %get-tuple-element.16.refs_1_.refs_4_.refs_6_), channel_id=1, source_target_pairs={{0,1},{1,0},{2,3},{3,2},{4,5},{5,4},{6,7},{7,6},{8,9},{9,8},{10,11... | collective-permute-start | bytes 1769480 | tf_op jit(solution)/shard_map/ppermute | solution.py:289
  11.6 0.8 %copy-start.1 = (bf16[256,1152]{1,0:T(8,128)(2,1)}, bf16[256,1152]{1,0:T(8,128)(2,1)S(1)}, u32[]{:S(2)}) copy-start(bf16[256,1152]{1,0:T(8,128)(2,1)S(1)} %collective-permute-done.4.refs_5_.refs_6_.refs_8_) | copy-start | bytes 1769476
  12.4 30.2 %collective-permute-start.6 = (bf16[256,1152]{1,0:T(8,128)(2,1)}, bf16[256,1152]{1,0:T(8,128)(2,1)}, u32[]{:S(2)}, u32[]{:S(2)}) collective-permute-start(bf16[256,1152]{1,0:T(8,128)(2,1)} %get-tuple-element.16.refs_1_.refs_4_.refs_6_), channel_id=1, source_target_pairs={{0,2},{1,3},{2,0},{3,1},{4,6},{5,7},{6,4},{7,5},{8,10},{9,11},{10,... | collective-permute-start | bytes 1769480 | tf_op jit(solution)/shard_map/ppermute | solution.py:289
  14.4 1.1 %copy-start.2 = (bf16[256,1152]{1,0:T(8,128)(2,1)S(1)}, bf16[256,1152]{1,0:T(8,128)(2,1)}, u32[]{:S(2)}) copy-start(bf16[256,1152]{1,0:T(8,128)(2,1)} %copy-done.1) | copy-start | bytes 1769476
  40.3 3.1 %collective-permute-start.5 = (bf16[512,1152]{1,0:T(8,128)(2,1)S(1)}, bf16[512,1152]{1,0:T(8,128)(2,1)S(1)}, u32[]{:S(2)}, u32[]{:S(2)}) collective-permute-start(bf16[512,1152]{1,0:T(8,128)(2,1)S(1)} %after.2.refs_0_.refs_1_.refs_2_), channel_id=1, source_target_pairs={{0,1},{1,0},{2,3},{3,2},{4,5},{5,4},{6,7},{7,6},{8,9},{9,8},{10,11... | collective-permute-start | bytes 3538952 | tf_op jit(solution)/shard_map/ppermute | solution.py:289
  42.6 3.2 %collective-permute-start.7 = (bf16[272,1152]{1,0:T(8,128)(2,1)S(1)}, bf16[272,1152]{1,0:T(8,128)(2,1)S(1)}, u32[]{:S(2)}, u32[]{:S(2)}) collective-permute-start(bf16[272,1152]{1,0:T(8,128)(2,1)S(1)} %get-tuple-element.23.refs_0_.refs_1_.refs_5_), channel_id=1, source_target_pairs={{0,1},{1,0},{2,3},{3,2},{4,5},{5,4},{6,7},{7,6},{8,9},{9,8},{10,11... | collective-permute-start | bytes 1880072 | tf_op jit(solution)/shard_map/ppermute | solution.py:289
  42.7 3.1 %collective-permute-start.8 = (bf16[256,1152]{1,0:T(8,128)(2,1)}, bf16[256,1152]{1,0:T(8,128)(2,1)S(1)}, u32[]{:S(2)}, u32[]{:S(2)}) collective-permute-start(bf16[256,1152]{1,0:T(8,128)(2,1)} %get-tuple-element.24.refs_2_.refs_0_.refs_6_), channel_id=1, source_target_pairs={{0,1},{1,0},{2,3},{3,2},{4,5},{5,4},{6,7},{7,6},{8,9},{9,8},{10,11... | collective-permute-start | bytes 1769480 | tf_op jit(solution)/shard_map/ppermute | solution.py:289
  45.1 25.8 %collective-permute-start.10 = (bf16[256,1152]{1,0:T(8,128)(2,1)S(1)}, bf16[256,1152]{1,0:T(8,128)(2,1)S(1)}, u32[]{:S(2)}, u32[]{:S(2)}) collective-permute-start(bf16[256,1152]{1,0:T(8,128)(2,1)S(1)} %far_0.1.refs_6_), channel_id=1, source_target_pairs={{0,2},{1,3},{2,0},{3,1},{4,6},{5,7},{6,4},{7,5},{8,10},{9,11},{10,... | collective-permute-start | bytes 1769480 | tf_op jit(solution)/shard_map/ppermute | solution.py:289
  48.5 7.7 %copy-start.3 = (bf16[256,1152]{1,0:T(8,128)(2,1)S(1)}, bf16[256,1152]{1,0:T(8,128)(2,1)}, u32[]{:S(2)}) copy-start(bf16[256,1152]{1,0:T(8,128)(2,1)} %copy-done.1) | copy-start | bytes 1769476
  48.5 23.4 %collective-permute-start.11 = (bf16[256,1152]{1,0:T(8,128)(2,1)S(1)}, bf16[256,1152]{1,0:T(8,128)(2,1)S(1)}, u32[]{:S(2)}, u32[]{:S(2)}) collective-permute-start(bf16[256,1152]{1,0:T(8,128)(2,1)S(1)} %past_0.1.refs_6_), channel_id=1, source_target_pairs={{4,0},{5,1},{6,2},{7,3},{8,4},{9,5},{10,6},{11,7},{12,8},{13,9},{1... | collective-permute-start | bytes 1769480 | tf_op jit(solution)/shard_map/ppermute | solution.py:289
  56.1 16.9 %collective-permute-start.9 = (bf16[256,1152]{1,0:T(8,128)(2,1)S(1)}, bf16[256,1152]{1,0:T(8,128)(2,1)S(1)}, u32[]{:S(2)}, u32[]{:S(2)}) collective-permute-start(bf16[256,1152]{1,0:T(8,128)(2,1)S(1)} %far_1.1.refs_9_), channel_id=1, source_target_pairs={{0,2},{1,3},{2,0},{3,1},{4,6},{5,7},{6,4},{7,5},{8,10},{9,11},{10,... | collective-permute-start | bytes 1769480 | tf_op jit(solution)/shard_map/ppermute | solution.py:289
  56.2 7.2 %copy-start = (f32[512,1152]{1,0:T(8,128)S(1)}, f32[512,1152]{1,0:T(8,128)}, u32[]{:S(2)}) copy-start(f32[512,1152]{1,0:T(8,128)} %get-tuple-element.17.refs_7_.refs_9_) | copy-start | bytes 7077892
  56.3 7.2 %copy-start.4 = (f32[512,1152]{1,0:T(8,128)S(1)}, f32[512,1152]{1,0:T(8,128)}, u32[]{:S(2)}) copy-start(f32[512,1152]{1,0:T(8,128)} %get-tuple-element.25.refs_10_) | copy-start | bytes 7077892
  61.0 15.5 %collective-permute-start.12 = (bf16[256,1152]{1,0:T(8,128)(2,1)S(1)}, bf16[256,1152]{1,0:T(8,128)(2,1)S(1)}, u32[]{:S(2)}, u32[]{:S(2)}) collective-permute-start(bf16[256,1152]{1,0:T(8,128)(2,1)S(1)} %past_1.1.refs_11_), channel_id=1, source_target_pairs={{4,0},{5,1},{6,2},{7,3},{8,4},{9,5},{10,6},{11,7},{12,8},{13,9},{1... | collective-permute-start | bytes 1769480 | tf_op jit(solution)/shard_map/ppermute | solution.py:289

commit v4 on v3

--- a/solution.py
+++ b/solution.py
@@ -66,7 +66,7 @@
     return copies
 
 
-def image_norm_body(pos_ref, a_ref, token, image_0, image_1, held, pos_held, sems, pos_sem):
+def image_norm_body(pos_ref, a_ref, token, image_0, image_1, again, held, pos_held, sems, pos_sem):
     pos_copy = pltpu.make_async_copy(pos_ref, pos_held, pos_sem)
     pos_copy.start()
     copies = fetch(a_ref, held, sems)
@@ -81,7 +81,10 @@
     for at, out in zip(range(0, ROWS, FR), (image_0, image_1)):
         for k in range(at // PIECE, (at + FR) // PIECE):
             copies[k].wait()
-        out[pl.ds(0, FR)] = unit_rows(held[pl.ds(at, FR)])
+        values = unit_rows(held[pl.ds(at, FR)])
+        out[pl.ds(0, FR)] = values
+        if at:
+            again[...] = values
 
 
 def hbm(x):
@@ -135,9 +138,9 @@
 def image_norm(pos, a, earlier):
     return pl.pallas_call(
         image_norm_body,
-        out_shape=[block(FR + EXTRA), block(FR)],
+        out_shape=[block(FR + EXTRA), block(FR), pltpu.HBM((FR, D), jnp.bfloat16)],
         in_specs=[HBM, HBM, ANY],
-        out_specs=[VMEM, VMEM],
+        out_specs=[VMEM] * 3,
         scratch_shapes=[
             block(ROWS),
             pltpu.VMEM((1, ROWS), jnp.int32),
@@ -299,16 +302,20 @@
 
     text = text_norm(caption_vectors)
     past, text_mate = move(text, ahead), move(text, core)
-    image = list(image_norm(pos, picture_vectors, text))
-    far, image_mate = [move(b, chip) for b in image], [move(b, core) for b in image]
+    *image, again = image_norm(pos, picture_vectors, text)
+    far, image_mate = [move(image[0], chip)], [move(b, core) for b in image]
 
     images, texts = image_parts(*image), text_parts(text, 0)
     images_near, texts_near = images + image_parts(*image_mate), texts + text_parts(text_mate, 1)
-    image_sum, text_sum = run(
-        [image_job(images, texts_near, None, f32), text_job(texts, images_near, None, f32)], [], "near", True
-    )
+    (image_sum,) = run([image_job(images, texts_near, None, f32)], [], "near_image", True)
+    (again,) = after([again], [hbm(image_sum)])
+    far.append(move(again, chip))
+    (text_sum,) = run([text_job(texts, images_near, None, f32)], [again], "near_text", True)
     far_sum, *copies = run(
-        [image_job(image_parts(*far)[:1], texts_near, None, f32)], [hbm(image_sum)], "far_near", keep=image + image_mate
+        [image_job(image_parts(*far)[:1], texts_near, None, f32)],
+        [hbm(text_sum)],
+        "far_near",
+        keep=image + image_mate,
     )
     (past,) = after([past], [far_sum])
     past_mate = move(past, core)

time: 78.1 us -> 76.8 us (0.983)
  local copies, waits for them, and re-layouts: 1.89 us -> 0.01 us
  Pallas kernels: 44 us -> 45.5 us
  waiting for transfers between devices: 16.8 us -> 15.7 us
    unnamed x10 -> x6, local copies, waits for them, and re-layouts: 1.89 us -> 0.01 us
    pallas_call x8 -> x9, Pallas kernels: 35.6 us -> 36.9 us  [gram(): pl.pallas_call(functools.partial(gram_body, n=len(arrays), n_given=len(gi...]
    ppermute x13, waiting for transfers between devices: 16.8 us -> 15.7 us  [shards(): move = lambda block, route: lax.ppermute(block, AXES, route)]
  transfers between devices with their start and end apart: 13 -> 13, of which waited for: 5 -> 5; matrix products, arithmetic and copies ran while one was open for 0% -> 0% of each run, Pallas kernels for 53% -> 56%
where the time goes in v4:
time: 76.8 us; the launch traced here: 76.5 us
  Pallas kernels  45.5 us (59%)
  waiting for transfers between devices  15.7 us (20%)
  starting transfers between devices  13.1 us (17%)
  between operations  2.28 us (3%)
    pallas_call x9, Pallas kernels, gram(): pl.pallas_call(functools.partial(gram_body, n=len(arrays), n_given=len(gi...  36.9 us
    ppermute x13, waiting for transfers between devices, shards(): move = lambda block, route: lax.ppermute(block, AXES, route)  15.7 us
    ppermute x13, starting transfers between devices, shards(): move = lambda block, route: lax.ppermute(block, AXES, route)  13.1 us
    pallas_call x4, Pallas kernels, add(): pl.pallas_call(functools.partial(add_body, start=start), out_shape=jax.Sh...  4.29 us
    pallas_call x1, Pallas kernels, image_norm(): pl.pallas_call(image_norm_body, out_shape=[block(FR + EXTRA), block(FR),...  2.64 us
    pallas_call x1, Pallas kernels, text_norm(): pl.pallas_call(text_norm_body, out_shape=block(ROWS), in_specs=[HBM], out...  1.61 us
  transfers between devices with their start and end apart: 13, of which 5 were waited for; matrix products, arithmetic and copies ran while one was open for 0% of the time, Pallas kernels for 56%

profile of v4, /device:TPU:1, one launch (start us, length us, event | category | flops | bytes accessed | tf_op | source)
XLA Modules:
  0.0 76.5 jit_solution(5739470381368381168)
XLA Ops:
  0.6 1.6 %text_norm.1.token.refs_2_.refs_0_.refs_1_.refs_4_ = bf16[512,1152]{1,0:T(8,128)(2,1)S(1)} custom-call(bf16[512,1152]{1,0:T(8,128)(2,1)} %t_ref.1), custom_call_target="tpu_custom_call" | custom-call | tf_op jit(solution)/shard_map/text_norm/pallas_call | solution.py:156
  2.2 3.3 %collective-permute-start.2 = (bf16[512,1152]{1,0:T(8,128)(2,1)S(1)}, bf16[512,1152]{1,0:T(8,128)(2,1)}, u32[]{:S(2)}, u32[]{:S(2)}) collective-permute-start(bf16[512,1152]{1,0:T(8,128)(2,1)S(1)} %text_norm.1.token.refs_2_.refs_0_.refs_1_.refs_4_), channel_id=1, source_target_pairs={{0,1},{1,0},{2,3},{3,2},{4,5},{5,4},{6,7},{7,6},{8,9},{9,8},{10,11... | collective-permute-start | bytes 3538952 | tf_op jit(solution)/shard_map/ppermute | solution.py:292
  5.6 2.6 %image_norm.1 = (bf16[272,1152]{1,0:T(8,128)(2,1)}, bf16[256,1152]{1,0:T(8,128)(2,1)}, bf16[256,1152]{1,0:T(8,128)(2,1)}) custom-call(s32[1,512]{1,0:T(1,128)} %bitcast.5, bf16[512,1152]{1,0:T(8,128)(2,1)} %a_ref.1, bf16[512,1152]{1,0:T(8,128)(2,1)S(1)} %text_norm.1.token.refs_2_.refs_0_.refs_1_.refs_4_), custom_call_target="tpu_custom_call" | custom-call | tf_op jit(solution)/shard_map/image_norm/pallas_call | solution.py:139
  8.4 1.0 %collective-permute-start.1 = (bf16[272,1152]{1,0:T(8,128)(2,1)}, bf16[272,1152]{1,0:T(8,128)(2,1)S(1)}, u32[]{:S(2)}, u32[]{:S(2)}) collective-permute-start(bf16[272,1152]{1,0:T(8,128)(2,1)} %get-tuple-element.14.refs_0_.refs_1_.refs_3_.refs_5_), channel_id=1, source_target_pairs={{0,2},{1,3},{2,0},{3,1},{4,6},{5,7},{6,4},{7,5},{8,10},{9,11},{10,... | collective-permute-start | bytes 1880072 | tf_op jit(solution)/shard_map/ppermute | solution.py:292
  11.2 6.1 %near_image.1.refs_1_.refs_9_ = f32[512,1152]{1,0:T(8,128)} custom-call(f32[8,128]{1,0:T(8,128)S(1)} %scalars.1.scalar_ref, bf16[272,1152]{1,0:T(8,128)(2,1)} %get-tuple-element.14.refs_0_.refs_1_.refs_3_.refs_5_, bf16[256,1152]{1,0:T(8,128)(2,1)} %get-tuple-element.15.refs_1_.refs_2_.refs_4_.refs_6_, ...), custom_call_target="tpu_custom_call" | custom-call | tf_op jit(solution)/shard_map/near_image/pallas_call | solution.py:249
  17.4 0.7 collective-permute-start.6
  18.0 6.0 %near_text.1.refs_7_.refs_10_ = f32[512,1152]{1,0:T(8,128)} custom-call(f32[8,128]{1,0:T(8,128)S(1)} %scalars.1.scalar_ref, bf16[512,1152]{1,0:T(8,128)(2,1)S(1)} %text_norm.1.token.refs_2_.refs_0_.refs_1_.refs_4_, bf16[272,1152]{1,0:T(8,128)(2,1)} %get-tuple-element.14.refs_0_.refs_1_.refs_3_.refs_5_, ...), custom_call_target="tpu_custom_call" | custom-call | tf_op jit(solution)/shard_map/near_text/pallas_call | solution.py:249
  24.0 3.7 %far_near.1 = (f32[256,1152]{1,0:T(8,128)S(1)}, bf16[272,1152]{1,0:T(8,128)(2,1)S(1)}, bf16[256,1152]{1,0:T(8,128)(2,1)S(1)}, bf16[272,1152]{1,0:T(8,128)(2,1)S(1)}, bf16[256,1152]{1,0:T(8,128)(2,1)S(1)}) custom-call(f32[8,128]{1,0:T(8,128)S(1)} %scalars.1.scalar_ref, bf16[272,1152]{1,0:T(8,128)(2,1)S(1)} %collective-permute-done.1.refs_0_, ...), custom_call_target="tpu_custom_call" | custom-call | tf_op jit(solution)/shard_map/far_near/pallas_call | solution.py:249
  27.8 12.5 %collective-permute-done.refs_0_ = bf16[512,1152]{1,0:T(8,128)(2,1)S(1)} collective-permute-done((bf16[512,1152]{1,0:T(8,128)(2,1)S(1)}, bf16[512,1152]{1,0:T(8,128)(2,1)S(1)}, u32[]{:S(2)}, u32[]{:S(2)}) %collective-permute-start) | collective-permute-done | bytes 1179680 | tf_op jit(solution)/shard_map/ppermute | solution.py:292
  40.3 0.7 collective-permute-start.5
  41.0 1.6 %past_near.1.refs_2_.refs_4_.refs_5_ = f32[256,1152]{1,0:T(8,128)S(1)} custom-call(f32[8,128]{1,0:T(8,128)S(1)} %scalars.1.scalar_ref, bf16[512,1152]{1,0:T(8,128)(2,1)S(1)} %after.4.refs_0_.refs_1_.refs_2_, bf16[272,1152]{1,0:T(8,128)(2,1)S(1)} %get-tuple-element.18.refs_1_, bf16[256,1152]{1,0:T(8,128)(2,1)S(1)} %get-tuple-element.19.refs_2_, ...), custom_call_target="tpu_custom_call" | custom-call | tf_op jit(solution)/shard_map/past_near/pallas_call | solution.py:249
  43.5 1.6 %far_0.1.refs_6_ = bf16[256,1152]{1,0:T(8,128)(2,1)S(1)} custom-call(f32[8,128]{1,0:T(8,128)S(1)} %scalars.1.scalar_ref, bf16[272,1152]{1,0:T(8,128)(2,1)S(1)} %get-tuple-element.22.refs_0_.refs_1_.refs_5_, bf16[512,1152]{1,0:T(8,128)(2,1)S(1)} %after.4.refs_0_.refs_1_.refs_2_, bf16[512,1152]{1,0:T(8,128)(2,1)S(1)} %collective-permute-done.5.refs_2_.refs_3_, ...), custom_call_target="tpu_custom_call" | custom-call | tf_op jit(solution)/shard_map/far_0/pallas_call | solution.py:249
  45.6 1.6 %past_0.1.refs_6_ = bf16[256,1152]{1,0:T(8,128)(2,1)S(1)} custom-call(f32[8,128]{1,0:T(8,128)S(1)} %scalars.1.scalar_ref, bf16[512,1152]{1,0:T(8,128)(2,1)S(1)} %after.4.refs_0_.refs_1_.refs_2_, bf16[272,1152]{1,0:T(8,128)(2,1)S(1)} %get-tuple-element.22.refs_0_.refs_1_.refs_5_, bf16[256,1152]{1,0:T(8,128)(2,1)S(1)} %get-tuple-element.23.refs_2_.refs_0_.refs_6_, ...), custom_call_target="tpu_custom_call" | custom-call | tf_op jit(solution)/shard_map/past_0/pallas_call | solution.py:249
  47.3 3.3 %collective-permute-start.11 = (bf16[256,1152]{1,0:T(8,128)(2,1)S(1)}, bf16[256,1152]{1,0:T(8,128)(2,1)S(1)}, u32[]{:S(2)}, u32[]{:S(2)}) collective-permute-start(bf16[256,1152]{1,0:T(8,128)(2,1)S(1)} %past_0.1.refs_6_), channel_id=1, source_target_pairs={{4,0},{5,1},{6,2},{7,3},{8,4},{9,5},{10,6},{11,7},{12,8},{13,9},{1... | collective-permute-start | bytes 1769480 | tf_op jit(solution)/shard_map/ppermute | solution.py:292
  50.5 4.3 %far_1.1.refs_9_ = bf16[256,1152]{1,0:T(8,128)(2,1)S(1)} custom-call(f32[8,128]{1,0:T(8,128)S(1)} %scalars.1.scalar_ref, bf16[256,1152]{1,0:T(8,128)(2,1)S(1)} %get-tuple-element.23.refs_2_.refs_0_.refs_6_, bf16[272,1152]{1,0:T(8,128)(2,1)S(1)} %get-tuple-element.22.refs_0_.refs_1_.refs_5_, bf16[512,1152]{1,0:T(8,128)(2,1)S(1)} %after.4.refs_0_.refs_1_.refs_2_, ...), custom_call_target="tpu_custom_call" | custom-call | tf_op jit(solution)/shard_map/far_1/pallas_call | solution.py:249
  54.9 4.7 %past_1.1.refs_11_ = bf16[256,1152]{1,0:T(8,128)(2,1)S(1)} custom-call(f32[8,128]{1,0:T(8,128)S(1)} %scalars.1.scalar_ref, bf16[512,1152]{1,0:T(8,128)(2,1)S(1)} %after.4.refs_0_.refs_1_.refs_2_, bf16[272,1152]{1,0:T(8,128)(2,1)S(1)} %get-tuple-element.22.refs_0_.refs_1_.refs_5_, bf16[256,1152]{1,0:T(8,128)(2,1)S(1)} %get-tuple-element.23.refs_2_.refs_0_.refs_6_, ...), custom_call_target="tpu_custom_call" | custom-call | tf_op jit(solution)/shard_map/past_1/pallas_call | solution.py:249
  59.7 2.6 %collective-permute-start.12 = (bf16[256,1152]{1,0:T(8,128)(2,1)S(1)}, bf16[256,1152]{1,0:T(8,128)(2,1)S(1)}, u32[]{:S(2)}, u32[]{:S(2)}) collective-permute-start(bf16[256,1152]{1,0:T(8,128)(2,1)S(1)} %past_1.1.refs_11_), channel_id=1, source_target_pairs={{4,0},{5,1},{6,2},{7,3},{8,4},{9,5},{10,6},{11,7},{12,8},{13,9},{1... | collective-permute-start | bytes 1769480 | tf_op jit(solution)/shard_map/ppermute | solution.py:292
  62.3 7.2 %last.1 = (f32[512,1152]{1,0:T(8,128)S(1)}, f32[512,1152]{1,0:T(8,128)S(1)}) custom-call(f32[8,128]{1,0:T(8,128)S(1)} %scalars.1.scalar_ref, bf16[272,1152]{1,0:T(8,128)(2,1)} %get-tuple-element.14.refs_0_.refs_1_.refs_3_.refs_5_, bf16[256,1152]{1,0:T(8,128)(2,1)} %get-tuple-element.15.refs_1_.refs_2_.refs_4_.refs_6_, ...), custom_call_target="tpu_custom_call" | custom-call | tf_op jit(solution)/shard_map/last/pallas_call | solution.py:249
  69.5 1.1 %image_add_0.1.refs_2_ = f32[512,1152]{1,0:T(8,128)} custom-call(f32[512,1152]{1,0:T(8,128)S(1)} %get-tuple-element.24.refs_0_, bf16[256,1152]{1,0:T(8,128)(2,1)S(1)} %collective-permute-done.10.refs_1_), custom_call_target="tpu_custom_call" | custom-call | tf_op jit(solution)/shard_map/image_add_0/pallas_call | solution.py:276
  70.6 1.1 %text_add_0.1.refs_3_.refs_2_ = f32[512,1152]{1,0:T(8,128)} custom-call(f32[512,1152]{1,0:T(8,128)S(1)} %get-tuple-element.25.refs_0_, bf16[256,1152]{1,0:T(8,128)(2,1)S(1)} %collective-permute-done.11.refs_1_, f32[512,1152]{1,0:T(8,128)} %image_add_0.1.refs_2_), custom_call_target="tpu_custom_call" | custom-call | tf_op jit(solution)/shard_map/text_add_0/pallas_call | solution.py:276
  71.7 0.6 collective-permute-done.9.refs_1_
  72.3 1.1 %image_add_1.1.refs_3_ = f32[512,1152]{1,0:T(8,128)} custom-call(f32[512,1152]{1,0:T(8,128)S(1)} %get-tuple-element.24.refs_0_, bf16[256,1152]{1,0:T(8,128)(2,1)S(1)} %collective-permute-done.9.refs_1_, f32[512,1152]{1,0:T(8,128)} %image_add_0.1.refs_2_, f32[512,1152]{1,0:T(8,128)} %text_add_0.1.refs_3_.refs_2_), custom_call_target="tpu_custom_call", output_to_operand_aliasing={{}: (2, {})} | custom-call | tf_op jit(solution)/shard_map/image_add_1/pallas_call | solution.py:276
  73.4 1.9 %collective-permute-done.12.refs_1_ = bf16[256,1152]{1,0:T(8,128)(2,1)S(1)} collective-permute-done((bf16[256,1152]{1,0:T(8,128)(2,1)S(1)}, bf16[256,1152]{1,0:T(8,128)(2,1)S(1)}, u32[]{:S(2)}, u32[]{:S(2)}) %collective-permute-start.12) | collective-permute-done | bytes 589856 | tf_op jit(solution)/shard_map/ppermute | solution.py:292
  75.3 1.1 %text_add_1.1 = f32[512,1152]{1,0:T(8,128)} custom-call(f32[512,1152]{1,0:T(8,128)S(1)} %get-tuple-element.25.refs_0_, bf16[256,1152]{1,0:T(8,128)(2,1)S(1)} %collective-permute-done.12.refs_1_, f32[512,1152]{1,0:T(8,128)} %text_add_0.1.refs_3_.refs_2_, f32[512,1152]{1,0:T(8,128)} %image_add_1.1.refs_3_), custom_call_target="tpu_custom_call", output_to_operand_aliasing={{}: (2, {})} | custom-call | tf_op jit(solution)/shard_map/text_add_1/pallas_call | solution.py:276
  (27 shorter events, 2.2 us)
Async XLA Ops:
  2.2 9.0 %collective-permute-start.2 = (bf16[512,1152]{1,0:T(8,128)(2,1)S(1)}, bf16[512,1152]{1,0:T(8,128)(2,1)}, u32[]{:S(2)}, u32[]{:S(2)}) collective-permute-start(bf16[512,1152]{1,0:T(8,128)(2,1)S(1)} %text_norm.1.token.refs_2_.refs_0_.refs_1_.refs_4_), channel_id=1, source_target_pairs={{0,1},{1,0},{2,3},{3,2},{4,5},{5,4},{6,7},{7,6},{8,9},{9,8},{10,11... | collective-permute-start | bytes 3538952 | tf_op jit(solution)/shard_map/ppermute | solution.py:292
  5.6 34.7 %collective-permute-start = (bf16[512,1152]{1,0:T(8,128)(2,1)S(1)}, bf16[512,1152]{1,0:T(8,128)(2,1)S(1)}, u32[]{:S(2)}, u32[]{:S(2)}) collective-permute-start(bf16[512,1152]{1,0:T(8,128)(2,1)S(1)} %text_norm.1.token.refs_2_.refs_0_.refs_1_.refs_4_), channel_id=1, source_target_pairs={{0,4},{1,5},{2,6},{3,7},{4,8},{5,9},{6,10},{7,11},{8,12},{9,13},{1... | collective-permute-start | bytes 3538952 | tf_op jit(solution)/shard_map/ppermute | solution.py:292
  8.2 9.8 %collective-permute-start.3 = (bf16[272,1152]{1,0:T(8,128)(2,1)}, bf16[272,1152]{1,0:T(8,128)(2,1)}, u32[]{:S(2)}, u32[]{:S(2)}) collective-permute-start(bf16[272,1152]{1,0:T(8,128)(2,1)} %get-tuple-element.14.refs_0_.refs_1_.refs_3_.refs_5_), channel_id=1, source_target_pairs={{0,1},{1,0},{2,3},{3,2},{4,5},{5,4},{6,7},{7,6},{8,9},{9,8},{10,11... | collective-permute-start | bytes 1880072 | tf_op jit(solution)/shard_map/ppermute | solution.py:292
  8.4 15.6 %collective-permute-start.1 = (bf16[272,1152]{1,0:T(8,128)(2,1)}, bf16[272,1152]{1,0:T(8,128)(2,1)S(1)}, u32[]{:S(2)}, u32[]{:S(2)}) collective-permute-start(bf16[272,1152]{1,0:T(8,128)(2,1)} %get-tuple-element.14.refs_0_.refs_1_.refs_3_.refs_5_), channel_id=1, source_target_pairs={{0,2},{1,3},{2,0},{3,1},{4,6},{5,7},{6,4},{7,5},{8,10},{9,11},{10,... | collective-permute-start | bytes 1880072 | tf_op jit(solution)/shard_map/ppermute | solution.py:292
  9.5 8.6 %collective-permute-start.4 = (bf16[256,1152]{1,0:T(8,128)(2,1)}, bf16[256,1152]{1,0:T(8,128)(2,1)}, u32[]{:S(2)}, u32[]{:S(2)}) collective-permute-start(bf16[256,1152]{1,0:T(8,128)(2,1)} %get-tuple-element.15.refs_1_.refs_2_.refs_4_.refs_6_), channel_id=1, source_target_pairs={{0,1},{1,0},{2,3},{3,2},{4,5},{5,4},{6,7},{7,6},{8,9},{9,8},{10,11... | collective-permute-start | bytes 1769480 | tf_op jit(solution)/shard_map/ppermute | solution.py:292
  11.2 6.1 %copy-start.2 = (bf16[256,1152]{1,0:T(8,128)(2,1)S(1)}, bf16[256,1152]{1,0:T(8,128)(2,1)}, u32[]{:S(2)}) copy-start(bf16[256,1152]{1,0:T(8,128)(2,1)} %get-tuple-element.16.refs_0_) | copy-start | bytes 1769476
  17.4 25.3 %collective-permute-start.6 = (bf16[256,1152]{1,0:T(8,128)(2,1)S(1)}, bf16[256,1152]{1,0:T(8,128)(2,1)S(1)}, u32[]{:S(2)}, u32[]{:S(2)}) collective-permute-start(bf16[256,1152]{1,0:T(8,128)(2,1)S(1)} %after.3.refs_5_), channel_id=1, source_target_pairs={{0,2},{1,3},{2,0},{3,1},{4,6},{5,7},{6,4},{7,5},{8,10},{9,11},{10,... | collective-permute-start | bytes 1769480 | tf_op jit(solution)/shard_map/ppermute | solution.py:292
  40.3 3.1 %collective-permute-start.5 = (bf16[512,1152]{1,0:T(8,128)(2,1)S(1)}, bf16[512,1152]{1,0:T(8,128)(2,1)S(1)}, u32[]{:S(2)}, u32[]{:S(2)}) collective-permute-start(bf16[512,1152]{1,0:T(8,128)(2,1)S(1)} %after.4.refs_0_.refs_1_.refs_2_), channel_id=1, source_target_pairs={{0,1},{1,0},{2,3},{3,2},{4,5},{5,4},{6,7},{7,6},{8,9},{9,8},{10,11... | collective-permute-start | bytes 3538952 | tf_op jit(solution)/shard_map/ppermute | solution.py:292
  42.6 3.0 %collective-permute-start.7 = (bf16[272,1152]{1,0:T(8,128)(2,1)S(1)}, bf16[272,1152]{1,0:T(8,128)(2,1)S(1)}, u32[]{:S(2)}, u32[]{:S(2)}) collective-permute-start(bf16[272,1152]{1,0:T(8,128)(2,1)S(1)} %get-tuple-element.22.refs_0_.refs_1_.refs_5_), channel_id=1, source_target_pairs={{0,1},{1,0},{2,3},{3,2},{4,5},{5,4},{6,7},{7,6},{8,9},{9,8},{10,11... | collective-permute-start | bytes 1880072 | tf_op jit(solution)/shard_map/ppermute | solution.py:292
  42.7 2.9 %collective-permute-start.8 = (bf16[256,1152]{1,0:T(8,128)(2,1)S(1)}, bf16[256,1152]{1,0:T(8,128)(2,1)S(1)}, u32[]{:S(2)}, u32[]{:S(2)}) collective-permute-start(bf16[256,1152]{1,0:T(8,128)(2,1)S(1)} %get-tuple-element.23.refs_2_.refs_0_.refs_6_), channel_id=1, source_target_pairs={{0,1},{1,0},{2,3},{3,2},{4,5},{5,4},{6,7},{7,6},{8,9},{9,8},{10,11... | collective-permute-start | bytes 1769480 | tf_op jit(solution)/shard_map/ppermute | solution.py:292
  45.1 24.5 %collective-permute-start.10 = (bf16[256,1152]{1,0:T(8,128)(2,1)S(1)}, bf16[256,1152]{1,0:T(8,128)(2,1)S(1)}, u32[]{:S(2)}, u32[]{:S(2)}) collective-permute-start(bf16[256,1152]{1,0:T(8,128)(2,1)S(1)} %far_0.1.refs_6_), channel_id=1, source_target_pairs={{0,2},{1,3},{2,0},{3,1},{4,6},{5,7},{6,4},{7,5},{8,10},{9,11},{10,... | collective-permute-start | bytes 1769480 | tf_op jit(solution)/shard_map/ppermute | solution.py:292
  47.3 23.4 %collective-permute-start.11 = (bf16[256,1152]{1,0:T(8,128)(2,1)S(1)}, bf16[256,1152]{1,0:T(8,128)(2,1)S(1)}, u32[]{:S(2)}, u32[]{:S(2)}) collective-permute-start(bf16[256,1152]{1,0:T(8,128)(2,1)S(1)} %past_0.1.refs_6_), channel_id=1, source_target_pairs={{4,0},{5,1},{6,2},{7,3},{8,4},{9,5},{10,6},{11,7},{12,8},{13,9},{1... | collective-permute-start | bytes 1769480 | tf_op jit(solution)/shard_map/ppermute | solution.py:292
  54.8 17.6 %collective-permute-start.9 = (bf16[256,1152]{1,0:T(8,128)(2,1)S(1)}, bf16[256,1152]{1,0:T(8,128)(2,1)S(1)}, u32[]{:S(2)}, u32[]{:S(2)}) collective-permute-start(bf16[256,1152]{1,0:T(8,128)(2,1)S(1)} %far_1.1.refs_9_), channel_id=1, source_target_pairs={{0,2},{1,3},{2,0},{3,1},{4,6},{5,7},{6,4},{7,5},{8,10},{9,11},{10,... | collective-permute-start | bytes 1769480 | tf_op jit(solution)/shard_map/ppermute | solution.py:292
  54.9 7.4 %copy-start = (f32[512,1152]{1,0:T(8,128)S(1)}, f32[512,1152]{1,0:T(8,128)}, u32[]{:S(2)}) copy-start(f32[512,1152]{1,0:T(8,128)} %near_image.1.refs_1_.refs_9_) | copy-start | bytes 7077892
  54.9 7.4 %copy-start.1 = (f32[512,1152]{1,0:T(8,128)S(1)}, f32[512,1152]{1,0:T(8,128)}, u32[]{:S(2)}) copy-start(f32[512,1152]{1,0:T(8,128)} %near_text.1.refs_7_.refs_10_) | copy-start | bytes 7077892
  59.7 15.6 %collective-permute-start.12 = (bf16[256,1152]{1,0:T(8,128)(2,1)S(1)}, bf16[256,1152]{1,0:T(8,128)(2,1)S(1)}, u32[]{:S(2)}, u32[]{:S(2)}) collective-permute-start(bf16[256,1152]{1,0:T(8,128)(2,1)S(1)} %past_1.1.refs_11_), channel_id=1, source_target_pairs={{4,0},{5,1},{6,2},{7,3},{8,4},{9,5},{10,6},{11,7},{12,8},{13,9},{1... | collective-permute-start | bytes 1769480 | tf_op jit(solution)/shard_map/ppermute | solution.py:292

commit v5 on v4

--- a/solution.py
+++ b/solution.py
@@ -208,14 +208,18 @@
     total = scale * total
     if given is not None:
         total = total + given[0][pl.ds(given[1], len(xs) * FR)]
-    out[...] = total.astype(out.dtype)
-
-
-def gram_body(scalar_ref, *refs, n, n_given, jobs, kept):
+    rows = total.shape[0] // len(out)
+    for k, ref in enumerate(out):
+        ref[...] = total[k * rows : (k + 1) * rows].astype(ref.dtype)
+
+
+def gram_body(scalar_ref, *refs, n, n_given, jobs, kept, halves):
     arrays = refs[:n]
     scalar = [scalar_ref[0:1, k : k + 1] for k in range(6)]
     given = list(refs[n : n + n_given])
-    outs, extras, weights = refs[-1 - len(jobs) - len(kept) : -1 - len(kept)], refs[-1 - len(kept) : -1], refs[-1]
+    n_outs = halves * len(jobs)
+    outs, extras, weights = refs[-1 - n_outs - len(kept) : -1 - len(kept)], refs[-1 - len(kept) : -1], refs[-1]
+    outs = [outs[k : k + halves] for k in range(0, n_outs, halves)]
     for k, extra in zip(kept, extras):
         extra[...] = arrays[k][...]
     for out, (xs, ys, with_sum, x_is_image) in zip(outs, jobs):
@@ -223,7 +227,7 @@
         gram_rows(scalar, arrays, xs, ys, before, out, weights, x_is_image)
 
 
-def gram(scalars, jobs, earlier, name, far=False, keep=()):
+def gram(scalars, jobs, earlier, name, far=False, keep=(), halves=1):
     arrays, given, plans, outs = [], [], [], []
 
     def number(array):
@@ -240,14 +244,14 @@
 
     for xs, ys, before, dtype, x_is_image in jobs:
         plans.append(([place(p) for p in xs], [place(p) for p in ys], before and before[1:], x_is_image))
-        outs.append((pltpu.HBM if far else pltpu.VMEM)((len(xs) * FR, D), dtype))
+        outs += [(pltpu.HBM if far else pltpu.VMEM)((len(xs) * FR // halves, D), dtype)] * halves
         if before is not None:
             given.append(before[0])
     kept = [number(a) for a in keep]
     rows = max(len(p[0]) for p in plans) * FR
     columns = max(len(p[1]) for p in plans) * FR
     return pl.pallas_call(
-        functools.partial(gram_body, n=len(arrays), n_given=len(given), jobs=plans, kept=kept),
+        functools.partial(gram_body, n=len(arrays), n_given=len(given), jobs=plans, kept=kept, halves=halves),
         out_shape=outs + [block(a.shape[0]) for a in keep],
         in_specs=[VMEM] * (1 + len(arrays) + len(given)) + [ANY] * len(earlier),
         out_specs=[VMEM] * (len(outs) + len(keep)),
@@ -261,7 +265,7 @@
 def add_body(*refs, start):
     total, got, out, held, sems = *refs[:2], *refs[-3:]
     copies = []
-    for k in range(FR // PIECE):
+    for k in range(got.shape[0] // PIECE):
         rows = pl.ds(k * PIECE, PIECE)
         at = pl.ds(start + k * PIECE, PIECE)
         held[rows] = total[at] + got[rows].astype(jnp.float32)
@@ -279,7 +283,7 @@
         in_specs=[VMEM, VMEM] + [HBM] * (len(given) + len(earlier)),
         out_specs=HBM,
         input_output_aliases={2: 0} if given else {},
-        scratch_shapes=[pltpu.VMEM((FR, D), jnp.float32), pltpu.SemaphoreType.DMA((FR // PIECE,))],
+        scratch_shapes=[pltpu.VMEM(got.shape, jnp.float32), pltpu.SemaphoreType.DMA((got.shape[0] // PIECE,))],
         name=name,
         **params(16),
     )(total, got, *[hbm(x) for x in given + earlier])
@@ -337,10 +341,10 @@
         [image_job(images_far[1:], texts_there + texts_near, None, bf16)], [past_terms_0], "far_1"
     )
     far_back_1 = move(far_terms_1, chip)
-    (past_terms_1,) = run(
-        [text_job(texts_past[1:], images_there + images_near, None, bf16)], [far_terms_1], "past_1"
-    )
-    past_back_1 = move(past_terms_1, behind)
+    past_terms_1, past_terms_2 = run(
+        [text_job(texts_past[1:], images_there + images_near, None, bf16)], [far_terms_1], "past_1", halves=2
+    )
+    past_back_1, past_back_2 = move(past_terms_1, behind), move(past_terms_2, behind)
     image_sum, text_sum = run(
         [
             image_job(images, texts_there, (image_sum, 0), f32),
@@ -353,6 +357,7 @@
     out_t = add(text_sum, past_back_0, None, 0, [out_a], "text_add_0")
     out_a = add(image_sum, far_back_1, out_a, FR, [out_t], "image_add_1")
     out_t = add(text_sum, past_back_1, out_t, FR, [out_a], "text_add_1")
+    out_t = add(text_sum, past_back_2, out_t, FR + FR // 2, [], "text_add_2")
     return (out_a, out_t)
 
 

time: 76.8 us -> 76.7 us (level)
  waiting for transfers between devices: 15.7 us -> 14.1 us
    ppermute x13 -> x14, waiting for transfers between devices: 15.7 us -> 14.1 us  [shards(): move = lambda block, route: lax.ppermute(block, AXES, route)]
    ppermute x13 -> x14, starting transfers between devices: 13.1 us -> 13.8 us  [shards(): move = lambda block, route: lax.ppermute(block, AXES, route)]
    pallas_call x4 -> x5, Pallas kernels: 4.29 us -> 4.94 us  [add(): pl.pallas_call(functools.partial(add_body, start=start), out_shape=jax.Sh...]
  transfers between devices with their start and end apart: 13 -> 14, of which waited for: 5 -> 4; matrix products, arithmetic and copies ran while one was open for 0% -> 0% of each run, Pallas kernels for 56% -> 57%
where the time goes in v5:
time: 76.7 us; the launch traced here: 76.4 us
  Pallas kernels  46.2 us (60%)
  waiting for transfers between devices  14.1 us (18%)
  starting transfers between devices  13.8 us (18%)
  between operations  2.32 us (3%)
    pallas_call x9, Pallas kernels, gram(): pl.pallas_call(functools.partial(gram_body, n=len(arrays), n_given=len(gi...  36.9 us
    ppermute x14, waiting for transfers between devices, shards(): move = lambda block, route: lax.ppermute(block, AXES, route)  14.1 us
    ppermute x14, starting transfers between devices, shards(): move = lambda block, route: lax.ppermute(block, AXES, route)  13.8 us
    pallas_call x5, Pallas kernels, add(): pl.pallas_call(functools.partial(add_body, start=start), out_shape=jax.Sh...  4.94 us
    pallas_call x1, Pallas kernels, image_norm(): pl.pallas_call(image_norm_body, out_shape=[block(FR + EXTRA), block(FR),...  2.64 us
    pallas_call x1, Pallas kernels, text_norm(): pl.pallas_call(text_norm_body, out_shape=block(ROWS), in_specs=[HBM], out...  1.61 us
  transfers between devices with their start and end apart: 14, of which 4 were waited for; matrix products, arithmetic and copies ran while one was open for 0% of the time, Pallas kernels for 57%

profile of v5, /device:TPU:1, one launch (start us, length us, event | category | flops | bytes accessed | tf_op | source)
XLA Modules:
  0.0 76.4 jit_solution(1621707011597579271)
XLA Ops:
  0.6 1.6 %text_norm.1.token.refs_2_.refs_0_.refs_1_.refs_4_ = bf16[512,1152]{1,0:T(8,128)(2,1)S(1)} custom-call(bf16[512,1152]{1,0:T(8,128)(2,1)} %t_ref.1), custom_call_target="tpu_custom_call" | custom-call | tf_op jit(solution)/shard_map/text_norm/pallas_call | solution.py:156
  2.2 3.3 %collective-permute-start.2 = (bf16[512,1152]{1,0:T(8,128)(2,1)S(1)}, bf16[512,1152]{1,0:T(8,128)(2,1)}, u32[]{:S(2)}, u32[]{:S(2)}) collective-permute-start(bf16[512,1152]{1,0:T(8,128)(2,1)S(1)} %text_norm.1.token.refs_2_.refs_0_.refs_1_.refs_4_), channel_id=1, source_target_pairs={{0,1},{1,0},{2,3},{3,2},{4,5},{5,4},{6,7},{7,6},{8,9},{9,8},{10,11... | collective-permute-start | bytes 3538952 | tf_op jit(solution)/shard_map/ppermute | solution.py:296
  5.6 2.6 %image_norm.1 = (bf16[272,1152]{1,0:T(8,128)(2,1)}, bf16[256,1152]{1,0:T(8,128)(2,1)}, bf16[256,1152]{1,0:T(8,128)(2,1)}) custom-call(s32[1,512]{1,0:T(1,128)} %bitcast.5, bf16[512,1152]{1,0:T(8,128)(2,1)} %a_ref.1, bf16[512,1152]{1,0:T(8,128)(2,1)S(1)} %text_norm.1.token.refs_2_.refs_0_.refs_1_.refs_4_), custom_call_target="tpu_custom_call" | custom-call | tf_op jit(solution)/shard_map/image_norm/pallas_call | solution.py:139
  8.4 1.0 %collective-permute-start.1 = (bf16[272,1152]{1,0:T(8,128)(2,1)}, bf16[272,1152]{1,0:T(8,128)(2,1)S(1)}, u32[]{:S(2)}, u32[]{:S(2)}) collective-permute-start(bf16[272,1152]{1,0:T(8,128)(2,1)} %get-tuple-element.16.refs_0_.refs_1_.refs_3_.refs_5_), channel_id=1, source_target_pairs={{0,2},{1,3},{2,0},{3,1},{4,6},{5,7},{6,4},{7,5},{8,10},{9,11},{10,... | collective-permute-start | bytes 1880072 | tf_op jit(solution)/shard_map/ppermute | solution.py:296
  11.2 6.1 %near_image.1.refs_1_.refs_9_ = f32[512,1152]{1,0:T(8,128)} custom-call(f32[8,128]{1,0:T(8,128)S(1)} %scalars.1.scalar_ref, bf16[272,1152]{1,0:T(8,128)(2,1)} %get-tuple-element.16.refs_0_.refs_1_.refs_3_.refs_5_, bf16[256,1152]{1,0:T(8,128)(2,1)} %get-tuple-element.17.refs_1_.refs_2_.refs_4_.refs_6_, ...), custom_call_target="tpu_custom_call" | custom-call | tf_op jit(solution)/shard_map/near_image/pallas_call | solution.py:253
  17.4 0.7 collective-permute-start.6
  18.0 6.0 %near_text.1.refs_7_.refs_10_ = f32[512,1152]{1,0:T(8,128)} custom-call(f32[8,128]{1,0:T(8,128)S(1)} %scalars.1.scalar_ref, bf16[512,1152]{1,0:T(8,128)(2,1)S(1)} %text_norm.1.token.refs_2_.refs_0_.refs_1_.refs_4_, bf16[272,1152]{1,0:T(8,128)(2,1)} %get-tuple-element.16.refs_0_.refs_1_.refs_3_.refs_5_, ...), custom_call_target="tpu_custom_call" | custom-call | tf_op jit(solution)/shard_map/near_text/pallas_call | solution.py:253
  24.0 3.7 %far_near.1 = (f32[256,1152]{1,0:T(8,128)S(1)}, bf16[272,1152]{1,0:T(8,128)(2,1)S(1)}, bf16[256,1152]{1,0:T(8,128)(2,1)S(1)}, bf16[272,1152]{1,0:T(8,128)(2,1)S(1)}, bf16[256,1152]{1,0:T(8,128)(2,1)S(1)}) custom-call(f32[8,128]{1,0:T(8,128)S(1)} %scalars.1.scalar_ref, bf16[272,1152]{1,0:T(8,128)(2,1)S(1)} %collective-permute-done.1.refs_0_, ...), custom_call_target="tpu_custom_call" | custom-call | tf_op jit(solution)/shard_map/far_near/pallas_call | solution.py:253
  27.8 12.5 %collective-permute-done.refs_0_ = bf16[512,1152]{1,0:T(8,128)(2,1)S(1)} collective-permute-done((bf16[512,1152]{1,0:T(8,128)(2,1)S(1)}, bf16[512,1152]{1,0:T(8,128)(2,1)S(1)}, u32[]{:S(2)}, u32[]{:S(2)}) %collective-permute-start) | collective-permute-done | bytes 1179680 | tf_op jit(solution)/shard_map/ppermute | solution.py:296
  40.3 0.7 collective-permute-start.5
  41.0 1.6 %past_near.1.refs_2_.refs_4_.refs_5_ = f32[256,1152]{1,0:T(8,128)S(1)} custom-call(f32[8,128]{1,0:T(8,128)S(1)} %scalars.1.scalar_ref, bf16[512,1152]{1,0:T(8,128)(2,1)S(1)} %after.4.refs_0_.refs_1_.refs_2_, bf16[272,1152]{1,0:T(8,128)(2,1)S(1)} %get-tuple-element.20.refs_1_, bf16[256,1152]{1,0:T(8,128)(2,1)S(1)} %get-tuple-element.21.refs_2_, ...), custom_call_target="tpu_custom_call" | custom-call | tf_op jit(solution)/shard_map/past_near/pallas_call | solution.py:253
  43.5 1.6 %far_0.1.refs_6_ = bf16[256,1152]{1,0:T(8,128)(2,1)S(1)} custom-call(f32[8,128]{1,0:T(8,128)S(1)} %scalars.1.scalar_ref, bf16[272,1152]{1,0:T(8,128)(2,1)S(1)} %get-tuple-element.24.refs_0_.refs_1_.refs_5_, bf16[512,1152]{1,0:T(8,128)(2,1)S(1)} %after.4.refs_0_.refs_1_.refs_2_, bf16[512,1152]{1,0:T(8,128)(2,1)S(1)} %collective-permute-done.5.refs_2_.refs_3_, ...), custom_call_target="tpu_custom_call" | custom-call | tf_op jit(solution)/shard_map/far_0/pallas_call | solution.py:253
  45.6 1.6 %past_0.1.refs_6_ = bf16[256,1152]{1,0:T(8,128)(2,1)S(1)} custom-call(f32[8,128]{1,0:T(8,128)S(1)} %scalars.1.scalar_ref, bf16[512,1152]{1,0:T(8,128)(2,1)S(1)} %after.4.refs_0_.refs_1_.refs_2_, bf16[272,1152]{1,0:T(8,128)(2,1)S(1)} %get-tuple-element.24.refs_0_.refs_1_.refs_5_, bf16[256,1152]{1,0:T(8,128)(2,1)S(1)} %get-tuple-element.25.refs_2_.refs_0_.refs_6_, ...), custom_call_target="tpu_custom_call" | custom-call | tf_op jit(solution)/shard_map/past_0/pallas_call | solution.py:253
  47.3 3.3 %collective-permute-start.11 = (bf16[256,1152]{1,0:T(8,128)(2,1)S(1)}, bf16[256,1152]{1,0:T(8,128)(2,1)S(1)}, u32[]{:S(2)}, u32[]{:S(2)}) collective-permute-start(bf16[256,1152]{1,0:T(8,128)(2,1)S(1)} %past_0.1.refs_6_), channel_id=1, source_target_pairs={{4,0},{5,1},{6,2},{7,3},{8,4},{9,5},{10,6},{11,7},{12,8},{13,9},{1... | collective-permute-start | bytes 1769480 | tf_op jit(solution)/shard_map/ppermute | solution.py:296
  50.5 4.3 %far_1.1.refs_9_ = bf16[256,1152]{1,0:T(8,128)(2,1)S(1)} custom-call(f32[8,128]{1,0:T(8,128)S(1)} %scalars.1.scalar_ref, bf16[256,1152]{1,0:T(8,128)(2,1)S(1)} %get-tuple-element.25.refs_2_.refs_0_.refs_6_, bf16[272,1152]{1,0:T(8,128)(2,1)S(1)} %get-tuple-element.24.refs_0_.refs_1_.refs_5_, bf16[512,1152]{1,0:T(8,128)(2,1)S(1)} %after.4.refs_0_.refs_1_.refs_2_, ...), custom_call_target="tpu_custom_call" | custom-call | tf_op jit(solution)/shard_map/far_1/pallas_call | solution.py:253
  54.9 4.7 %past_1.1 = (bf16[128,1152]{1,0:T(8,128)(2,1)S(1)}, bf16[128,1152]{1,0:T(8,128)(2,1)S(1)}) custom-call(f32[8,128]{1,0:T(8,128)S(1)} %scalars.1.scalar_ref, bf16[512,1152]{1,0:T(8,128)(2,1)S(1)} %after.4.refs_0_.refs_1_.refs_2_, bf16[272,1152]{1,0:T(8,128)(2,1)S(1)} %get-tuple-element.24.refs_0_.refs_1_.refs_5_, ...), custom_call_target="tpu_custom_call" | custom-call | tf_op jit(solution)/shard_map/past_1/pallas_call | solution.py:253
  59.7 2.8 %collective-permute-start.13 = (bf16[128,1152]{1,0:T(8,128)(2,1)S(1)}, bf16[128,1152]{1,0:T(8,128)(2,1)S(1)}, u32[]{:S(2)}, u32[]{:S(2)}) collective-permute-start(bf16[128,1152]{1,0:T(8,128)(2,1)S(1)} %get-tuple-element.26.refs_11_), channel_id=1, source_target_pairs={{4,0},{5,1},{6,2},{7,3},{8,4},{9,5},{10,6},{11,7},{12,8},{13,9},{1... | collective-permute-start | bytes 884744 | tf_op jit(solution)/shard_map/ppermute | solution.py:296
  63.1 7.2 %last.1 = (f32[512,1152]{1,0:T(8,128)S(1)}, f32[512,1152]{1,0:T(8,128)S(1)}) custom-call(f32[8,128]{1,0:T(8,128)S(1)} %scalars.1.scalar_ref, bf16[272,1152]{1,0:T(8,128)(2,1)} %get-tuple-element.16.refs_0_.refs_1_.refs_3_.refs_5_, bf16[256,1152]{1,0:T(8,128)(2,1)} %get-tuple-element.17.refs_1_.refs_2_.refs_4_.refs_6_, ...), custom_call_target="tpu_custom_call" | custom-call | tf_op jit(solution)/shard_map/last/pallas_call | solution.py:253
  70.4 1.1 %image_add_0.1.refs_2_ = f32[512,1152]{1,0:T(8,128)} custom-call(f32[512,1152]{1,0:T(8,128)S(1)} %get-tuple-element.27.refs_0_, bf16[256,1152]{1,0:T(8,128)(2,1)S(1)} %collective-permute-done.10.refs_1_), custom_call_target="tpu_custom_call" | custom-call | tf_op jit(solution)/shard_map/image_add_0/pallas_call | solution.py:280
  71.4 1.1 %text_add_0.1.refs_3_.refs_2_ = f32[512,1152]{1,0:T(8,128)} custom-call(f32[512,1152]{1,0:T(8,128)S(1)} %get-tuple-element.28.refs_0_, bf16[256,1152]{1,0:T(8,128)(2,1)S(1)} %collective-permute-done.11.refs_1_, f32[512,1152]{1,0:T(8,128)} %image_add_0.1.refs_2_), custom_call_target="tpu_custom_call" | custom-call | tf_op jit(solution)/shard_map/text_add_0/pallas_call | solution.py:280
  72.5 1.1 %image_add_1.1.refs_3_ = f32[512,1152]{1,0:T(8,128)} custom-call(f32[512,1152]{1,0:T(8,128)S(1)} %get-tuple-element.27.refs_0_, bf16[256,1152]{1,0:T(8,128)(2,1)S(1)} %collective-permute-done.9.refs_1_, f32[512,1152]{1,0:T(8,128)} %image_add_0.1.refs_2_, f32[512,1152]{1,0:T(8,128)} %text_add_0.1.refs_3_.refs_2_), custom_call_target="tpu_custom_call", output_to_operand_aliasing={{}: (2, {})} | custom-call | tf_op jit(solution)/shard_map/image_add_1/pallas_call | solution.py:280
  73.6 0.9 %text_add_1.1.refs_2_ = f32[512,1152]{1,0:T(8,128)} custom-call(f32[512,1152]{1,0:T(8,128)S(1)} %get-tuple-element.28.refs_0_, bf16[128,1152]{1,0:T(8,128)(2,1)S(1)} %collective-permute-done.13.refs_1_, f32[512,1152]{1,0:T(8,128)} %text_add_0.1.refs_3_.refs_2_, f32[512,1152]{1,0:T(8,128)} %image_add_1.1.refs_3_), custom_call_target="tpu_custom_call", output_to_operand_aliasing={{}: (2, {})} | custom-call | tf_op jit(solution)/shard_map/text_add_1/pallas_call | solution.py:280
  74.5 0.9 %collective-permute-done.12.refs_1_ = bf16[128,1152]{1,0:T(8,128)(2,1)S(1)} collective-permute-done((bf16[128,1152]{1,0:T(8,128)(2,1)S(1)}, bf16[128,1152]{1,0:T(8,128)(2,1)S(1)}, u32[]{:S(2)}, u32[]{:S(2)}) %collective-permute-start.12) | collective-permute-done | bytes 294944 | tf_op jit(solution)/shard_map/ppermute | solution.py:296
  75.4 0.9 %text_add_2.1 = f32[512,1152]{1,0:T(8,128)} custom-call(f32[512,1152]{1,0:T(8,128)S(1)} %get-tuple-element.28.refs_0_, bf16[128,1152]{1,0:T(8,128)(2,1)S(1)} %collective-permute-done.12.refs_1_, f32[512,1152]{1,0:T(8,128)} %text_add_1.1.refs_2_), custom_call_target="tpu_custom_call", output_to_operand_aliasing={{}: (2, {})} | custom-call | tf_op jit(solution)/shard_map/text_add_2/pallas_call | solution.py:280
  (30 shorter events, 2.8 us)
Async XLA Ops:
  2.2 9.0 %collective-permute-start.2 = (bf16[512,1152]{1,0:T(8,128)(2,1)S(1)}, bf16[512,1152]{1,0:T(8,128)(2,1)}, u32[]{:S(2)}, u32[]{:S(2)}) collective-permute-start(bf16[512,1152]{1,0:T(8,128)(2,1)S(1)} %text_norm.1.token.refs_2_.refs_0_.refs_1_.refs_4_), channel_id=1, source_target_pairs={{0,1},{1,0},{2,3},{3,2},{4,5},{5,4},{6,7},{7,6},{8,9},{9,8},{10,11... | collective-permute-start | bytes 3538952 | tf_op jit(solution)/shard_map/ppermute | solution.py:296
  5.6 34.7 %collective-permute-start = (bf16[512,1152]{1,0:T(8,128)(2,1)S(1)}, bf16[512,1152]{1,0:T(8,128)(2,1)S(1)}, u32[]{:S(2)}, u32[]{:S(2)}) collective-permute-start(bf16[512,1152]{1,0:T(8,128)(2,1)S(1)} %text_norm.1.token.refs_2_.refs_0_.refs_1_.refs_4_), channel_id=1, source_target_pairs={{0,4},{1,5},{2,6},{3,7},{4,8},{5,9},{6,10},{7,11},{8,12},{9,13},{1... | collective-permute-start | bytes 3538952 | tf_op jit(solution)/shard_map/ppermute | solution.py:296
  8.2 9.8 %collective-permute-start.3 = (bf16[272,1152]{1,0:T(8,128)(2,1)}, bf16[272,1152]{1,0:T(8,128)(2,1)}, u32[]{:S(2)}, u32[]{:S(2)}) collective-permute-start(bf16[272,1152]{1,0:T(8,128)(2,1)} %get-tuple-element.16.refs_0_.refs_1_.refs_3_.refs_5_), channel_id=1, source_target_pairs={{0,1},{1,0},{2,3},{3,2},{4,5},{5,4},{6,7},{7,6},{8,9},{9,8},{10,11... | collective-permute-start | bytes 1880072 | tf_op jit(solution)/shard_map/ppermute | solution.py:296
  8.4 15.6 %collective-permute-start.1 = (bf16[272,1152]{1,0:T(8,128)(2,1)}, bf16[272,1152]{1,0:T(8,128)(2,1)S(1)}, u32[]{:S(2)}, u32[]{:S(2)}) collective-permute-start(bf16[272,1152]{1,0:T(8,128)(2,1)} %get-tuple-element.16.refs_0_.refs_1_.refs_3_.refs_5_), channel_id=1, source_target_pairs={{0,2},{1,3},{2,0},{3,1},{4,6},{5,7},{6,4},{7,5},{8,10},{9,11},{10,... | collective-permute-start | bytes 1880072 | tf_op jit(solution)/shard_map/ppermute | solution.py:296
  9.5 8.6 %collective-permute-start.4 = (bf16[256,1152]{1,0:T(8,128)(2,1)}, bf16[256,1152]{1,0:T(8,128)(2,1)}, u32[]{:S(2)}, u32[]{:S(2)}) collective-permute-start(bf16[256,1152]{1,0:T(8,128)(2,1)} %get-tuple-element.17.refs_1_.refs_2_.refs_4_.refs_6_), channel_id=1, source_target_pairs={{0,1},{1,0},{2,3},{3,2},{4,5},{5,4},{6,7},{7,6},{8,9},{9,8},{10,11... | collective-permute-start | bytes 1769480 | tf_op jit(solution)/shard_map/ppermute | solution.py:296
  11.2 6.1 %copy-start.2 = (bf16[256,1152]{1,0:T(8,128)(2,1)S(1)}, bf16[256,1152]{1,0:T(8,128)(2,1)}, u32[]{:S(2)}) copy-start(bf16[256,1152]{1,0:T(8,128)(2,1)} %get-tuple-element.18.refs_0_) | copy-start | bytes 1769476
  17.4 25.3 %collective-permute-start.6 = (bf16[256,1152]{1,0:T(8,128)(2,1)S(1)}, bf16[256,1152]{1,0:T(8,128)(2,1)S(1)}, u32[]{:S(2)}, u32[]{:S(2)}) collective-permute-start(bf16[256,1152]{1,0:T(8,128)(2,1)S(1)} %after.3.refs_5_), channel_id=1, source_target_pairs={{0,2},{1,3},{2,0},{3,1},{4,6},{5,7},{6,4},{7,5},{8,10},{9,11},{10,... | collective-permute-start | bytes 1769480 | tf_op jit(solution)/shard_map/ppermute | solution.py:296
  40.3 3.1 %collective-permute-start.5 = (bf16[512,1152]{1,0:T(8,128)(2,1)S(1)}, bf16[512,1152]{1,0:T(8,128)(2,1)S(1)}, u32[]{:S(2)}, u32[]{:S(2)}) collective-permute-start(bf16[512,1152]{1,0:T(8,128)(2,1)S(1)} %after.4.refs_0_.refs_1_.refs_2_), channel_id=1, source_target_pairs={{0,1},{1,0},{2,3},{3,2},{4,5},{5,4},{6,7},{7,6},{8,9},{9,8},{10,11... | collective-permute-start | bytes 3538952 | tf_op jit(solution)/shard_map/ppermute | solution.py:296
  42.6 3.0 %collective-permute-start.7 = (bf16[272,1152]{1,0:T(8,128)(2,1)S(1)}, bf16[272,1152]{1,0:T(8,128)(2,1)S(1)}, u32[]{:S(2)}, u32[]{:S(2)}) collective-permute-start(bf16[272,1152]{1,0:T(8,128)(2,1)S(1)} %get-tuple-element.24.refs_0_.refs_1_.refs_5_), channel_id=1, source_target_pairs={{0,1},{1,0},{2,3},{3,2},{4,5},{5,4},{6,7},{7,6},{8,9},{9,8},{10,11... | collective-permute-start | bytes 1880072 | tf_op jit(solution)/shard_map/ppermute | solution.py:296
  42.7 2.9 %collective-permute-start.8 = (bf16[256,1152]{1,0:T(8,128)(2,1)S(1)}, bf16[256,1152]{1,0:T(8,128)(2,1)S(1)}, u32[]{:S(2)}, u32[]{:S(2)}) collective-permute-start(bf16[256,1152]{1,0:T(8,128)(2,1)S(1)} %get-tuple-element.25.refs_2_.refs_0_.refs_6_), channel_id=1, source_target_pairs={{0,1},{1,0},{2,3},{3,2},{4,5},{5,4},{6,7},{7,6},{8,9},{9,8},{10,11... | collective-permute-start | bytes 1769480 | tf_op jit(solution)/shard_map/ppermute | solution.py:296
  45.1 25.3 %collective-permute-start.10 = (bf16[256,1152]{1,0:T(8,128)(2,1)S(1)}, bf16[256,1152]{1,0:T(8,128)(2,1)S(1)}, u32[]{:S(2)}, u32[]{:S(2)}) collective-permute-start(bf16[256,1152]{1,0:T(8,128)(2,1)S(1)} %far_0.1.refs_6_), channel_id=1, source_target_pairs={{0,2},{1,3},{2,0},{3,1},{4,6},{5,7},{6,4},{7,5},{8,10},{9,11},{10,... | collective-permute-start | bytes 1769480 | tf_op jit(solution)/shard_map/ppermute | solution.py:296
  47.3 24.2 %collective-permute-start.11 = (bf16[256,1152]{1,0:T(8,128)(2,1)S(1)}, bf16[256,1152]{1,0:T(8,128)(2,1)S(1)}, u32[]{:S(2)}, u32[]{:S(2)}) collective-permute-start(bf16[256,1152]{1,0:T(8,128)(2,1)S(1)} %past_0.1.refs_6_), channel_id=1, source_target_pairs={{4,0},{5,1},{6,2},{7,3},{8,4},{9,5},{10,6},{11,7},{12,8},{13,9},{1... | collective-permute-start | bytes 1769480 | tf_op jit(solution)/shard_map/ppermute | solution.py:296
  54.8 8.3 %copy-start = (f32[512,1152]{1,0:T(8,128)S(1)}, f32[512,1152]{1,0:T(8,128)}, u32[]{:S(2)}) copy-start(f32[512,1152]{1,0:T(8,128)} %near_image.1.refs_1_.refs_9_) | copy-start | bytes 7077892
  54.8 8.3 %copy-start.1 = (f32[512,1152]{1,0:T(8,128)S(1)}, f32[512,1152]{1,0:T(8,128)}, u32[]{:S(2)}) copy-start(f32[512,1152]{1,0:T(8,128)} %near_text.1.refs_7_.refs_10_) | copy-start | bytes 7077892
  54.8 17.7 %collective-permute-start.9 = (bf16[256,1152]{1,0:T(8,128)(2,1)S(1)}, bf16[256,1152]{1,0:T(8,128)(2,1)S(1)}, u32[]{:S(2)}, u32[]{:S(2)}) collective-permute-start(bf16[256,1152]{1,0:T(8,128)(2,1)S(1)} %far_1.1.refs_9_), channel_id=1, source_target_pairs={{0,2},{1,3},{2,0},{3,1},{4,6},{5,7},{6,4},{7,5},{8,10},{9,11},{10,... | collective-permute-start | bytes 1769480 | tf_op jit(solution)/shard_map/ppermute | solution.py:296
  59.7 13.9 %collective-permute-start.13 = (bf16[128,1152]{1,0:T(8,128)(2,1)S(1)}, bf16[128,1152]{1,0:T(8,128)(2,1)S(1)}, u32[]{:S(2)}, u32[]{:S(2)}) collective-permute-start(bf16[128,1152]{1,0:T(8,128)(2,1)S(1)} %get-tuple-element.26.refs_11_), channel_id=1, source_target_pairs={{4,0},{5,1},{6,2},{7,3},{8,4},{9,5},{10,6},{11,7},{12,8},{13,9},{1... | collective-permute-start | bytes 884744 | tf_op jit(solution)/shard_map/ppermute | solution.py:296
  62.5 12.9 %collective-permute-start.12 = (bf16[128,1152]{1,0:T(8,128)(2,1)S(1)}, bf16[128,1152]{1,0:T(8,128)(2,1)S(1)}, u32[]{:S(2)}, u32[]{:S(2)}) collective-permute-start(bf16[128,1152]{1,0:T(8,128)(2,1)S(1)} %get-tuple-element.29), channel_id=1, source_target_pairs={{4,0},{5,1},{6,2},{7,3},{8,4},{9,5},{10,6},{11,7},{12,8},{13,9},{1... | collective-permute-start | bytes 884744 | tf_op jit(solution)/shard_map/ppermute | solution.py:296

commit v6 on v4

--- a/solution.py
+++ b/solution.py
@@ -321,12 +321,12 @@
     past_mate = move(past, core)
     texts_past = text_parts(past, 2)
     texts_there = texts_past + text_parts(past_mate, 3)
-    (past_sum,) = run(
-        [text_job(texts_past[:1], image_parts(*copies[:2]) + image_parts(*copies[2:]), None, f32)], [], "past_near"
-    )
-    far = after(far, [past_sum])
+    far = after(far, [past])
     images_far = image_parts(*far)
     images_there = images_far + image_parts(*[move(b, core) for b in far])
+    (past_sum,) = run(
+        [text_job(texts_past[:1], image_parts(*copies[:2]) + image_parts(*copies[2:]), None, f32)], far[:1], "past_near"
+    )
     (far_terms_0,) = run([image_job(images_far[:1], texts_there, (far_sum, 0), bf16)], [past_sum], "far_0")
     far_back_0 = move(far_terms_0, chip)
     (past_terms_0,) = run(

time: 76.8 us -> 77.8 us (1.013)
  starting transfers between devices: 13.1 us -> 15.1 us
  waiting for transfers between devices: 15.7 us -> 14.6 us
    ppermute x13, starting transfers between devices: 13.1 us -> 15.1 us  [shards(): move = lambda block, route: lax.ppermute(block, AXES, route)]
    ppermute x13, waiting for transfers between devices: 15.7 us -> 14.6 us  [shards(): move = lambda block, route: lax.ppermute(block, AXES, route)]
  transfers between devices with their start and end apart: 13 -> 13, of which waited for: 5 -> 3; matrix products, arithmetic and copies ran while one was open for 0% -> 0% of each run, Pallas kernels for 56% -> 55%
where the time goes in v6:
time: 77.8 us; the launch traced here: 77.5 us
  Pallas kernels  45.5 us (58%)
  starting transfers between devices  15.1 us (19%)
  waiting for transfers between devices  14.6 us (19%)
  between operations  2.27 us (3%)
    pallas_call x9, Pallas kernels, gram(): pl.pallas_call(functools.partial(gram_body, n=len(arrays), n_given=len(gi...  36.9 us
    ppermute x13, starting transfers between devices, shards(): move = lambda block, route: lax.ppermute(block, AXES, route)  15.1 us
    ppermute x13, waiting for transfers between devices, shards(): move = lambda block, route: lax.ppermute(block, AXES, route)  14.6 us
    pallas_call x4, Pallas kernels, add(): pl.pallas_call(functools.partial(add_body, start=start), out_shape=jax.Sh...  4.31 us
    pallas_call x1, Pallas kernels, image_norm(): pl.pallas_call(image_norm_body, out_shape=[block(FR + EXTRA), block(FR),...  2.64 us
    pallas_call x1, Pallas kernels, text_norm(): pl.pallas_call(text_norm_body, out_shape=block(ROWS), in_specs=[HBM], out...  1.61 us
  transfers between devices with their start and end apart: 13, of which 3 were waited for; matrix products, arithmetic and copies ran while one was open for 0% of the time, Pallas kernels for 55%

profile of v6, /device:TPU:1, one launch (start us, length us, event | category | flops | bytes accessed | tf_op | source)
XLA Modules:
  0.0 77.5 jit_solution(1056013440619995512)
XLA Ops:
  0.6 1.6 %text_norm.1.token.refs_2_.refs_0_.refs_1_.refs_4_ = bf16[512,1152]{1,0:T(8,128)(2,1)S(1)} custom-call(bf16[512,1152]{1,0:T(8,128)(2,1)} %t_ref.1), custom_call_target="tpu_custom_call" | custom-call | tf_op jit(solution)/shard_map/text_norm/pallas_call | solution.py:156
  2.2 3.3 %collective-permute-start.2 = (bf16[512,1152]{1,0:T(8,128)(2,1)S(1)}, bf16[512,1152]{1,0:T(8,128)(2,1)}, u32[]{:S(2)}, u32[]{:S(2)}) collective-permute-start(bf16[512,1152]{1,0:T(8,128)(2,1)S(1)} %text_norm.1.token.refs_2_.refs_0_.refs_1_.refs_4_), channel_id=1, source_target_pairs={{0,1},{1,0},{2,3},{3,2},{4,5},{5,4},{6,7},{7,6},{8,9},{9,8},{10,11... | collective-permute-start | bytes 3538952 | tf_op jit(solution)/shard_map/ppermute | solution.py:292
  5.6 2.6 %image_norm.1 = (bf16[272,1152]{1,0:T(8,128)(2,1)}, bf16[256,1152]{1,0:T(8,128)(2,1)}, bf16[256,1152]{1,0:T(8,128)(2,1)}) custom-call(s32[1,512]{1,0:T(1,128)} %bitcast.5, bf16[512,1152]{1,0:T(8,128)(2,1)} %a_ref.1, bf16[512,1152]{1,0:T(8,128)(2,1)S(1)} %text_norm.1.token.refs_2_.refs_0_.refs_1_.refs_4_), custom_call_target="tpu_custom_call" | custom-call | tf_op jit(solution)/shard_map/image_norm/pallas_call | solution.py:139
  8.4 1.0 %collective-permute-start.1 = (bf16[272,1152]{1,0:T(8,128)(2,1)}, bf16[272,1152]{1,0:T(8,128)(2,1)S(1)}, u32[]{:S(2)}, u32[]{:S(2)}) collective-permute-start(bf16[272,1152]{1,0:T(8,128)(2,1)} %get-tuple-element.14.refs_0_.refs_1_.refs_3_.refs_5_), channel_id=1, source_target_pairs={{0,2},{1,3},{2,0},{3,1},{4,6},{5,7},{6,4},{7,5},{8,10},{9,11},{10,... | collective-permute-start | bytes 1880072 | tf_op jit(solution)/shard_map/ppermute | solution.py:292
  11.2 6.1 %near_image.1.refs_1_.refs_9_ = f32[512,1152]{1,0:T(8,128)} custom-call(f32[8,128]{1,0:T(8,128)S(1)} %scalars.1.scalar_ref, bf16[272,1152]{1,0:T(8,128)(2,1)} %get-tuple-element.14.refs_0_.refs_1_.refs_3_.refs_5_, bf16[256,1152]{1,0:T(8,128)(2,1)} %get-tuple-element.15.refs_1_.refs_2_.refs_4_.refs_6_, ...), custom_call_target="tpu_custom_call" | custom-call | tf_op jit(solution)/shard_map/near_image/pallas_call | solution.py:249
  17.4 0.7 collective-permute-start.6
  18.0 6.0 %near_text.1.refs_7_.refs_10_ = f32[512,1152]{1,0:T(8,128)} custom-call(f32[8,128]{1,0:T(8,128)S(1)} %scalars.1.scalar_ref, bf16[512,1152]{1,0:T(8,128)(2,1)S(1)} %text_norm.1.token.refs_2_.refs_0_.refs_1_.refs_4_, bf16[272,1152]{1,0:T(8,128)(2,1)} %get-tuple-element.14.refs_0_.refs_1_.refs_3_.refs_5_, ...), custom_call_target="tpu_custom_call" | custom-call | tf_op jit(solution)/shard_map/near_text/pallas_call | solution.py:249
  24.0 3.7 %far_near.1 = (f32[256,1152]{1,0:T(8,128)S(1)}, bf16[272,1152]{1,0:T(8,128)(2,1)S(1)}, bf16[256,1152]{1,0:T(8,128)(2,1)S(1)}, bf16[272,1152]{1,0:T(8,128)(2,1)S(1)}, bf16[256,1152]{1,0:T(8,128)(2,1)S(1)}) custom-call(f32[8,128]{1,0:T(8,128)S(1)} %scalars.1.scalar_ref, bf16[272,1152]{1,0:T(8,128)(2,1)S(1)} %collective-permute-done.1.refs_0_, ...), custom_call_target="tpu_custom_call" | custom-call | tf_op jit(solution)/shard_map/far_near/pallas_call | solution.py:249
  27.8 12.5 %collective-permute-done.refs_0_ = bf16[512,1152]{1,0:T(8,128)(2,1)S(1)} collective-permute-done((bf16[512,1152]{1,0:T(8,128)(2,1)S(1)}, bf16[512,1152]{1,0:T(8,128)(2,1)S(1)}, u32[]{:S(2)}, u32[]{:S(2)}) %collective-permute-start) | collective-permute-done | bytes 1179680 | tf_op jit(solution)/shard_map/ppermute | solution.py:292
  40.3 0.7 collective-permute-start.5
  41.5 1.6 %past_near.1.refs_4_.refs_5_ = f32[256,1152]{1,0:T(8,128)S(1)} custom-call(f32[8,128]{1,0:T(8,128)S(1)} %scalars.1.scalar_ref, bf16[512,1152]{1,0:T(8,128)(2,1)S(1)} %after.4.refs_2_.refs_0_.refs_1_, bf16[272,1152]{1,0:T(8,128)(2,1)S(1)} %get-tuple-element.20.refs_1_, bf16[256,1152]{1,0:T(8,128)(2,1)S(1)} %get-tuple-element.21.refs_2_, ...), custom_call_target="tpu_custom_call" | custom-call | tf_op jit(solution)/shard_map/past_near/pallas_call | solution.py:249
  43.5 1.6 %far_0.1.refs_6_ = bf16[256,1152]{1,0:T(8,128)(2,1)S(1)} custom-call(f32[8,128]{1,0:T(8,128)S(1)} %scalars.1.scalar_ref, bf16[272,1152]{1,0:T(8,128)(2,1)S(1)} %get-tuple-element.18.refs_5_.refs_0_.refs_1_, bf16[512,1152]{1,0:T(8,128)(2,1)S(1)} %after.4.refs_2_.refs_0_.refs_1_, bf16[512,1152]{1,0:T(8,128)(2,1)S(1)} %collective-permute-done.5.refs_2_.refs_3_, ...), custom_call_target="tpu_custom_call" | custom-call | tf_op jit(solution)/shard_map/far_0/pallas_call | solution.py:249
  45.2 1.6 %past_0.1.refs_6_ = bf16[256,1152]{1,0:T(8,128)(2,1)S(1)} custom-call(f32[8,128]{1,0:T(8,128)S(1)} %scalars.1.scalar_ref, bf16[512,1152]{1,0:T(8,128)(2,1)S(1)} %after.4.refs_2_.refs_0_.refs_1_, bf16[272,1152]{1,0:T(8,128)(2,1)S(1)} %get-tuple-element.18.refs_5_.refs_0_.refs_1_, bf16[256,1152]{1,0:T(8,128)(2,1)S(1)} %get-tuple-element.19.refs_2_.refs_0_.refs_6_, ...), custom_call_target="tpu_custom_call" | custom-call | tf_op jit(solution)/shard_map/past_0/pallas_call | solution.py:249
  46.8 5.0 %collective-permute-start.11 = (bf16[256,1152]{1,0:T(8,128)(2,1)S(1)}, bf16[256,1152]{1,0:T(8,128)(2,1)S(1)}, u32[]{:S(2)}, u32[]{:S(2)}) collective-permute-start(bf16[256,1152]{1,0:T(8,128)(2,1)S(1)} %past_0.1.refs_6_), channel_id=1, source_target_pairs={{4,0},{5,1},{6,2},{7,3},{8,4},{9,5},{10,6},{11,7},{12,8},{13,9},{1... | collective-permute-start | bytes 1769480 | tf_op jit(solution)/shard_map/ppermute | solution.py:292
  51.8 4.2 %far_1.1.refs_9_ = bf16[256,1152]{1,0:T(8,128)(2,1)S(1)} custom-call(f32[8,128]{1,0:T(8,128)S(1)} %scalars.1.scalar_ref, bf16[256,1152]{1,0:T(8,128)(2,1)S(1)} %get-tuple-element.19.refs_2_.refs_0_.refs_6_, bf16[272,1152]{1,0:T(8,128)(2,1)S(1)} %get-tuple-element.18.refs_5_.refs_0_.refs_1_, bf16[512,1152]{1,0:T(8,128)(2,1)S(1)} %after.4.refs_2_.refs_0_.refs_1_, ...), custom_call_target="tpu_custom_call" | custom-call | tf_op jit(solution)/shard_map/far_1/pallas_call | solution.py:249
  56.1 0.5 collective-permute-start.9
  56.6 4.7 %past_1.1.refs_11_ = bf16[256,1152]{1,0:T(8,128)(2,1)S(1)} custom-call(f32[8,128]{1,0:T(8,128)S(1)} %scalars.1.scalar_ref, bf16[512,1152]{1,0:T(8,128)(2,1)S(1)} %after.4.refs_2_.refs_0_.refs_1_, bf16[272,1152]{1,0:T(8,128)(2,1)S(1)} %get-tuple-element.18.refs_5_.refs_0_.refs_1_, bf16[256,1152]{1,0:T(8,128)(2,1)S(1)} %get-tuple-element.19.refs_2_.refs_0_.refs_6_, ...), custom_call_target="tpu_custom_call" | custom-call | tf_op jit(solution)/shard_map/past_1/pallas_call | solution.py:249
  61.3 2.6 %collective-permute-start.12 = (bf16[256,1152]{1,0:T(8,128)(2,1)S(1)}, bf16[256,1152]{1,0:T(8,128)(2,1)S(1)}, u32[]{:S(2)}, u32[]{:S(2)}) collective-permute-start(bf16[256,1152]{1,0:T(8,128)(2,1)S(1)} %past_1.1.refs_11_), channel_id=1, source_target_pairs={{4,0},{5,1},{6,2},{7,3},{8,4},{9,5},{10,6},{11,7},{12,8},{13,9},{1... | collective-permute-start | bytes 1769480 | tf_op jit(solution)/shard_map/ppermute | solution.py:292
  63.9 7.2 %last.1 = (f32[512,1152]{1,0:T(8,128)S(1)}, f32[512,1152]{1,0:T(8,128)S(1)}) custom-call(f32[8,128]{1,0:T(8,128)S(1)} %scalars.1.scalar_ref, bf16[272,1152]{1,0:T(8,128)(2,1)} %get-tuple-element.14.refs_0_.refs_1_.refs_3_.refs_5_, bf16[256,1152]{1,0:T(8,128)(2,1)} %get-tuple-element.15.refs_1_.refs_2_.refs_4_.refs_6_, ...), custom_call_target="tpu_custom_call" | custom-call | tf_op jit(solution)/shard_map/last/pallas_call | solution.py:249
  71.2 1.1 %image_add_0.1.refs_2_ = f32[512,1152]{1,0:T(8,128)} custom-call(f32[512,1152]{1,0:T(8,128)S(1)} %get-tuple-element.24.refs_0_, bf16[256,1152]{1,0:T(8,128)(2,1)S(1)} %collective-permute-done.10.refs_1_), custom_call_target="tpu_custom_call" | custom-call | tf_op jit(solution)/shard_map/image_add_0/pallas_call | solution.py:276
  72.3 1.1 %text_add_0.1.refs_3_.refs_2_ = f32[512,1152]{1,0:T(8,128)} custom-call(f32[512,1152]{1,0:T(8,128)S(1)} %get-tuple-element.25.refs_0_, bf16[256,1152]{1,0:T(8,128)(2,1)S(1)} %collective-permute-done.11.refs_1_, f32[512,1152]{1,0:T(8,128)} %image_add_0.1.refs_2_), custom_call_target="tpu_custom_call" | custom-call | tf_op jit(solution)/shard_map/text_add_0/pallas_call | solution.py:276
  73.4 1.1 %image_add_1.1.refs_3_ = f32[512,1152]{1,0:T(8,128)} custom-call(f32[512,1152]{1,0:T(8,128)S(1)} %get-tuple-element.24.refs_0_, bf16[256,1152]{1,0:T(8,128)(2,1)S(1)} %collective-permute-done.9.refs_1_, f32[512,1152]{1,0:T(8,128)} %image_add_0.1.refs_2_, f32[512,1152]{1,0:T(8,128)} %text_add_0.1.refs_3_.refs_2_), custom_call_target="tpu_custom_call", output_to_operand_aliasing={{}: (2, {})} | custom-call | tf_op jit(solution)/shard_map/image_add_1/pallas_call | solution.py:276
  74.5 1.8 %collective-permute-done.12.refs_1_ = bf16[256,1152]{1,0:T(8,128)(2,1)S(1)} collective-permute-done((bf16[256,1152]{1,0:T(8,128)(2,1)S(1)}, bf16[256,1152]{1,0:T(8,128)(2,1)S(1)}, u32[]{:S(2)}, u32[]{:S(2)}) %collective-permute-start.12) | collective-permute-done | bytes 589856 | tf_op jit(solution)/shard_map/ppermute | solution.py:292
  76.2 1.1 %text_add_1.1 = f32[512,1152]{1,0:T(8,128)} custom-call(f32[512,1152]{1,0:T(8,128)S(1)} %get-tuple-element.25.refs_0_, bf16[256,1152]{1,0:T(8,128)(2,1)S(1)} %collective-permute-done.12.refs_1_, f32[512,1152]{1,0:T(8,128)} %text_add_0.1.refs_3_.refs_2_, f32[512,1152]{1,0:T(8,128)} %image_add_1.1.refs_3_), custom_call_target="tpu_custom_call", output_to_operand_aliasing={{}: (2, {})} | custom-call | tf_op jit(solution)/shard_map/text_add_1/pallas_call | solution.py:276
  (27 shorter events, 1.6 us)
Async XLA Ops:
  2.2 9.0 %collective-permute-start.2 = (bf16[512,1152]{1,0:T(8,128)(2,1)S(1)}, bf16[512,1152]{1,0:T(8,128)(2,1)}, u32[]{:S(2)}, u32[]{:S(2)}) collective-permute-start(bf16[512,1152]{1,0:T(8,128)(2,1)S(1)} %text_norm.1.token.refs_2_.refs_0_.refs_1_.refs_4_), channel_id=1, source_target_pairs={{0,1},{1,0},{2,3},{3,2},{4,5},{5,4},{6,7},{7,6},{8,9},{9,8},{10,11... | collective-permute-start | bytes 3538952 | tf_op jit(solution)/shard_map/ppermute | solution.py:292
  5.6 34.7 %collective-permute-start = (bf16[512,1152]{1,0:T(8,128)(2,1)S(1)}, bf16[512,1152]{1,0:T(8,128)(2,1)S(1)}, u32[]{:S(2)}, u32[]{:S(2)}) collective-permute-start(bf16[512,1152]{1,0:T(8,128)(2,1)S(1)} %text_norm.1.token.refs_2_.refs_0_.refs_1_.refs_4_), channel_id=1, source_target_pairs={{0,4},{1,5},{2,6},{3,7},{4,8},{5,9},{6,10},{7,11},{8,12},{9,13},{1... | collective-permute-start | bytes 3538952 | tf_op jit(solution)/shard_map/ppermute | solution.py:292
  8.2 9.8 %collective-permute-start.3 = (bf16[272,1152]{1,0:T(8,128)(2,1)}, bf16[272,1152]{1,0:T(8,128)(2,1)}, u32[]{:S(2)}, u32[]{:S(2)}) collective-permute-start(bf16[272,1152]{1,0:T(8,128)(2,1)} %get-tuple-element.14.refs_0_.refs_1_.refs_3_.refs_5_), channel_id=1, source_target_pairs={{0,1},{1,0},{2,3},{3,2},{4,5},{5,4},{6,7},{7,6},{8,9},{9,8},{10,11... | collective-permute-start | bytes 1880072 | tf_op jit(solution)/shard_map/ppermute | solution.py:292
  8.4 15.6 %collective-permute-start.1 = (bf16[272,1152]{1,0:T(8,128)(2,1)}, bf16[272,1152]{1,0:T(8,128)(2,1)S(1)}, u32[]{:S(2)}, u32[]{:S(2)}) collective-permute-start(bf16[272,1152]{1,0:T(8,128)(2,1)} %get-tuple-element.14.refs_0_.refs_1_.refs_3_.refs_5_), channel_id=1, source_target_pairs={{0,2},{1,3},{2,0},{3,1},{4,6},{5,7},{6,4},{7,5},{8,10},{9,11},{10,... | collective-permute-start | bytes 1880072 | tf_op jit(solution)/shard_map/ppermute | solution.py:292
  9.5 8.6 %collective-permute-start.4 = (bf16[256,1152]{1,0:T(8,128)(2,1)}, bf16[256,1152]{1,0:T(8,128)(2,1)}, u32[]{:S(2)}, u32[]{:S(2)}) collective-permute-start(bf16[256,1152]{1,0:T(8,128)(2,1)} %get-tuple-element.15.refs_1_.refs_2_.refs_4_.refs_6_), channel_id=1, source_target_pairs={{0,1},{1,0},{2,3},{3,2},{4,5},{5,4},{6,7},{7,6},{8,9},{9,8},{10,11... | collective-permute-start | bytes 1769480 | tf_op jit(solution)/shard_map/ppermute | solution.py:292
  11.2 6.1 %copy-start.2 = (bf16[256,1152]{1,0:T(8,128)(2,1)S(1)}, bf16[256,1152]{1,0:T(8,128)(2,1)}, u32[]{:S(2)}) copy-start(bf16[256,1152]{1,0:T(8,128)(2,1)} %get-tuple-element.16.refs_0_) | copy-start | bytes 1769476
  17.4 23.6 %collective-permute-start.6 = (bf16[256,1152]{1,0:T(8,128)(2,1)S(1)}, bf16[256,1152]{1,0:T(8,128)(2,1)S(1)}, u32[]{:S(2)}, u32[]{:S(2)}) collective-permute-start(bf16[256,1152]{1,0:T(8,128)(2,1)S(1)} %after.3.refs_5_), channel_id=1, source_target_pairs={{0,2},{1,3},{2,0},{3,1},{4,6},{5,7},{6,4},{7,5},{8,10},{9,11},{10,... | collective-permute-start | bytes 1769480 | tf_op jit(solution)/shard_map/ppermute | solution.py:292
  40.3 3.1 %collective-permute-start.5 = (bf16[512,1152]{1,0:T(8,128)(2,1)S(1)}, bf16[512,1152]{1,0:T(8,128)(2,1)S(1)}, u32[]{:S(2)}, u32[]{:S(2)}) collective-permute-start(bf16[512,1152]{1,0:T(8,128)(2,1)S(1)} %after.4.refs_2_.refs_0_.refs_1_), channel_id=1, source_target_pairs={{0,1},{1,0},{2,3},{3,2},{4,5},{5,4},{6,7},{7,6},{8,9},{9,8},{10,11... | collective-permute-start | bytes 3538952 | tf_op jit(solution)/shard_map/ppermute | solution.py:292
  41.0 4.2 %collective-permute-start.7 = (bf16[272,1152]{1,0:T(8,128)(2,1)S(1)}, bf16[272,1152]{1,0:T(8,128)(2,1)S(1)}, u32[]{:S(2)}, u32[]{:S(2)}) collective-permute-start(bf16[272,1152]{1,0:T(8,128)(2,1)S(1)} %get-tuple-element.18.refs_5_.refs_0_.refs_1_), channel_id=1, source_target_pairs={{0,1},{1,0},{2,3},{3,2},{4,5},{5,4},{6,7},{7,6},{8,9},{9,8},{10,11... | collective-permute-start | bytes 1880072 | tf_op jit(solution)/shard_map/ppermute | solution.py:292
  41.3 3.9 %collective-permute-start.8 = (bf16[256,1152]{1,0:T(8,128)(2,1)S(1)}, bf16[256,1152]{1,0:T(8,128)(2,1)S(1)}, u32[]{:S(2)}, u32[]{:S(2)}) collective-permute-start(bf16[256,1152]{1,0:T(8,128)(2,1)S(1)} %get-tuple-element.19.refs_2_.refs_0_.refs_6_), channel_id=1, source_target_pairs={{0,1},{1,0},{2,3},{3,2},{4,5},{5,4},{6,7},{7,6},{8,9},{9,8},{10,11... | collective-permute-start | bytes 1769480 | tf_op jit(solution)/shard_map/ppermute | solution.py:292
  45.1 26.1 %collective-permute-start.10 = (bf16[256,1152]{1,0:T(8,128)(2,1)S(1)}, bf16[256,1152]{1,0:T(8,128)(2,1)S(1)}, u32[]{:S(2)}, u32[]{:S(2)}) collective-permute-start(bf16[256,1152]{1,0:T(8,128)(2,1)S(1)} %far_0.1.refs_6_), channel_id=1, source_target_pairs={{0,2},{1,3},{2,0},{3,1},{4,6},{5,7},{6,4},{7,5},{8,10},{9,11},{10,... | collective-permute-start | bytes 1769480 | tf_op jit(solution)/shard_map/ppermute | solution.py:292
  46.8 25.5 %collective-permute-start.11 = (bf16[256,1152]{1,0:T(8,128)(2,1)S(1)}, bf16[256,1152]{1,0:T(8,128)(2,1)S(1)}, u32[]{:S(2)}, u32[]{:S(2)}) collective-permute-start(bf16[256,1152]{1,0:T(8,128)(2,1)S(1)} %past_0.1.refs_6_), channel_id=1, source_target_pairs={{4,0},{5,1},{6,2},{7,3},{8,4},{9,5},{10,6},{11,7},{12,8},{13,9},{1... | collective-permute-start | bytes 1769480 | tf_op jit(solution)/shard_map/ppermute | solution.py:292
  56.1 17.3 %collective-permute-start.9 = (bf16[256,1152]{1,0:T(8,128)(2,1)S(1)}, bf16[256,1152]{1,0:T(8,128)(2,1)S(1)}, u32[]{:S(2)}, u32[]{:S(2)}) collective-permute-start(bf16[256,1152]{1,0:T(8,128)(2,1)S(1)} %far_1.1.refs_9_), channel_id=1, source_target_pairs={{0,2},{1,3},{2,0},{3,1},{4,6},{5,7},{6,4},{7,5},{8,10},{9,11},{10,... | collective-permute-start | bytes 1769480 | tf_op jit(solution)/shard_map/ppermute | solution.py:292
  56.6 7.4 %copy-start = (f32[512,1152]{1,0:T(8,128)S(1)}, f32[512,1152]{1,0:T(8,128)}, u32[]{:S(2)}) copy-start(f32[512,1152]{1,0:T(8,128)} %near_image.1.refs_1_.refs_9_) | copy-start | bytes 7077892
  56.6 7.4 %copy-start.1 = (f32[512,1152]{1,0:T(8,128)S(1)}, f32[512,1152]{1,0:T(8,128)}, u32[]{:S(2)}) copy-start(f32[512,1152]{1,0:T(8,128)} %near_text.1.refs_7_.refs_10_) | copy-start | bytes 7077892
  61.3 14.9 %collective-permute-start.12 = (bf16[256,1152]{1,0:T(8,128)(2,1)S(1)}, bf16[256,1152]{1,0:T(8,128)(2,1)S(1)}, u32[]{:S(2)}, u32[]{:S(2)}) collective-permute-start(bf16[256,1152]{1,0:T(8,128)(2,1)S(1)} %past_1.1.refs_11_), channel_id=1, source_target_pairs={{4,0},{5,1},{6,2},{7,3},{8,4},{9,5},{10,6},{11,7},{12,8},{13,9},{1... | collective-permute-start | bytes 1769480 | tf_op jit(solution)/shard_map/ppermute | solution.py:292
